TPU v7x, 256 devices: a whole 4x4x8 slice. The times are simulated.
256 devices in a mesh: seq: 64 (over z, x, core), chan: 4 (over y).
Axes of the slice: x: 4, y: 4, z: 8, core: 2. Of those that a mesh axis runs over, the one named last changes fastest.
Arguments:
- inputs: bfloat16 [8192, 2048], P('seq', 'chan'), may hold values from -6 to 6
- gate_branch: bfloat16 [8192, 2048], P('seq', 'chan'), may hold values from -6 to 6
- short_taps: float32 [4, 2048], P(None, 'chan'), may hold values from -3 to 3
- filters: float32 [8192, 2048], P('seq', 'chan'), may hold values from -0.0625 to 0.0625
- w_out: bfloat16 [2048, 2048], P('chan'), may hold values from -0.125 to 0.125
- cotangent: bfloat16 [8192, 2048], P('seq', 'chan'), may hold values from -16 to 16
Outputs:
- output: bfloat16 [8192, 2048], P('seq', 'chan')
- grad_inputs: bfloat16 [8192, 2048], P('seq', 'chan')
- grad_gate: bfloat16 [8192, 2048], P('seq', 'chan')
- grad_filters: float32 [8192, 2048], P('seq', 'chan')
- grad_taps: float32 [4, 2048], P(None, 'chan')
- grad_wout: float32 [2048, 2048], P('chan', 'seq')
All inputs are finite; a program needn't handle non-finite values.
Results may differ from a plain program's by a relative error of at most 0.0047.
The roundings to bfloat16 on the way count: a program that leaves them out, or rounds other values in their place, can miss the bound.
Values may be sent and summed in bfloat16 or wider, within the bound.
No kernel may reach another device: no remote copies, remote signals or barrier semaphores. Data moves between devices by JAX's collectives and lax.ppermute only.
A program may use at most 64 MiB of HBM per device.

v0:
```python
import math

import jax
import jax.numpy as jnp
from jax import lax
from jax.sharding import PartitionSpec as P

HIGHEST = lax.Precision.HIGHEST


def from_behind(value, axis, steps):
    count = lax.axis_size(axis)
    first, last = (max(0, -steps), min(count, count - steps))
    return lax.ppermute(value, axis, [(source, source + steps) for source in range(first, last)])


def angle_table(row_len, col_len, modulus, row_start, col_start, direction):
    row_ids = lax.iota(jnp.int32, row_len)[:, None] + row_start
    col_ids = lax.iota(jnp.int32, col_len)[None, :] + col_start
    phase = row_ids * col_ids % modulus
    angles = phase.astype(jnp.float32) * (direction * 2.0 * math.pi / modulus)
    return (jnp.cos(angles), jnp.sin(angles))


def column_dft(real_part, imag_part, length, form, direction):
    cos_table, sin_table = angle_table(length, length, length, 0, 0, direction)
    new_real = jnp.einsum(form, real_part, cos_table, precision=HIGHEST) - jnp.einsum(
        form, imag_part, sin_table, precision=HIGHEST
    )
    new_imag = jnp.einsum(form, real_part, sin_table, precision=HIGHEST) + jnp.einsum(
        form, imag_part, cos_table, precision=HIGHEST
    )
    return (new_real, new_imag)


def panel_forward(signal):
    stack_size = signal.shape[0]
    block_len = signal.shape[1]
    part_count = lax.axis_size("seq")
    my_index = lax.axis_index("seq")
    narrow = block_len // part_count
    row_order = 2 * part_count
    full_len = row_order * block_len
    by_column = lax.all_to_all(signal[:, None], "seq", split_axis=2, concat_axis=1, tiled=True)
    row_cos, row_sin = angle_table(row_order, part_count, row_order, 0, 0, -1.0)
    real_part = jnp.einsum("ja,kabf->kjbf", row_cos, by_column, precision=HIGHEST)
    imag_part = jnp.einsum("ja,kabf->kjbf", row_sin, by_column, precision=HIGHEST)
    twist_cos, twist_sin = angle_table(row_order, narrow, full_len, 0, my_index * narrow, -1.0)
    twist_cos = twist_cos[None, :, :, None]
    twist_sin = twist_sin[None, :, :, None]
    real_twist = real_part * twist_cos - imag_part * twist_sin
    imag_twist = real_part * twist_sin + imag_part * twist_cos
    by_rows = lax.all_to_all(
        jnp.concatenate([real_twist, imag_twist], 0), "seq", split_axis=1, concat_axis=2, tiled=True
    )
    return column_dft(by_rows[:stack_size], by_rows[stack_size:], block_len, "kjbf,bm->kjmf", -1.0)


def panel_inverse(real_part, imag_part):
    stack_size = real_part.shape[0]
    block_len = real_part.shape[2]
    part_count = lax.axis_size("seq")
    my_index = lax.axis_index("seq")
    row_order = 2 * part_count
    full_len = row_order * block_len
    real_back, imag_back = column_dft(real_part, imag_part, block_len, "kjmf,mb->kjbf", 1.0)
    twist_cos, twist_sin = angle_table(2, block_len, full_len, my_index * 2, 0, 1.0)
    twist_cos = twist_cos[None, :, :, None]
    twist_sin = twist_sin[None, :, :, None]
    real_twist = (real_back * twist_cos - imag_back * twist_sin) / block_len
    imag_twist = (real_back * twist_sin + imag_back * twist_cos) / block_len
    by_column = lax.all_to_all(
        jnp.concatenate([real_twist, imag_twist], 0), "seq", split_axis=2, concat_axis=1, tiled=True
    )
    row_cos, row_sin = angle_table(part_count, row_order, row_order, 0, 0, 1.0)
    signal = (
        jnp.einsum("aj,kjbf->kabf", row_cos, by_column[:stack_size], precision=HIGHEST)
        - jnp.einsum("aj,kjbf->kabf", row_sin, by_column[stack_size:], precision=HIGHEST)
    ) / row_order
    returned = lax.all_to_all(signal, "seq", split_axis=1, concat_axis=2, tiled=True)
    return returned[:, 0]


def local(inputs, gate_branch, short_taps, filters, w_out, cotangent):
    forward_fn, inverse_fn = (panel_forward, panel_inverse)
    tap_count = short_taps.shape[0]
    row_count = inputs.shape[0]
    left_tail = from_behind(inputs[row_count - (tap_count - 1) :], "seq", 1)
    extended = jnp.concatenate([left_tail, inputs], 0).astype(jnp.float32)
    mixed = jnp.zeros((row_count, inputs.shape[1]), jnp.float32)
    for tap_index in range(tap_count):
        start_row = tap_count - 1 - tap_index
        mixed = mixed + short_taps[tap_index] * extended[start_row : start_row + row_count]
    spec_real, spec_imag = forward_fn(jnp.stack([mixed, filters], 0))
    mixed_real, filter_real = (spec_real[0], spec_real[1])
    mixed_imag, filter_imag = (spec_imag[0], spec_imag[1])
    prod_real = mixed_real * filter_real - mixed_imag * filter_imag
    prod_imag = mixed_real * filter_imag + mixed_imag * filter_real
    convolved = inverse_fn(prod_real[None], prod_imag[None])[0]
    gate_wide = gate_branch.astype(jnp.float32)
    gated = (gate_wide * convolved).astype(jnp.bfloat16)
    out_terms = jnp.dot(gated, w_out, preferred_element_type=jnp.float32)
    output = lax.psum_scatter(out_terms, "chan", scatter_dimension=1, tiled=True).astype(
        jnp.bfloat16
    )
    full_cot = lax.all_gather(cotangent, "chan", axis=1, tiled=True)
    grad_gated = lax.dot_general(
        full_cot, w_out, (((1,), (1,)), ((), ())), preferred_element_type=jnp.float32
    )
    grad_gate = (grad_gated * convolved).astype(jnp.bfloat16)
    grad_conv = grad_gated * gate_wide
    grad_real, grad_imag = forward_fn(grad_conv[None])
    grad_real = grad_real[0]
    grad_imag = grad_imag[0]
    back_real = jnp.stack(
        [
            filter_real * grad_real + filter_imag * grad_imag,
            mixed_real * grad_real + mixed_imag * grad_imag,
        ],
        0,
    )
    back_imag = jnp.stack(
        [
            filter_real * grad_imag - filter_imag * grad_real,
            mixed_real * grad_imag - mixed_imag * grad_real,
        ],
        0,
    )
    gradients = inverse_fn(back_real, back_imag)
    grad_mixed = gradients[0]
    grad_filters = gradients[1]
    right_head = from_behind(grad_mixed[: tap_count - 1], "seq", -1)
    grad_ext = jnp.concatenate([grad_mixed, right_head], 0)
    grad_wide = jnp.zeros_like(grad_mixed)
    tap_rows = []
    for tap_index in range(tap_count):
        start_row = tap_count - 1 - tap_index
        grad_wide = grad_wide + short_taps[tap_index] * grad_ext[tap_index : tap_index + row_count]
        tap_rows.append(jnp.sum(extended[start_row : start_row + row_count] * grad_mixed, axis=0))
    grad_inputs = grad_wide.astype(jnp.bfloat16)
    grad_taps = lax.psum(jnp.stack(tap_rows, 0), "seq")
    weight_terms = lax.dot_general(
        gated, full_cot, (((0,), (0,)), ((), ())), preferred_element_type=jnp.float32
    )
    grad_wout = lax.psum_scatter(weight_terms, "seq", scatter_dimension=1, tiled=True)
    return (output, grad_inputs, grad_gate, grad_filters, grad_taps, grad_wout)


def solution(mesh):
    in_specs = (
        P("seq", "chan"),
        P("seq", "chan"),
        P(None, "chan"),
        P("seq", "chan"),
        P("chan", None),
        P("seq", "chan"),
    )
    out_specs = (
        P("seq", "chan"),
        P("seq", "chan"),
        P("seq", "chan"),
        P("seq", "chan"),
        P(None, "chan"),
        P("chan", "seq"),
    )
    return jax.shard_map(local, mesh=mesh, in_specs=in_specs, out_specs=out_specs, check_vma=False)
```

profile of v0, /device:TPU:8, one launch (start us, length us, event | category | flops | bytes accessed | tf_op | source)
XLA Modules:
  0.0 510.3 jit_solution(5139699814598067409)
XLA Ops:
  8.0 1.7 collective-permute-start
  9.8 13.9 %all_gather.3 = bf16[128,2048]{1,0:T(8,128)(2,1)S(1)} all-gather(bf16[128,512]{1,0:T(8,128)(2,1)} %param.11), channel_id=1, replica_groups=mesh['seq'=64,'chan'=4] {'chan'}, dimensions={1}, use_global_device_ids=true | all-gather | bytes 655360 | tf_op jit(solution)/shard_map/all_gather | solution.py:106
  26.3 12.1 %all-to-all-start.4 = ((f32[1,1,128,512]{3,1,0,2:T(1,128)}), f32[1,1,128,512]{3,1,0,2:T(1,128)S(1)}, u32[]{:S(2)}, u32[]{:S(2)}) async-start(f32[1,1,128,512]{3,1,0,2:T(1,128)} %copy.68), calls=%async_computation.5 | async-start | bytes 524288 | tf_op jit(solution)/shard_map/all_to_all | solution.py:44
  38.8 1.2 copy.58
  40.0 11.4 %all-to-all-done.4 = f32[1,1,128,512]{3,1,0,2:T(1,128)S(1)} async-done(((f32[1,1,128,512]{3,1,0,2:T(1,128)}), f32[1,1,128,512]{3,1,0,2:T(1,128)S(1)}, u32[]{:S(2)}, u32[]{:S(2)}) %all-to-all-start.4) | async-done | bytes 262176 | tf_op jit(solution)/shard_map/all_to_all | solution.py:44
  51.4 4.9 all-to-all-start
  58.4 1.1 convolution_bitcast_fusion.3
  59.4 1.8 multiply_subtract_fusion.3
  61.2 1.1 pad_maximum_fusion.3
  62.3 2.3 copy.71
  64.6 9.5 %all-to-all-done = f32[2,1,128,512]{3,0,1,2:T(2,128)S(1)} async-done(((f32[2,1,128,512]{3,0,1,2:T(2,128)}), f32[2,1,128,512]{3,0,1,2:T(2,128)S(1)}, u32[]{:S(2)}, u32[]{:S(2)}) %all-to-all-start) | async-done | bytes 524320 | tf_op jit(solution)/shard_map/all_to_all | solution.py:44
  74.0 6.3 %all-to-all-start.5 = ((f32[2,128,2,512]{3,2,0,1:T(2,128)}), f32[2,128,2,512]{3,2,0,1:T(2,128)}, u32[]{:S(2)}, u32[]{:S(2)}) async-start(f32[2,128,2,512]{3,2,0,1:T(2,128)} %copy.71), calls=%async_computation.6 | async-start | bytes 2097152 | tf_op jit(solution)/shard_map/all_to_all | solution.py:53
  80.3 1.9 convolution_bitcast_fusion.1
  82.3 1.9 multiply_subtract_fusion
  84.2 1.5 pad_maximum_fusion
  85.7 4.2 copy.61
  89.9 19.1 %all-to-all-done.5 = f32[2,128,2,512]{3,2,0,1:T(2,128)} async-done(((f32[2,128,2,512]{3,2,0,1:T(2,128)}), f32[2,128,2,512]{3,2,0,1:T(2,128)}, u32[]{:S(2)}, u32[]{:S(2)}) %all-to-all-start.5) | async-done | bytes 1048608 | tf_op jit(solution)/shard_map/all_to_all | solution.py:53
  109.0 5.8 %all-to-all-start.1 = ((f32[4,128,2,512]{3,2,0,1:T(2,128)}), f32[4,128,2,512]{3,2,0,1:T(2,128)}, u32[]{:S(2)}, u32[]{:S(2)}) async-start(f32[4,128,2,512]{3,2,0,1:T(2,128)} %copy.61), calls=%async_computation.1 | async-start | bytes 4194304 | tf_op jit(solution)/shard_map/all_to_all | solution.py:53
  115.6 1.6 copy.72
  117.2 1.2 fusion.237
  118.8 1.9 copy.74
  120.7 1.4 reshape.169
  123.0 1.7 fusion.6
  124.6 1.7 fusion.40
  126.3 39.8 %all-to-all-done.1 = f32[4,128,2,512]{3,2,0,1:T(2,128)} async-done(((f32[4,128,2,512]{3,2,0,1:T(2,128)}), f32[4,128,2,512]{3,2,0,1:T(2,128)}, u32[]{:S(2)}, u32[]{:S(2)}) %all-to-all-start.1) | async-done | bytes 2097184 | tf_op jit(solution)/shard_map/all_to_all | solution.py:53
  166.1 2.3 copy.62
  168.4 1.8 fusion.236
  170.2 1.3 copy.63
  171.5 1.9 slice.118
  173.5 2.3 fusion.45
  175.7 2.2 fusion.47
  178.0 1.4 copy.64
  179.4 1.9 slice.120
  181.3 2.6 fusion.3
  184.0 9.4 %fusion.2 = f32[2,2,128,512]{3,2,1,0:T(8,128)S(1)} fusion(f32[128,2,2,512]{3,0,2,1:T(8,128)S(1)} %copy-done.8, f32[2,2,128,512]{3,2,1,0:T(8,128)S(1)} %slice.120), kind=kOutput, calls=%fused_computation.10 | convolution fusion | flops 403144704 | bytes 3145728 | tf_op jit(solution)/shard_map/kjbf,bm->kjmf/dot_general | solution.py:30
  193.4 2.4 multiply_subtract_fusion.2
  200.3 34.0 %all_to_all.99 = f32[2,2,128,512]{3,1,0,2:T(2,128)S(1)} all-to-all(f32[2,2,128,512]{3,1,0,2:T(2,128)S(1)} %copy.65), channel_id=1, replica_groups=mesh['seq'=64,'chan'=4] {'seq'}, dimensions={2} | all-to-all | bytes 2097152 | tf_op jit(solution)/shard_map/all_to_all | solution.py:72
  234.7 1.3 fusion.238
  236.0 2.2 reshape.165
  238.2 1.6 fusion.69
  239.8 2.2 reshape.166
  242.0 1.6 fusion.11
  243.9 18.6 %all_to_all.100 = f32[1,64,2,512]{3,2,0,1:T(2,128)} all-to-all(f32[1,64,2,512]{3,2,0,1:T(2,128)S(1)} %copy.67), channel_id=1, replica_groups=mesh['seq'=64,'chan'=4] {'seq'}, dimensions={1} | all-to-all | bytes 524288 | tf_op jit(solution)/shard_map/all_to_all | solution.py:80
  262.5 1.1 squeeze_squeeze.3
  263.6 1.4 fusion.233
  265.1 2.6 fusion.12
  267.7 1.3 fusion.13
  269.0 1.3 fusion.1
  270.3 1.6 subtract_multiply_fusion
  272.1 3.0 copy.75
  275.2 5.7 %all-to-all-start.6 = ((f32[4,2,128,512]{3,1,0,2:T(2,128)}), f32[4,2,128,512]{3,1,0,2:T(2,128)}, u32[]{:S(2)}, u32[]{:S(2)}) async-start(f32[4,2,128,512]{3,1,0,2:T(2,128)} %copy.75), calls=%async_computation.7 | async-start | bytes 4194304 | tf_op jit(solution)/shard_map/all_to_all | solution.py:72
  281.2 2.7 fusion.231
  283.9 48.2 %all-to-all-done.6 = f32[4,2,128,512]{3,1,0,2:T(2,128)} async-done(((f32[4,2,128,512]{3,1,0,2:T(2,128)}), f32[4,2,128,512]{3,1,0,2:T(2,128)}, u32[]{:S(2)}, u32[]{:S(2)}) %all-to-all-start.6) | async-done | bytes 2097184 | tf_op jit(solution)/shard_map/all_to_all | solution.py:72
  332.1 2.4 copy.101
  334.5 2.0 fusion.235
  336.5 2.9 slice.130
  339.4 2.9 slice.132
  342.4 2.2 fusion.62
  345.4 1.2 copy.77
  346.6 5.3 %all-to-all-start.7 = ((f32[2,64,2,512]{3,2,0,1:T(2,128)}), f32[2,64,2,512]{3,2,0,1:T(2,128)S(1)}, u32[]{:S(2)}, u32[]{:S(2)}) async-start(f32[2,64,2,512]{3,2,0,1:T(2,128)} %copy.77), calls=%async_computation.8 | async-start | bytes 1048576 | tf_op jit(solution)/shard_map/all_to_all | solution.py:80
  352.7 1.6 convert_element_type.98
  354.3 15.3 %all-to-all-done.7 = f32[2,64,2,512]{3,2,0,1:T(2,128)S(1)} async-done(((f32[2,64,2,512]{3,2,0,1:T(2,128)}), f32[2,64,2,512]{3,2,0,1:T(2,128)S(1)}, u32[]{:S(2)}, u32[]{:S(2)}) %all-to-all-start.7) | async-done | bytes 524320 | tf_op jit(solution)/shard_map/all_to_all | solution.py:80
  370.6 1.3 collective-permute-start.1
  372.9 129.3 %psum.7 = f32[4,512]{1,0:T(4,128)} all-reduce(f32[4,512]{1,0:T(4,128)S(1)} %pad_maximum_fusion.10), channel_id=1, replica_groups=mesh['seq'=64,'chan'=4] {'seq'}, use_global_device_ids=true, to_apply=%region_5.6 | all-reduce | flops 2048 | bytes 16384 | tf_op jit(solution)/shard_map/psum | solution.py:141
  (115 shorter events, 17.6 us)
Async XLA Ops:
  7.2 17.3 %copy-start = (bf16[512,2048]{1,0:T(8,128)(2,1)S(1)}, bf16[512,2048]{1,0:T(8,128)(2,1)}, u32[]{:S(2)}) copy-start(bf16[512,2048]{1,0:T(8,128)(2,1)} %param.10) | copy-start | bytes 6291460
  7.2 18.1 %copy-start.15 = (bf16[128,512]{1,0:T(8,128)(2,1)S(1)}, bf16[128,512]{1,0:T(8,128)(2,1)}, u32[]{:S(2)}) copy-start(bf16[128,512]{1,0:T(8,128)(2,1)} %param.7) | copy-start | bytes 393220
  8.0 30.5 %collective-permute-start = (bf16[3,512]{1,0:T(4,128)(2,1)S(1)}, bf16[3,512]{1,0:T(4,128)(2,1)S(1)}, u32[]{:S(2)}, u32[]{:S(2)}) collective-permute-start(bf16[3,512]{1,0:T(4,128)(2,1)S(1)} %slice.109), channel_id=1, source_target_pairs={{0,4},{4,8},{8,12},{12,16},{16,20},{20,24},{24,28},{28,32},{32,36}... | collective-permute-start | bytes 9224 | tf_op jit(solution)/shard_map/ppermute | solution.py:14
  23.7 0.8 copy-start.1
  24.5 14.0 %copy-start.33 = (f32[4,512]{1,0:T(4,128)S(1)}, f32[4,512]{1,0:T(4,128)}, u32[]{:S(2)}) copy-start(f32[4,512]{1,0:T(4,128)} %param.8) | copy-start | bytes 24580
  24.5 14.1 %copy-start.18 = (bf16[128,512]{1,0:T(8,128)(2,1)S(1)}, bf16[128,512]{1,0:T(8,128)(2,1)}, u32[]{:S(2)}) copy-start(bf16[128,512]{1,0:T(8,128)(2,1)} %param.6) | copy-start | bytes 393220
  25.3 13.2 %copy-start.11 = (f32[128,512]{1,0:T(8,128)}, f32[128,512]{1,0:T(8,128)S(1)}, u32[]{:S(2)}) copy-start(f32[128,512]{1,0:T(8,128)S(1)} %fusion.241) | copy-start | bytes 786436
  25.3 13.4 %copy-start.17 = (f32[128,512]{1,0:T(8,128)S(1)}, f32[128,512]{1,0:T(8,128)}, u32[]{:S(2)}) copy-start(f32[128,512]{1,0:T(8,128)} %param.9) | copy-start | bytes 786436
  26.3 25.1 %all-to-all-start.4 = ((f32[1,1,128,512]{3,1,0,2:T(1,128)}), f32[1,1,128,512]{3,1,0,2:T(1,128)S(1)}, u32[]{:S(2)}, u32[]{:S(2)}) async-start(f32[1,1,128,512]{3,1,0,2:T(1,128)} %copy.68), calls=%async_computation.5 | async-start | bytes 524288 | tf_op jit(solution)/shard_map/all_to_all | solution.py:44
  38.5 12.9 %copy-start.19 = (f32[1,512]{1,0:T(1,128)}, f32[1,512]{1,0:T(1,128)S(1)}, u32[]{:S(2)}) copy-start(f32[1,512]{1,0:T(1,128)S(1)} %get-tuple-element.35) | copy-start | bytes 6148
  38.5 12.9 %copy-start.21 = (f32[1,512]{1,0:T(1,128)}, f32[1,512]{1,0:T(1,128)S(1)}, u32[]{:S(2)}) copy-start(f32[1,512]{1,0:T(1,128)S(1)} %get-tuple-element.36) | copy-start | bytes 6148
  38.5 12.9 %copy-start.23 = (f32[1,512]{1,0:T(1,128)}, f32[1,512]{1,0:T(1,128)S(1)}, u32[]{:S(2)}) copy-start(f32[1,512]{1,0:T(1,128)S(1)} %get-tuple-element.37) | copy-start | bytes 6148
  38.5 12.9 %copy-start.25 = (f32[1,512]{1,0:T(1,128)}, f32[1,512]{1,0:T(1,128)S(1)}, u32[]{:S(2)}) copy-start(f32[1,512]{1,0:T(1,128)S(1)} %get-tuple-element.38) | copy-start | bytes 6148
  51.4 22.6 %all-to-all-start = ((f32[2,1,128,512]{3,0,1,2:T(2,128)}), f32[2,1,128,512]{3,0,1,2:T(2,128)S(1)}, u32[]{:S(2)}, u32[]{:S(2)}) async-start(f32[2,1,128,512]{3,0,1,2:T(2,128)} %copy.58), calls=%async_computation | async-start | bytes 1048576 | tf_op jit(solution)/shard_map/all_to_all | solution.py:44
  56.4 0.5 copy-start.34
  64.5 17.7 %copy-start.31 = (f32[128,2]{0,1:T(2,128)S(1)}, f32[128,2]{0,1:T(2,128)}, u32[]{:S(2)}) copy-start(f32[128,2]{0,1:T(2,128)} %get-tuple-element.41) | copy-start | bytes 3076
  64.6 17.7 %copy-start.32 = (f32[128,2]{0,1:T(2,128)S(1)}, f32[128,2]{0,1:T(2,128)}, u32[]{:S(2)}) copy-start(f32[128,2]{0,1:T(2,128)} %get-tuple-element.42) | copy-start | bytes 3076
  74.0 35.0 %all-to-all-start.5 = ((f32[2,128,2,512]{3,2,0,1:T(2,128)}), f32[2,128,2,512]{3,2,0,1:T(2,128)}, u32[]{:S(2)}, u32[]{:S(2)}) async-start(f32[2,128,2,512]{3,2,0,1:T(2,128)} %copy.71), calls=%async_computation.6 | async-start | bytes 2097152 | tf_op jit(solution)/shard_map/all_to_all | solution.py:53
  89.9 25.0 %copy-start.35 = (s32[2]{0:T(128)S(1)}, s32[2]{0:T(128)}, u32[]{:S(2)}) copy-start(s32[2]{0:T(128)} %copy-done.34) | copy-start | bytes 28
  109.0 57.0 %all-to-all-start.1 = ((f32[4,128,2,512]{3,2,0,1:T(2,128)}), f32[4,128,2,512]{3,2,0,1:T(2,128)}, u32[]{:S(2)}, u32[]{:S(2)}) async-start(f32[4,128,2,512]{3,2,0,1:T(2,128)} %copy.61), calls=%async_computation.1 | async-start | bytes 4194304 | tf_op jit(solution)/shard_map/all_to_all | solution.py:53
  114.9 237.8 %reduce-scatter.3.cloned.1.call-start = ((), (), s32[]{:S(2)}) async-start(), calls=%async_computation.10 | async-start | bytes 1310720 | tf_op jit(solution)/shard_map/reduce_scatter | solution.py:103
  122.1 46.3 %copy-start.3 = (f32[2,128,512]{2,1,0:T(8,128)}, f32[2,128,512]{2,1,0:T(8,128)S(1)}, u32[]{:S(2)}) copy-start(f32[2,128,512]{2,1,0:T(8,128)S(1)} %reshape.169) | copy-start | bytes 1572868
  173.5 4.5 copy-start.10
  181.3 2.6 copy-start.8
  183.9 9.5 %copy-start.4 = (f32[2,128,512]{2,1,0:T(8,128)S(1)}, f32[2,128,512]{2,1,0:T(8,128)}, u32[]{:S(2)}) copy-start(f32[2,128,512]{2,1,0:T(8,128)} %copy-done.3) | copy-start | bytes 1572868
  183.9 9.5 %copy-start.13 = (f32[1,2,128,512]{3,2,1,0:T(8,128)S(1)}, f32[1,2,128,512]{3,2,1,0:T(8,128)}, u32[]{:S(2)}) copy-start(f32[1,2,128,512]{3,2,1,0:T(8,128)} %fusion.6) | copy-start | bytes 1572868
  184.0 9.5 %copy-start.14 = (f32[128,2,512]{2,0,1:T(8,128)S(1)}, f32[128,2,512]{2,0,1:T(8,128)}, u32[]{:S(2)}) copy-start(f32[128,2,512]{2,0,1:T(8,128)} %fusion.40) | copy-start | bytes 1572868
  195.8 2.6 copy-start.27
  195.8 2.6 copy-start.29
  265.1 2.6 copy-start.6
  265.1 2.6 copy-start.7
  265.1 3.9 copy-start.5
  269.0 1.3 copy-start.28
  269.0 1.3 copy-start.30
  275.2 6.0 %copy-start.2 = (bf16[128,2048]{1,0:T(8,128)(2,1)S(1)}, bf16[128,2048]{1,0:T(8,128)(2,1)}, u32[]{:S(2)}) copy-start(bf16[128,2048]{1,0:T(8,128)(2,1)} %copy-done.1) | copy-start | bytes 1572868
  275.2 56.9 %all-to-all-start.6 = ((f32[4,2,128,512]{3,1,0,2:T(2,128)}), f32[4,2,128,512]{3,1,0,2:T(2,128)}, u32[]{:S(2)}, u32[]{:S(2)}) async-start(f32[4,2,128,512]{3,1,0,2:T(2,128)} %copy.75), calls=%async_computation.7 | async-start | bytes 4194304 | tf_op jit(solution)/shard_map/all_to_all | solution.py:72
  280.9 222.2 %reduce-scatter.5.cloned.1.call-start = ((), (), s32[]{:S(2)}) async-start(), calls=%async_computation.11 | async-start | bytes 4259840 | tf_op jit(solution)/shard_map/reduce_scatter | solution.py:145
  342.4 2.2 copy-start.9
  344.6 7.4 %copy-start.12 = (f32[128,512]{1,0:T(8,128)S(1)}, f32[128,512]{1,0:T(8,128)}, u32[]{:S(2)}) copy-start(f32[128,512]{1,0:T(8,128)} %copy-done.11) | copy-start | bytes 786436
  346.6 23.0 %all-to-all-start.7 = ((f32[2,64,2,512]{3,2,0,1:T(2,128)}), f32[2,64,2,512]{3,2,0,1:T(2,128)S(1)}, u32[]{:S(2)}, u32[]{:S(2)}) async-start(f32[2,64,2,512]{3,2,0,1:T(2,128)} %copy.77), calls=%async_computation.8 | async-start | bytes 1048576 | tf_op jit(solution)/shard_map/all_to_all | solution.py:80
  352.7 149.6 %copy-start.20 = (f32[1,512]{1,0:T(1,128)S(1)}, f32[1,512]{1,0:T(1,128)}, u32[]{:S(2)}) copy-start(f32[1,512]{1,0:T(1,128)} %copy-done.19) | copy-start | bytes 6148
  352.7 149.6 %copy-start.22 = (f32[1,512]{1,0:T(1,128)S(1)}, f32[1,512]{1,0:T(1,128)}, u32[]{:S(2)}) copy-start(f32[1,512]{1,0:T(1,128)} %copy-done.21) | copy-start | bytes 6148
  352.7 149.6 %copy-start.24 = (f32[1,512]{1,0:T(1,128)S(1)}, f32[1,512]{1,0:T(1,128)}, u32[]{:S(2)}) copy-start(f32[1,512]{1,0:T(1,128)} %copy-done.23) | copy-start | bytes 6148
  352.7 149.6 %copy-start.26 = (f32[1,512]{1,0:T(1,128)S(1)}, f32[1,512]{1,0:T(1,128)}, u32[]{:S(2)}) copy-start(f32[1,512]{1,0:T(1,128)} %copy-done.25) | copy-start | bytes 6148
  370.4 1.7 copy-start.16
  370.6 131.7 %collective-permute-start.1 = (f32[3,512]{1,0:T(4,128)S(1)}, f32[3,512]{1,0:T(4,128)S(1)}, u32[]{:S(2)}, u32[]{:S(2)}) collective-permute-start(f32[3,512]{1,0:T(4,128)S(1)} %slice.156), channel_id=1, source_target_pairs={{4,0},{8,4},{12,8},{16,12},{20,16},{24,20},{28,24},{32,28},{36,32}... | collective-permute-start | bytes 18440 | tf_op jit(solution)/shard_map/ppermute | solution.py:14
Sparse Core Ops, SparseCore 0:
  265.2 19.5 reduce-scatter.2
  290.1 145.6 reduce-scatter.4
where the time goes:
time: 518 us; the launch traced here: 510 us
  blocking collectives  196 us (38%)
  waiting for transfers between devices  143 us (28%)
  local copies, waits for them, and re-layouts  52.8 us (10%)
  matrix products  51.2 us (10%)
  starting transfers between devices  43.6 us (8%)
  between operations  15.3 us (3%)
  other arithmetic  8.31 us (2%)
    psum x1, blocking collectives, local(): grad_taps = lax.psum(jnp.stack(tap_rows, 0), 'seq')  129 us
    all_to_all x2, waiting for transfers between devices, panel_forward(): lax.all_to_all(jnp.concatenate([real_twist, imag_twist], 0), 'seq', split...  58.9 us
    all_to_all x1, waiting for transfers between devices, panel_inverse(): lax.all_to_all(jnp.concatenate([real_twist, imag_twist], 0), 'seq', split...  48.2 us
    all_to_all x1, blocking collectives, panel_inverse(): lax.all_to_all(jnp.concatenate([real_twist, imag_twist], 0), 'seq', split...  34 us
    all_to_all x2, waiting for transfers between devices, panel_forward(): lax.all_to_all(signal[:, None], 'seq', split_axis=2, concat_axis=1, tiled...  20.9 us
    all_to_all x1, blocking collectives, panel_inverse(): lax.all_to_all(signal, 'seq', split_axis=1, concat_axis=2, tiled=True)  18.6 us
    all_to_all x2, starting transfers between devices, panel_forward(): lax.all_to_all(signal[:, None], 'seq', split_axis=2, concat_axis=1, tiled...  17 us
    all_to_all x1, waiting for transfers between devices, panel_inverse(): lax.all_to_all(signal, 'seq', split_axis=1, concat_axis=2, tiled=True)  15.3 us
  transfers between devices with their start and end apart: 10, of which 6 were waited for; matrix products, arithmetic and copies ran while one was open for 13% of the time, Pallas kernels for 0%

commit v1 on v0

v1 whole, which is shorter than its diff:
```python
import functools
import math

import jax
import jax.numpy as jnp
import ml_dtypes
import numpy as np
from jax import lax
from jax.experimental import pallas as pl
from jax.experimental.pallas import tpu as pltpu
from jax.sharding import PartitionSpec as P

F32 = jnp.float32
BF16 = jnp.bfloat16
VMEM = pl.BlockSpec(memory_space=pltpu.VMEM)
SMEM = pl.BlockSpec(memory_space=pltpu.SMEM)


def split_table(table):
    high = table.astype(ml_dtypes.bfloat16)
    low = (table - high.astype(np.float64)).astype(ml_dtypes.bfloat16)
    return high, low


def transform_tables(coarse, fine):
    length = coarse * fine
    k1 = np.arange(coarse)[:, None] + 0.25
    angle = 2.0 * math.pi * k1 * np.arange(coarse)[None, :] / coarse
    first = np.concatenate([np.cos(angle), -np.sin(angle)], 0)
    high, low = split_table(first)
    first_cat = np.concatenate([high, high, low], 1)
    last = np.concatenate([np.cos(angle).T, -np.sin(angle).T], 1)
    high, low = split_table(last)
    last_cat = np.concatenate([high, high, low], 1)
    angle = 2.0 * math.pi * k1 * np.arange(fine)[None, :] / length
    twist = np.stack([np.cos(angle), np.sin(angle)], 0).astype(np.float32)
    angle = 2.0 * math.pi * (np.outer(np.arange(fine), np.arange(fine)) % fine) / fine
    cos, sin = np.cos(angle), np.sin(angle)
    forward = np.concatenate([np.concatenate([cos, -sin], 1), np.concatenate([sin, cos], 1)], 0)
    inverse = np.concatenate([np.concatenate([cos, sin], 1), np.concatenate([-sin, cos], 1)], 0) / length
    second = np.stack([*split_table(forward), *split_table(inverse)], 0)
    return first_cat, last_cat, twist, second


def split(value):
    high = value.astype(BF16)
    return high, (value - high.astype(F32)).astype(BF16)


def dot(a, b, dims=(((1,), (0,)), ((), ()))):
    return lax.dot_general(a, b, dims, preferred_element_type=F32)


NT = (((1,), (1,)), ((), ()))


def pre_kernel(me_ref, inputs_ref, filters_ref, gate_ref, w_ref, c0, c1, c2, c3, out_ref, gg_ref):
    chan = me_ref[1]
    width = inputs_ref.shape[1]
    owners = out_ref.shape[0]
    total = None
    for step, piece in enumerate((c0, c1, c2, c3)):
        owner = lax.rem(chan + 4 - step, 4)
        cols = pl.ds(pl.multiple_of(owner * width, width), width)
        term = dot(w_ref[:, cols], piece[...], NT)
        total = term if total is None else total + term
    gg_ref[...] = total
    grad_conv = total * gate_ref[...].astype(F32).T
    rows = [inputs_ref[...].astype(F32).T]
    filters = filters_ref[...].T
    high = filters.astype(BF16).astype(F32)
    rows += [high, grad_conv, filters - high]
    rows = [r.reshape(owners, 8, r.shape[1]) for r in rows]
    out_ref[...] = jnp.concatenate(rows, 1).astype(BF16)


def cot_kernel(me_ref, c0, c1, c2, c3, own_ref, send_ref, scratch):
    core = lax.rem(me_ref[0], 2)
    chan = me_ref[1]
    for step, piece in enumerate((c0, c1, c2, c3)):
        owner = lax.rem(chan + 4 - step, 4)
        flipped = piece[...].astype(F32).T.astype(BF16)
        scratch[pl.ds(owner * 8, 8)] = flipped.reshape(8, 2, 32, flipped.shape[1])
    own_ref[...] = scratch[:, core]
    send_ref[...] = scratch[:, 1 - core]


def conv_kernel(taps_ref, recv_ref, first_ref, last_ref, twist_ref, second_ref, out_ref, sig, stage, spec):
    blocks, _, fine = recv_ref.shape
    taps = taps_ref[...]
    lane = lax.broadcasted_iota(jnp.int32, (blocks, 8, fine), 2)
    received = recv_ref[...].astype(F32)
    given = received[:, 0:8]
    zero = jnp.zeros((1, 8, fine), F32)

    def delayed(value, t):
        if t == 0:
            return value
        turned = pltpu.roll(value, t, 2)
        return jnp.where(lane < t, jnp.concatenate([zero, turned[:-1]], 0), turned)

    mixed = jnp.zeros_like(given)
    for t in range(4):
        mixed = mixed + taps[:, t : t + 1][None] * delayed(given, t)
    sig[0] = mixed.reshape(blocks * 8, fine)
    sig[1] = (received[:, 8:16] + received[:, 24:32]).reshape(blocks * 8, fine)
    sig[2] = received[:, 16:24].reshape(blocks * 8, fine)

    twist_re, twist_im = twist_ref[0], twist_ref[1]
    for s in range(3):
        for pair in range(4):
            both = jnp.concatenate([sig[s, pl.ds(2 * pair + h, blocks, stride=8), :] for h in range(2)], 1)
            high, low = split(both)
            coarse = dot(first_ref[...], jnp.concatenate([high, low, high], 0))
            for h in range(2):
                re = coarse[:blocks, h * fine : (h + 1) * fine]
                im = coarse[blocks:, h * fine : (h + 1) * fine]
                new_re = re * twist_re + im * twist_im
                new_im = im * twist_re - re * twist_im
                rows = pl.ds((s * 8 + 2 * pair + h) * blocks, blocks)
                high, low = split(jnp.concatenate([new_re, new_im], 1))
                stage[rows, : 2 * fine] = high
                stage[rows, 2 * fine :] = low

    def second(rows, which):
        high = stage[rows, : 2 * fine]
        low = stage[rows, 2 * fine :]
        return dot(high, second_ref[which]) + dot(low, second_ref[which]) + dot(high, second_ref[which + 1])

    count = 8 * blocks
    for s in range(3):
        spec[pl.ds(s * count, count), :] = second(pl.ds(s * count, count), 0)
    for c in range(8):
        parts = []
        for s in range(3):
            rows = pl.ds((s * 8 + c) * blocks, blocks)
            parts.append((spec[rows, :fine], spec[rows, fine:]))
        (mr, mi), (fr, fi), (gr, gi) = parts
        products = (
            (mr * fr - mi * fi, mr * fi + mi * fr),
            (fr * gr + fi * gi, fr * gi - fi * gr),
            (mr * gr + mi * gi, mr * gi - mi * gr),
        )
        for s in range(3):
            rows = pl.ds((s * 8 + c) * blocks, blocks)
            high, low = split(jnp.concatenate(products[s], 1))
            stage[rows, : 2 * fine] = high
            stage[rows, 2 * fine :] = low
    for s in range(3):
        spec[pl.ds(s * count, count), :] = second(pl.ds(s * count, count), 2)
    for s in range(3):
        for pair in range(4):
            halves = []
            for h in range(2):
                rows = pl.ds((s * 8 + 2 * pair + h) * blocks, blocks)
                re, im = spec[rows, :fine], spec[rows, fine:]
                halves.append(jnp.concatenate([re * twist_re - im * twist_im, im * twist_re + re * twist_im], 0))
            high, low = split(jnp.concatenate(halves, 1))
            back = dot(last_ref[...], jnp.concatenate([high, low, high], 0))
            for h in range(2):
                sig[s, pl.ds(2 * pair + h, blocks, stride=8), :] = back[:, h * fine : (h + 1) * fine]

    convolved, grad_mixed, grad_filters = (sig[s].reshape(blocks, 8, fine) for s in range(3))
    grad_inputs = taps[:, 0:1][None] * grad_mixed
    for t in range(1, 4):
        turned = pltpu.roll(grad_mixed, fine - t, 2)
        ahead = jnp.where(lane >= fine - t, jnp.concatenate([turned[1:], zero], 0), turned)
        grad_inputs = grad_inputs + taps[:, t : t + 1][None] * ahead
    column = lax.broadcasted_iota(jnp.int32, (8, fine), 1)
    tap_tile = jnp.zeros((8, fine), F32)
    for t in range(4):
        total = jnp.sum(jnp.sum(delayed(given, t) * grad_mixed, axis=0), axis=1, keepdims=True)
        high = total.astype(BF16).astype(F32)
        tap_tile = jnp.where(column == t, high, tap_tile)
        tap_tile = jnp.where(column == t + 4, total - high, tap_tile)
    tap_rows = jnp.broadcast_to(tap_tile[None], (blocks, 8, fine))
    out_ref[...] = jnp.concatenate([convolved, grad_inputs, grad_filters, tap_rows], 1).astype(BF16)


def gate_kernel(recv_ref, gate_ref, gated_ref):
    blocks, _, rows = recv_ref.shape
    convolved = recv_ref[:, 0:16].astype(F32)[:, 0:8].reshape(blocks * 8, rows)
    gated_ref[...] = (gate_ref[...].astype(F32) * convolved.T).astype(BF16)


def weight_kernel(cot_own, cot_other, gated_own, gated_other, out_ref):
    depth = cot_own.shape[2]
    left = cot_own[...].reshape(-1, depth)
    right = cot_other[...].reshape(-1, depth)
    total = dot(left, gated_own[...]) + dot(right, gated_other[...])
    out_ref[...] = total.reshape(out_ref.shape).astype(BF16)


def post_kernel(me_ref, recv_ref, gated_ref, gg_ref, w_ref, gi_ref, gate_grad_ref, gf_ref, taps_ref, own_ref, s1, s2, s3):
    chan = me_ref[1]
    blocks, _, rows = recv_ref.shape
    width = blocks * 8
    received = recv_ref[...].astype(F32)
    convolved = received[:, 0:8].reshape(width, rows)
    gate_grad_ref[...] = (gg_ref[...] * convolved).T.astype(BF16)
    gi_ref[...] = received[:, 8:16].reshape(width, rows).T.astype(BF16)
    gf_ref[...] = received[:, 16:24].reshape(width, rows).T
    flat = received[:, 24:32].reshape(width, rows).T
    taps_ref[...] = flat[0:4] + flat[4:8]
    for step, out in enumerate((own_ref, s1, s2, s3)):
        owner = lax.rem(chan + step, 4)
        cols = pl.ds(pl.multiple_of(owner * width, width), width)
        out[...] = dot(gated_ref[...], w_ref[:, cols]).astype(out.dtype)


def sum_kernel(recv_ref, out_ref):
    out_ref[...] = jnp.sum(recv_ref[...].astype(F32), axis=0).T


def call(kernel, outs, in_specs, scratch=()):
    return pl.pallas_call(
        kernel,
        out_shape=outs,
        in_specs=in_specs,
        out_specs=jax.tree.map(lambda _: VMEM, outs),
        scratch_shapes=list(scratch),
        compiler_params=pltpu.CompilerParams(vmem_limit_bytes=50 * 1024 * 1024),
    )


def shifted(value, axis, steps):
    count = lax.axis_size(axis)
    return lax.ppermute(value, axis, [(i, (i + steps) % count) for i in range(count)])


def local(inputs, gate_branch, short_taps, filters, w_out, cotangent):
    shape = jax.ShapeDtypeStruct
    owners = lax.axis_size("seq")
    rows, width = inputs.shape
    me = jnp.stack([lax.axis_index("seq"), lax.axis_index("chan")]).astype(jnp.int32)
    tables = transform_tables(owners, rows)
    my_taps = lax.dynamic_slice_in_dim(short_taps, me[0] * 8, 8, 1).T

    pieces = [cotangent] + [shifted(cotangent, "chan", d) for d in (1, 2, 3)]
    packed, grad_gated = call(
        pre_kernel,
        (shape((owners, 32, rows), BF16), shape((width, rows), F32)),
        [SMEM] + [VMEM] * 8,
    )(me, inputs, filters, gate_branch, w_out, *pieces)
    received = lax.all_to_all(packed, "seq", 0, 0, tiled=True)

    cot_own, cot_send = call(
        cot_kernel,
        (shape((32, 32, rows), BF16), shape((32, 32, rows), BF16)),
        [SMEM] + [VMEM] * 4,
        [pltpu.VMEM((32, 2, 32, rows), BF16)],
    )(me, *pieces)
    swap = [(i, i ^ 1) for i in range(owners)]
    cot_other = lax.ppermute(cot_send, "seq", swap)

    returned = call(
        conv_kernel,
        shape((owners, 32, rows), BF16),
        [VMEM] * 6,
        [
            pltpu.VMEM((3, width, rows), F32),
            pltpu.VMEM((3 * width, 4 * rows), BF16),
            pltpu.VMEM((3 * width, 2 * rows), F32),
        ],
    )(my_taps, received, *[jnp.asarray(t) for t in tables])
    arrived = lax.all_to_all(returned, "seq", 0, 0, tiled=True)

    gated = call(gate_kernel, shape((rows, width), BF16), [VMEM] * 2)(arrived, gate_branch)
    gated_other = lax.ppermute(gated, "seq", swap)
    weight_terms = call(weight_kernel, shape((32, 32, width), BF16), [VMEM] * 4)(
        cot_own, cot_other, gated, gated_other
    )
    groups = [list(range(k, owners, 2)) for k in range(2)]
    weight_parts = lax.all_to_all(weight_terms, "seq", 0, 0, axis_index_groups=groups, tiled=True)

    grad_inputs, grad_gate, grad_filters, grad_taps, own, s1, s2, s3 = call(
        post_kernel,
        (
            shape((rows, width), BF16),
            shape((rows, width), BF16),
            shape((rows, width), F32),
            shape((4, width), F32),
            shape((rows, width), F32),
        )
        + (shape((rows, width), BF16),) * 3,
        [SMEM] + [VMEM] * 4,
    )(me, arrived, gated, grad_gated, w_out)
    others = [shifted(s, "chan", d) for d, s in ((1, s1), (2, s2), (3, s3))]
    output = (own + others[0].astype(F32) + others[1].astype(F32) + others[2].astype(F32)).astype(BF16)

    grad_wout = call(sum_kernel, shape((width, 32), F32), [VMEM])(weight_parts)
    return (output, grad_inputs, grad_gate, grad_filters, grad_taps, grad_wout)


def solution(mesh):
    in_specs = (
        P("seq", "chan"),
        P("seq", "chan"),
        P(None, "chan"),
        P("seq", "chan"),
        P("chan", None),
        P("seq", "chan"),
    )
    out_specs = (
        P("seq", "chan"),
        P("seq", "chan"),
        P("seq", "chan"),
        P("seq", "chan"),
        P(None, "chan"),
        P("chan", "seq"),
    )
    return jax.shard_map(local, mesh=mesh, in_specs=in_specs, out_specs=out_specs, check_vma=False)
```

time: 518 us -> 116 us (0.22); the launches traced: 510 us -> 114 us
  blocking collectives: 196 us -> 0 us
  waiting for transfers between devices: 143 us -> 61.7 us
  matrix products: 51.2 us -> 0 us
  local copies, waits for them, and re-layouts: 52.8 us -> 7.15 us
  between operations: 15.3 us -> 0.76 us
  Pallas kernels: 0 us -> 11.2 us
  starting transfers between devices: 43.6 us -> 32.8 us
  other arithmetic: 8.31 us -> 0.79 us
    psum x1 -> x0, blocking collectives: 129 us -> none  [local(): grad_taps = lax.psum(jnp.stack(tap_rows, 0), 'seq')]
    all_to_all x6 -> x3, waiting for transfers between devices: 143 us -> 49.1 us  [the longest x1 17.5 us: local(): received = lax.all_to_all(packed, 'seq', 0, 0, tiled=True)]
    all_to_all x2 -> x0, blocking collectives: 52.6 us -> none  [the longest x1 34 us: panel_inverse(): lax.all_to_all(jnp.concatenate([real_twist, imag_twist], 0), 'seq', split...]
    dot_general x27 -> x0, matrix products: 51.2 us -> none  [the longest x4 13.7 us: column_dft(): jnp.einsum(form, imag_part, cos_table, precision=HIGHEST)]
    slice x16 -> x0, local copies, waits for them, and re-layouts: 22.3 us -> none  [the longest x5 8.16 us: panel_forward(): by_rows[stack_size:]]
    all_to_all x6 -> x3, starting transfers between devices: 40.2 us -> 23.1 us  [the longest x1 12.1 us: local(): received = lax.all_to_all(packed, 'seq', 0, 0, tiled=True)]
    all_gather x1 -> x0, blocking collectives: 13.9 us -> none  [local(): full_cot = lax.all_gather(cotangent, 'chan', axis=1, tiled=True)]
    ppermute x2 -> x8, waiting for transfers between devices: 0.01 us -> 12.6 us  [the longest x6 11.3 us: shifted(): lax.ppermute(value, axis, [(i, (i + steps) % count) for i in range(count)])]
  transfers between devices with their start and end apart: 10 -> 11, of which waited for: 6 -> 10; matrix products, arithmetic and copies ran while one was open for 13% -> 1% of each run, Pallas kernels for 0% -> 3%
where the time goes in v1:
time: 116 us; the launch traced here: 114 us
  waiting for transfers between devices  61.7 us (53%)
  starting transfers between devices  32.8 us (28%)
  Pallas kernels  11.2 us (10%)
  local copies, waits for them, and re-layouts  7.15 us (6%)
    all_to_all x1, waiting for transfers between devices, local(): received = lax.all_to_all(packed, 'seq', 0, 0, tiled=True)  17.5 us
    all_to_all x1, waiting for transfers between devices, local(): arrived = lax.all_to_all(returned, 'seq', 0, 0, tiled=True)  16.1 us
    all_to_all x1, waiting for transfers between devices, local(): lax.all_to_all(weight_terms, 'seq', 0, 0, axis_index_groups=groups, tiled...  15.5 us
    all_to_all x1, starting transfers between devices, local(): received = lax.all_to_all(packed, 'seq', 0, 0, tiled=True)  12.1 us
    ppermute x6, waiting for transfers between devices, shifted(): lax.ppermute(value, axis, [(i, (i + steps) % count) for i in range(count)])  11.3 us
    ppermute x6, starting transfers between devices, shifted(): lax.ppermute(value, axis, [(i, (i + steps) % count) for i in range(count)])  9.42 us
    unnamed x30, local copies, waits for them, and re-layouts  7.07 us
    all_to_all x1, starting transfers between devices, local(): arrived = lax.all_to_all(returned, 'seq', 0, 0, tiled=True)  5.78 us
  transfers between devices with their start and end apart: 11, of which 10 were waited for; matrix products, arithmetic and copies ran while one was open for 1% of the time, Pallas kernels for 3%

profile of v1, /device:TPU:8, one launch (start us, length us, event | category | flops | bytes accessed | tf_op | source)
XLA Modules:
  0.0 114.4 jit_solution(1296776575087965244)
XLA Ops:
  0.6 0.0 copy-start
  0.6 1.7 %collective-permute-start = (bf16[128,512]{1,0:T(8,128)(2,1)}, bf16[128,512]{1,0:T(8,128)(2,1)S(1)}, u32[]{:S(2)}, u32[]{:S(2)}) collective-permute-start(bf16[128,512]{1,0:T(8,128)(2,1)} %c0.3), channel_id=1, source_target_pairs={{0,1},{1,2},{2,3},{3,0},{4,5},{5,6},{6,7},{7,4},{8,9},{9,10},{10,1... | collective-permute-start | bytes 393224 | tf_op jit(solution)/shard_map/ppermute | solution.py:228
  2.3 2.7 %collective-permute-start.1 = (bf16[128,512]{1,0:T(8,128)(2,1)}, bf16[128,512]{1,0:T(8,128)(2,1)S(1)}, u32[]{:S(2)}, u32[]{:S(2)}) collective-permute-start(bf16[128,512]{1,0:T(8,128)(2,1)} %c0.3), channel_id=1, source_target_pairs={{0,2},{1,3},{2,0},{3,1},{4,6},{5,7},{6,4},{7,5},{8,10},{9,11},{10,... | collective-permute-start | bytes 393224 | tf_op jit(solution)/shard_map/ppermute | solution.py:228
  5.0 0.7 collective-permute-start.2
  5.7 0.1 pad_add_fusion.me_ref
  5.7 0.6 collective-permute-done.c1
  6.3 4.1 %collective-permute-done.1.c2 = bf16[128,512]{1,0:T(8,128)(2,1)S(1)} collective-permute-done((bf16[128,512]{1,0:T(8,128)(2,1)}, bf16[128,512]{1,0:T(8,128)(2,1)S(1)}, u32[]{:S(2)}, u32[]{:S(2)}) %collective-permute-start.1) | collective-permute-done | bytes 131104 | tf_op jit(solution)/shard_map/ppermute | solution.py:228
  10.4 0.7 collective-permute-done.2.c3
  11.1 0.0 copy-start.1
  11.1 1.6 %copy-done.1 = bf16[512,2048]{1,0:T(8,128)(2,1)S(1)} copy-done((bf16[512,2048]{1,0:T(8,128)(2,1)S(1)}, bf16[512,2048]{1,0:T(8,128)(2,1)}, u32[]{:S(2)}) %copy-start.1) | copy-done | bytes 2097176
  12.7 0.0 copy-start.5
  12.7 0.9 copy-done.5
  13.6 0.0 copy-start.7
  13.6 0.9 copy-done.7
  14.5 0.0 copy-start.9
  14.5 0.9 copy-done.9
  15.5 0.0 copy-start.10
  15.5 0.9 copy-done.10
  16.4 0.0 copy-start.4
  16.4 0.0 copy-start.11
  16.4 0.0 copy-start.12
  16.4 0.0 copy-start.13
  16.4 2.1 %shard_map.145 = (bf16[64,32,128]{2,1,0:T(8,128)(2,1)}, f32[512,128]{1,0:T(8,128)S(1)}) custom-call(s32[2]{0:T(128)S(1)} %pad_add_fusion.me_ref, bf16[128,512]{1,0:T(8,128)(2,1)S(1)} %copy-done.10, f32[128,512]{1,0:T(8,128)S(1)} %copy-done.9, bf16[128,512]{1,0:T(8,128)(2,1)S(1)} %copy-done.7, bf16[512,2048]{1,0:T(8,128)(2,1)S(1)} %copy-done.1, ...), custom_call_target="tpu_custom_call" | custom-call | tf_op jit(solution)/shard_map/pallas_call | solution.py:240
  18.4 0.0 copy-start.6
  18.4 0.0 copy-start.8
  18.5 12.1 %all-to-all-start = ((bf16[64,32,128]{2,1,0:T(8,128)(2,1)}), bf16[64,32,128]{2,1,0:T(8,128)(2,1)S(1)}, u32[]{:S(2)}, u32[]{:S(2)}) async-start(bf16[64,32,128]{2,1,0:T(8,128)(2,1)} %get-tuple-element.18), calls=%async_computation | async-start | bytes 1048576 | tf_op jit(solution)/shard_map/all_to_all | solution.py:245
  30.5 0.0 copy-done
  30.5 0.1 constant_dynamic-slice_fusion
  30.6 0.1 copy.18
  30.7 17.5 %all-to-all-done.recv_ref = bf16[64,32,128]{2,1,0:T(8,128)(2,1)S(1)} async-done(((bf16[64,32,128]{2,1,0:T(8,128)(2,1)}), bf16[64,32,128]{2,1,0:T(8,128)(2,1)S(1)}, u32[]{:S(2)}, u32[]{:S(2)}) %all-to-all-start) | async-done | bytes 524320 | tf_op jit(solution)/shard_map/all_to_all | solution.py:245
  48.2 0.0 copy-done.4
  48.2 0.0 copy-done.11
  48.2 0.0 copy-done.12
  48.2 0.0 copy-done.13
  48.2 3.6 %shard_map.146 = bf16[64,32,128]{2,1,0:T(8,128)(2,1)} custom-call(f32[8,4]{1,0:T(8,128)S(1)} %bitcast.3, bf16[64,32,128]{2,1,0:T(8,128)(2,1)S(1)} %all-to-all-done.recv_ref, bf16[128,192]{1,0:T(8,128)(2,1)S(1)} %copy-done.11, bf16[64,384]{1,0:T(8,128)(2,1)S(1)} %copy-done.13, f32[2,64,128]{2,1,0:T(8,128)S(1)} %copy-done.12, bf16[4,256,256]{2,1,0:T(8,128)(2,1)S(1)} %copy-done.4), custom_call_target="tpu_custom_call" | custom-call | tf_op jit(solution)/shard_map/pallas_call | solution.py:256
  51.8 5.8 %all-to-all-start.1 = ((bf16[64,32,128]{2,1,0:T(8,128)(2,1)}), bf16[64,32,128]{2,1,0:T(8,128)(2,1)S(1)}, u32[]{:S(2)}, u32[]{:S(2)}) async-start(bf16[64,32,128]{2,1,0:T(8,128)(2,1)} %shard_map.146), calls=%async_computation.1 | async-start | bytes 1048576 | tf_op jit(solution)/shard_map/all_to_all | solution.py:266
  57.6 0.0 copy-done.6
  57.6 1.5 %shard_map.149 = (bf16[32,32,128]{2,1,0:T(8,128)(2,1)S(1)}, bf16[32,32,128]{2,1,0:T(8,128)(2,1)}) custom-call(s32[2]{0:T(128)S(1)} %pad_add_fusion.me_ref, bf16[128,512]{1,0:T(8,128)(2,1)S(1)} %copy-done.6, bf16[128,512]{1,0:T(8,128)(2,1)S(1)} %collective-permute-done.c1, bf16[128,512]{1,0:T(8,128)(2,1)S(1)} %collective-permute-done.1.c2, ...), custom_call_target="tpu_custom_call" | custom-call | tf_op jit(solution)/shard_map/pallas_call | solution.py:247
  59.1 0.1 collective-permute-start.6
  59.2 16.1 %all-to-all-done.1.recv_ref = bf16[64,32,128]{2,1,0:T(8,128)(2,1)S(1)} async-done(((bf16[64,32,128]{2,1,0:T(8,128)(2,1)}), bf16[64,32,128]{2,1,0:T(8,128)(2,1)S(1)}, u32[]{:S(2)}, u32[]{:S(2)}) %all-to-all-start.1) | async-done | bytes 524320 | tf_op jit(solution)/shard_map/all_to_all | solution.py:266
  75.3 0.0 copy-done.8
  75.3 0.1 shard_map.147.gated_ref.gated_own
  75.4 0.0 copy-start.2
  75.4 0.2 collective-permute-start.7
  75.6 0.0 collective-permute-done.6.cot_other
  75.6 1.2 %collective-permute-done.7.gated_other = bf16[128,512]{1,0:T(8,128)(2,1)S(1)} collective-permute-done((bf16[128,512]{1,0:T(8,128)(2,1)S(1)}, bf16[128,512]{1,0:T(8,128)(2,1)S(1)}, u32[]{:S(2)}, u32[]{:S(2)}) %collective-permute-start.7) | collective-permute-done | bytes 131104 | tf_op jit(solution)/shard_map/ppermute | solution.py:269
  76.8 0.7 shard_map.150
  77.5 0.0 copy-start.3
  77.5 1.0 copy-done.3
  78.5 5.3 %all-to-all-start.2 = ((bf16[32,32,512]{2,1,0:T(8,128)(2,1)}), bf16[32,32,512]{2,1,0:T(8,128)(2,1)}, u32[]{:S(2)}, u32[]{:S(2)}) async-start(bf16[32,32,512]{2,1,0:T(8,128)(2,1)} %copy-done.3), calls=%async_computation.2 | async-start | bytes 2097152 | tf_op jit(solution)/shard_map/all_to_all | solution.py:274
  83.8 0.0 copy-done.2
  83.8 1.7 %shard_map.148 = (bf16[128,512]{1,0:T(8,128)(2,1)}, bf16[128,512]{1,0:T(8,128)(2,1)}, f32[128,512]{1,0:T(8,128)}, f32[4,512]{1,0:T(4,128)}, f32[128,512]{1,0:T(8...) custom-call(s32[2]{0:T(128)S(1)} %pad_add_fusion.me_ref, ...), custom_call_target="tpu_custom_call" | custom-call | tf_op jit(solution)/shard_map/pallas_call | solution.py:276
  85.5 1.3 %collective-permute-start.3 = (bf16[128,512]{1,0:T(8,128)(2,1)S(1)}, bf16[128,512]{1,0:T(8,128)(2,1)S(1)}, u32[]{:S(2)}, u32[]{:S(2)}) collective-permute-start(bf16[128,512]{1,0:T(8,128)(2,1)S(1)} %get-tuple-element.21), channel_id=1, source_target_pairs={{0,1},{1,2},{2,3},{3,0},{4,5},{5,6},{6,7},{7,4},{8,9},{9,10},{10,1... | collective-permute-start | bytes 393224 | tf_op jit(solution)/shard_map/ppermute | solution.py:228
  86.8 1.6 %collective-permute-start.4 = (bf16[128,512]{1,0:T(8,128)(2,1)S(1)}, bf16[128,512]{1,0:T(8,128)(2,1)S(1)}, u32[]{:S(2)}, u32[]{:S(2)}) collective-permute-start(bf16[128,512]{1,0:T(8,128)(2,1)S(1)} %get-tuple-element.22), channel_id=1, source_target_pairs={{0,2},{1,3},{2,0},{3,1},{4,6},{5,7},{6,4},{7,5},{8,10},{9,11},{10,... | collective-permute-start | bytes 393224 | tf_op jit(solution)/shard_map/ppermute | solution.py:228
  88.4 1.6 %collective-permute-start.5 = (bf16[128,512]{1,0:T(8,128)(2,1)S(1)}, bf16[128,512]{1,0:T(8,128)(2,1)S(1)}, u32[]{:S(2)}, u32[]{:S(2)}) collective-permute-start(bf16[128,512]{1,0:T(8,128)(2,1)S(1)} %get-tuple-element.23), channel_id=1, source_target_pairs={{0,3},{1,0},{2,1},{3,2},{4,7},{5,4},{6,5},{7,6},{8,11},{9,8},{10,9... | collective-permute-start | bytes 393224 | tf_op jit(solution)/shard_map/ppermute | solution.py:228
  89.9 1.5 %collective-permute-done.3 = bf16[128,512]{1,0:T(8,128)(2,1)S(1)} collective-permute-done((bf16[128,512]{1,0:T(8,128)(2,1)S(1)}, bf16[128,512]{1,0:T(8,128)(2,1)S(1)}, u32[]{:S(2)}, u32[]{:S(2)}) %collective-permute-start.3) | collective-permute-done | bytes 131104 | tf_op jit(solution)/shard_map/ppermute | solution.py:228
  91.5 3.3 %collective-permute-done.4 = bf16[128,512]{1,0:T(8,128)(2,1)S(1)} collective-permute-done((bf16[128,512]{1,0:T(8,128)(2,1)S(1)}, bf16[128,512]{1,0:T(8,128)(2,1)S(1)}, u32[]{:S(2)}, u32[]{:S(2)}) %collective-permute-start.4) | collective-permute-done | bytes 131104 | tf_op jit(solution)/shard_map/ppermute | solution.py:228
  94.7 1.2 %collective-permute-done.5 = bf16[128,512]{1,0:T(8,128)(2,1)S(1)} collective-permute-done((bf16[128,512]{1,0:T(8,128)(2,1)S(1)}, bf16[128,512]{1,0:T(8,128)(2,1)S(1)}, u32[]{:S(2)}, u32[]{:S(2)}) %collective-permute-start.5) | collective-permute-done | bytes 131104 | tf_op jit(solution)/shard_map/ppermute | solution.py:228
  95.9 0.7 add_convert_fusion
  96.6 15.5 %all-to-all-done.2.recv_ref = bf16[32,32,512]{2,1,0:T(8,128)(2,1)} async-done(((bf16[32,32,512]{2,1,0:T(8,128)(2,1)}), bf16[32,32,512]{2,1,0:T(8,128)(2,1)}, u32[]{:S(2)}, u32[]{:S(2)}) %all-to-all-start.2) | async-done | bytes 1048608 | tf_op jit(solution)/shard_map/all_to_all | solution.py:274
  112.1 1.5 %shard_map.151 = f32[512,32]{1,0:T(8,128)S(1)} custom-call(bf16[32,32,512]{2,1,0:T(8,128)(2,1)} %all-to-all-done.2.recv_ref), custom_call_target="tpu_custom_call" | custom-call | tf_op jit(solution)/shard_map/pallas_call | solution.py:291
  113.6 0.7 copy.17
Async XLA Ops:
  0.6 29.9 %copy-start = (f32[4,512]{1,0:T(4,128)S(1)}, f32[4,512]{1,0:T(4,128)}, u32[]{:S(2)}) copy-start(f32[4,512]{1,0:T(4,128)} %param.12) | copy-start | bytes 24580
  0.6 5.7 %collective-permute-start = (bf16[128,512]{1,0:T(8,128)(2,1)}, bf16[128,512]{1,0:T(8,128)(2,1)S(1)}, u32[]{:S(2)}, u32[]{:S(2)}) collective-permute-start(bf16[128,512]{1,0:T(8,128)(2,1)} %c0.3), channel_id=1, source_target_pairs={{0,1},{1,2},{2,3},{3,0},{4,5},{5,6},{6,7},{7,4},{8,9},{9,10},{10,1... | collective-permute-start | bytes 393224 | tf_op jit(solution)/shard_map/ppermute | solution.py:228
  2.3 8.1 %collective-permute-start.1 = (bf16[128,512]{1,0:T(8,128)(2,1)}, bf16[128,512]{1,0:T(8,128)(2,1)S(1)}, u32[]{:S(2)}, u32[]{:S(2)}) collective-permute-start(bf16[128,512]{1,0:T(8,128)(2,1)} %c0.3), channel_id=1, source_target_pairs={{0,2},{1,3},{2,0},{3,1},{4,6},{5,7},{6,4},{7,5},{8,10},{9,11},{10,... | collective-permute-start | bytes 393224 | tf_op jit(solution)/shard_map/ppermute | solution.py:228
  5.0 6.1 %collective-permute-start.2 = (bf16[128,512]{1,0:T(8,128)(2,1)}, bf16[128,512]{1,0:T(8,128)(2,1)S(1)}, u32[]{:S(2)}, u32[]{:S(2)}) collective-permute-start(bf16[128,512]{1,0:T(8,128)(2,1)} %c0.3), channel_id=1, source_target_pairs={{0,3},{1,0},{2,1},{3,2},{4,7},{5,4},{6,5},{7,6},{8,11},{9,8},{10,9... | collective-permute-start | bytes 393224 | tf_op jit(solution)/shard_map/ppermute | solution.py:228
  11.1 1.6 %copy-start.1 = (bf16[512,2048]{1,0:T(8,128)(2,1)S(1)}, bf16[512,2048]{1,0:T(8,128)(2,1)}, u32[]{:S(2)}) copy-start(bf16[512,2048]{1,0:T(8,128)(2,1)} %w_ref.3) | copy-start | bytes 6291460
  12.7 0.9 copy-start.5
  13.6 0.9 copy-start.7
  14.5 0.9 copy-start.9
  15.5 0.9 copy-start.10
  16.4 31.8 %copy-start.4 = (bf16[4,256,256]{2,1,0:T(8,128)(2,1)S(1)}, bf16[4,256,256]{2,1,0:T(8,128)(2,1)}, u32[]{:S(2)}) copy-start(bf16[4,256,256]{2,1,0:T(8,128)(2,1)} %constant.26.clone.second_ref) | copy-start | bytes 1572868
  16.4 31.8 %copy-start.11 = (bf16[128,192]{1,0:T(8,128)(2,1)S(1)}, bf16[128,192]{1,0:T(8,128)(2,1)}, u32[]{:S(2)}) copy-start(bf16[128,192]{1,0:T(8,128)(2,1)} %constant.23.clone.first_ref) | copy-start | bytes 147460
  16.4 31.8 %copy-start.12 = (f32[2,64,128]{2,1,0:T(8,128)S(1)}, f32[2,64,128]{2,1,0:T(8,128)}, u32[]{:S(2)}) copy-start(f32[2,64,128]{2,1,0:T(8,128)} %constant.25.clone.twist_ref) | copy-start | bytes 196612
  16.4 31.8 %copy-start.13 = (bf16[64,384]{1,0:T(8,128)(2,1)S(1)}, bf16[64,384]{1,0:T(8,128)(2,1)}, u32[]{:S(2)}) copy-start(bf16[64,384]{1,0:T(8,128)(2,1)} %constant.24.clone.last_ref) | copy-start | bytes 147460
  18.4 39.2 %copy-start.6 = (bf16[128,512]{1,0:T(8,128)(2,1)S(1)}, bf16[128,512]{1,0:T(8,128)(2,1)}, u32[]{:S(2)}) copy-start(bf16[128,512]{1,0:T(8,128)(2,1)} %c0.3) | copy-start | bytes 393220
  18.4 56.8 %copy-start.8 = (bf16[128,512]{1,0:T(8,128)(2,1)S(1)}, bf16[128,512]{1,0:T(8,128)(2,1)}, u32[]{:S(2)}) copy-start(bf16[128,512]{1,0:T(8,128)(2,1)} %gate_ref.3) | copy-start | bytes 393220
  18.5 29.7 %all-to-all-start = ((bf16[64,32,128]{2,1,0:T(8,128)(2,1)}), bf16[64,32,128]{2,1,0:T(8,128)(2,1)S(1)}, u32[]{:S(2)}, u32[]{:S(2)}) async-start(bf16[64,32,128]{2,1,0:T(8,128)(2,1)} %get-tuple-element.18), calls=%async_computation | async-start | bytes 1048576 | tf_op jit(solution)/shard_map/all_to_all | solution.py:245
  51.8 23.4 %all-to-all-start.1 = ((bf16[64,32,128]{2,1,0:T(8,128)(2,1)}), bf16[64,32,128]{2,1,0:T(8,128)(2,1)S(1)}, u32[]{:S(2)}, u32[]{:S(2)}) async-start(bf16[64,32,128]{2,1,0:T(8,128)(2,1)} %shard_map.146), calls=%async_computation.1 | async-start | bytes 1048576 | tf_op jit(solution)/shard_map/all_to_all | solution.py:266
  59.1 16.5 %collective-permute-start.6 = (bf16[32,32,128]{2,1,0:T(8,128)(2,1)}, bf16[32,32,128]{2,1,0:T(8,128)(2,1)S(1)}, u32[]{:S(2)}, u32[]{:S(2)}) collective-permute-start(bf16[32,32,128]{2,1,0:T(8,128)(2,1)} %get-tuple-element.29), channel_id=1, source_target_pairs={{0,4},{4,0},{8,12},{12,8},{16,20},{20,16},{24,28},{28,24},{32,36},... | collective-permute-start | bytes 786440 | tf_op jit(solution)/shard_map/ppermute | solution.py:254
  75.4 8.4 %copy-start.2 = (bf16[512,2048]{1,0:T(8,128)(2,1)S(1)}, bf16[512,2048]{1,0:T(8,128)(2,1)}, u32[]{:S(2)}) copy-start(bf16[512,2048]{1,0:T(8,128)(2,1)} %w_ref.3) | copy-start | bytes 6291460
  75.4 1.4 %collective-permute-start.7 = (bf16[128,512]{1,0:T(8,128)(2,1)S(1)}, bf16[128,512]{1,0:T(8,128)(2,1)S(1)}, u32[]{:S(2)}, u32[]{:S(2)}) collective-permute-start(bf16[128,512]{1,0:T(8,128)(2,1)S(1)} %shard_map.147.gated_ref.gated_own), channel_id=1, source_target_pairs={{0,4},{4,0},{8,12},{12,8},{16,20},{20,16},{24,28},{28,24},{32,36},... | collective-permute-start | bytes 393224 | tf_op jit(solution)/shard_map/ppermute | solution.py:269
  77.5 1.0 copy-start.3
  78.5 33.6 %all-to-all-start.2 = ((bf16[32,32,512]{2,1,0:T(8,128)(2,1)}), bf16[32,32,512]{2,1,0:T(8,128)(2,1)}, u32[]{:S(2)}, u32[]{:S(2)}) async-start(bf16[32,32,512]{2,1,0:T(8,128)(2,1)} %copy-done.3), calls=%async_computation.2 | async-start | bytes 2097152 | tf_op jit(solution)/shard_map/all_to_all | solution.py:274
  85.5 6.0 %collective-permute-start.3 = (bf16[128,512]{1,0:T(8,128)(2,1)S(1)}, bf16[128,512]{1,0:T(8,128)(2,1)S(1)}, u32[]{:S(2)}, u32[]{:S(2)}) collective-permute-start(bf16[128,512]{1,0:T(8,128)(2,1)S(1)} %get-tuple-element.21), channel_id=1, source_target_pairs={{0,1},{1,2},{2,3},{3,0},{4,5},{5,6},{6,7},{7,4},{8,9},{9,10},{10,1... | collective-permute-start | bytes 393224 | tf_op jit(solution)/shard_map/ppermute | solution.py:228
  86.8 7.9 %collective-permute-start.4 = (bf16[128,512]{1,0:T(8,128)(2,1)S(1)}, bf16[128,512]{1,0:T(8,128)(2,1)S(1)}, u32[]{:S(2)}, u32[]{:S(2)}) collective-permute-start(bf16[128,512]{1,0:T(8,128)(2,1)S(1)} %get-tuple-element.22), channel_id=1, source_target_pairs={{0,2},{1,3},{2,0},{3,1},{4,6},{5,7},{6,4},{7,5},{8,10},{9,11},{10,... | collective-permute-start | bytes 393224 | tf_op jit(solution)/shard_map/ppermute | solution.py:228
  88.4 7.5 %collective-permute-start.5 = (bf16[128,512]{1,0:T(8,128)(2,1)S(1)}, bf16[128,512]{1,0:T(8,128)(2,1)S(1)}, u32[]{:S(2)}, u32[]{:S(2)}) collective-permute-start(bf16[128,512]{1,0:T(8,128)(2,1)S(1)} %get-tuple-element.23), channel_id=1, source_target_pairs={{0,3},{1,0},{2,1},{3,2},{4,7},{5,4},{6,5},{7,6},{8,11},{9,8},{10,9... | collective-permute-start | bytes 393224 | tf_op jit(solution)/shard_map/ppermute | solution.py:228

commit v2 on v1

v2 whole, which is shorter than its diff:
```python
import functools
import math

import jax
import jax.numpy as jnp
import ml_dtypes
import numpy as np
from jax import lax
from jax.experimental import pallas as pl
from jax.experimental.pallas import tpu as pltpu
from jax.sharding import PartitionSpec as P

F32 = jnp.float32
BF16 = jnp.bfloat16
VMEM = pl.BlockSpec(memory_space=pltpu.VMEM)
SMEM = pl.BlockSpec(memory_space=pltpu.SMEM)
ANY = pl.BlockSpec(memory_space=pl.ANY)


def split_table(table):
    high = table.astype(ml_dtypes.bfloat16)
    low = (table - high.astype(np.float64)).astype(ml_dtypes.bfloat16)
    return high, low


def transform_tables(coarse, fine):
    length = coarse * fine
    k1 = np.arange(coarse)[:, None] + 0.25
    angle = 2.0 * math.pi * k1 * np.arange(coarse)[None, :] / coarse
    first = np.concatenate([np.cos(angle), -np.sin(angle)], 0)
    high, low = split_table(first)
    first_cat = np.concatenate([high, high, low], 1)
    last = np.concatenate([np.cos(angle).T, -np.sin(angle).T], 1)
    high, low = split_table(last)
    last_cat = np.concatenate([high, high, low], 1)
    angle = 2.0 * math.pi * k1 * np.arange(fine)[None, :] / length
    twist = np.stack([np.cos(angle), np.sin(angle)], 0).astype(np.float32)
    angle = 2.0 * math.pi * (np.outer(np.arange(fine), np.arange(fine)) % fine) / fine
    cos, sin = np.cos(angle), np.sin(angle)
    forward = np.concatenate([np.concatenate([cos, -sin], 1), np.concatenate([sin, cos], 1)], 0)
    inverse = np.concatenate([np.concatenate([cos, sin], 1), np.concatenate([-sin, cos], 1)], 0) / length
    second = np.stack([*split_table(forward), *split_table(inverse)], 0)
    return first_cat, last_cat, twist, second


def split(value):
    high = value.astype(BF16)
    return high, (value - high.astype(F32)).astype(BF16)


def dot(a, b, dims=(((1,), (0,)), ((), ()))):
    return lax.dot_general(a, b, dims, preferred_element_type=F32)


NT = (((1,), (1,)), ((), ()))


def load(sources, buffers, sems):
    copies = [pltpu.make_async_copy(src, dst, sems.at[i]) for i, (src, dst) in enumerate(zip(sources, buffers))]
    for copy in copies:
        copy.start()
    for copy in copies:
        copy.wait()


def pack_kernel(inputs_hbm, filters_hbm, out_ref, inputs_ref, filters_ref, sems):
    load((inputs_hbm, filters_hbm), (inputs_ref, filters_ref), sems)
    owners = out_ref.shape[0]
    filters = filters_ref[...].T
    high = filters.astype(BF16).astype(F32)
    rows = [inputs_ref[...].astype(F32).T, high, filters - high]
    rows = [r.reshape(owners, 8, r.shape[1]) for r in rows]
    out_ref[...] = jnp.concatenate(rows, 1).astype(BF16)


def cotangent_kernel(me_ref, gate_hbm, w_hbm, c0_hbm, c1, c2, c3, out_ref, gg_ref, gate_ref, w_ref, c0, sems):
    load((gate_hbm, w_hbm, c0_hbm), (gate_ref, w_ref, c0), sems)
    chan = me_ref[1]
    width = gate_ref.shape[1]
    total = None
    for step, piece in enumerate((c0, c1, c2, c3)):
        owner = lax.rem(chan + 4 - step, 4)
        cols = pl.ds(pl.multiple_of(owner * width, width), width)
        term = dot(w_ref[:, cols], piece[...], NT)
        total = term if total is None else total + term
    gg_ref[...] = total
    out_ref[...] = (total * gate_ref[...].astype(F32).T).astype(BF16)


def cot_kernel(me_ref, c0, c1, c2, c3, o0, o1, o2, o3, scratch):
    kind = lax.rem(me_ref[0], 4)
    chan = me_ref[1]
    for step, piece in enumerate((c0, c1, c2, c3)):
        owner = lax.rem(chan + 4 - step, 4)
        flipped = piece[...].astype(F32).T.astype(BF16)
        scratch[pl.ds(owner * 4, 4)] = flipped.reshape(4, 4, 32, flipped.shape[1])
    for d, out in enumerate((o0, o1, o2, o3)):
        out[...] = scratch[:, kind ^ d]


def delayed(value, t):
    if t == 0:
        return value
    lane = lax.broadcasted_iota(jnp.int32, value.shape, 2)
    turned = pltpu.roll(value, t, 2)
    before = jnp.concatenate([jnp.zeros_like(turned[:1]), turned[:-1]], 0)
    return jnp.where(lane < t, before, turned)


def coarse_stage(sig, s, first_ref, twist_ref, stage):
    blocks, fine = twist_ref.shape[1:]
    twist_re, twist_im = twist_ref[0], twist_ref[1]
    for pair in range(4):
        both = jnp.concatenate([sig[s, pl.ds(2 * pair + h, blocks, stride=8), :] for h in range(2)], 1)
        high, low = split(both)
        coarse = dot(first_ref[...], jnp.concatenate([high, low, high], 0))
        for h in range(2):
            re = coarse[:blocks, h * fine : (h + 1) * fine]
            im = coarse[blocks:, h * fine : (h + 1) * fine]
            put(stage, s, 2 * pair + h, re * twist_re + im * twist_im, im * twist_re - re * twist_im)


def put(stage, s, c, re, im):
    blocks, fine = re.shape
    rows = pl.ds((s * 8 + c) * blocks, blocks)
    high, low = split(jnp.concatenate([re, im], 1))
    stage[rows, : 2 * fine] = high
    stage[rows, 2 * fine :] = low


def fine_stage(stage, s, second_ref, which):
    count = stage.shape[1]
    rows = pl.ds(s * count, count)
    high = stage[rows, : stage.shape[1] // 2]
    low = stage[rows, stage.shape[1] // 2 :]
    return dot(high, second_ref[which]) + dot(low, second_ref[which]) + dot(high, second_ref[which + 1])


def back_stage(spec, s, last_ref, twist_ref, sig):
    blocks, fine = twist_ref.shape[1:]
    twist_re, twist_im = twist_ref[0], twist_ref[1]
    for pair in range(4):
        halves = []
        for h in range(2):
            rows = pl.ds((s * 8 + 2 * pair + h) * blocks, blocks)
            re, im = spec[rows, :fine], spec[rows, fine:]
            halves.append(jnp.concatenate([re * twist_re - im * twist_im, im * twist_re + re * twist_im], 0))
        high, low = split(jnp.concatenate(halves, 1))
        back = dot(last_ref[...], jnp.concatenate([high, low, high], 0))
        for h in range(2):
            sig[s, pl.ds(2 * pair + h, blocks, stride=8), :] = back[:, h * fine : (h + 1) * fine]


def forward_kernel(taps_ref, recv_ref, grad_ref, first_ref, last_ref, twist_ref, second_ref, out_ref, spec, sig, stage, work):
    blocks, _, fine = recv_ref.shape
    count = 8 * blocks
    taps = taps_ref[...]
    received = recv_ref[...].astype(F32)
    given = received[:, 0:8]
    mixed = jnp.zeros_like(given)
    for t in range(4):
        mixed = mixed + taps[:, t : t + 1][None] * delayed(given, t)
    sig[0] = mixed.reshape(count, fine)
    sig[1] = (received[:, 8:16] + received[:, 16:24]).reshape(count, fine)
    for s in range(2):
        coarse_stage(sig, s, first_ref, twist_ref, stage)
    for s in range(2):
        spec[pl.ds(s * count, count), :] = fine_stage(stage, s, second_ref, 0)
    for c in range(8):
        (mr, mi), (fr, fi) = (
            (spec[pl.ds((s * 8 + c) * blocks, blocks), :fine], spec[pl.ds((s * 8 + c) * blocks, blocks), fine:])
            for s in range(2)
        )
        put(stage, 0, c, mr * fr - mi * fi, mr * fi + mi * fr)
    work[...] = fine_stage(stage, 0, second_ref, 2)
    back_stage(work, 0, last_ref, twist_ref, sig)
    convolved = sig[0].reshape(blocks, 8, fine)
    grad_conv = grad_ref[...].astype(F32).reshape(blocks, 8, fine)
    out_ref[...] = jnp.concatenate([convolved, grad_conv], 1).astype(BF16)


def backward_kernel(
    me_ref, taps_ref, recv_ref, back_ref, spec, first_ref, last_ref, twist_ref, second_ref,
    o0, o1, o2, o3, sig, stage, work, parts
):
    blocks, _, fine = recv_ref.shape
    count = 8 * blocks
    taps = taps_ref[...]
    sig[0] = back_ref[...].astype(F32)[:, 8:16].reshape(count, fine)
    coarse_stage(sig, 0, first_ref, twist_ref, stage)
    work[pl.ds(0, count), :] = fine_stage(stage, 0, second_ref, 0)
    for c in range(8):
        rows = pl.ds(c * blocks, blocks)
        gr, gi = work[rows, :fine], work[rows, fine:]
        for s in range(2):
            rows = pl.ds(((1 - s) * 8 + c) * blocks, blocks)
            re, im = spec[rows, :fine], spec[rows, fine:]
            put(stage, s, c, re * gr + im * gi, re * gi - im * gr)
    for s in range(2):
        work[pl.ds(s * count, count), :] = fine_stage(stage, s, second_ref, 2)
    for s in range(2):
        back_stage(work, s, last_ref, twist_ref, sig)
    grad_mixed, grad_filters = (sig[s].reshape(blocks, 8, fine) for s in range(2))
    lane = lax.broadcasted_iota(jnp.int32, (blocks, 8, fine), 2)
    zero = jnp.zeros((1, 8, fine), F32)
    grad_inputs = taps[:, 0:1][None] * grad_mixed
    for t in range(1, 4):
        turned = pltpu.roll(grad_mixed, fine - t, 2)
        ahead = jnp.where(lane >= fine - t, jnp.concatenate([turned[1:], zero], 0), turned)
        grad_inputs = grad_inputs + taps[:, t : t + 1][None] * ahead
    given = recv_ref[...].astype(F32)[:, 0:8]
    column = lax.broadcasted_iota(jnp.int32, (8, fine), 1)
    tap_tile = jnp.zeros((8, fine), F32)
    for t in range(4):
        total = jnp.sum(jnp.sum(delayed(given, t) * grad_mixed, axis=0), axis=1, keepdims=True)
        high = total.astype(BF16).astype(F32)
        tap_tile = jnp.where(column == t, high, tap_tile)
        tap_tile = jnp.where(column == t + 4, total - high, tap_tile)
    tap_rows = jnp.broadcast_to(tap_tile[None], (blocks, 8, fine))
    parts[...] = jnp.concatenate([grad_inputs, grad_filters, tap_rows], 1).reshape(blocks // 4, 4, 24, fine)
    kind = lax.rem(me_ref[0], 4)
    for d, out in enumerate((o0, o1, o2, o3)):
        out[...] = parts[:, kind ^ d].astype(BF16)


def gate_kernel(recv_ref, gate_ref, gated_ref):
    blocks, _, rows = recv_ref.shape
    convolved = recv_ref[...].astype(F32)[:, 0:8].reshape(blocks * 8, rows)
    gated_ref[...] = (gate_ref[...].astype(F32) * convolved.T).astype(BF16)


def weight_kernel(k0, k1, k2, k3, g0, g1, g2, g3, p0, p1, p2, p3, out_ref):
    groups, rows, depth = k0.shape
    left = jnp.concatenate([k[...].reshape(groups * rows, depth) for k in (k0, k1, k2, k3)], 1)
    total = dot(left, jnp.concatenate([g[...] for g in (g0, g1, g2, g3)], 0))
    for j in range(4):
        columns = total[:, j * depth : (j + 1) * depth].reshape(groups, rows, depth)
        out_ref[:, 64 + j * rows : 64 + (j + 1) * rows, :] = columns.astype(BF16)
    tap_rows = None
    for d, part in enumerate((p0, p1, p2, p3)):
        value = part[...].astype(F32)
        out_ref[:, 16 * d : 16 * (d + 1), :] = value[:, 0:16].astype(BF16)
        tile = pltpu.roll(value[:, 16:24], 8 * d, 2) if d else value[:, 16:24]
        tap_rows = tile if tap_rows is None else tap_rows + tile
    out_ref[:, 192:208, :] = jnp.concatenate([tap_rows, jnp.zeros_like(tap_rows)], 1).astype(BF16)


def project_kernel(me_ref, recv_ref, gated_ref, gg_ref, w_ref, gate_grad_ref, own_ref, s1, s2, s3):
    chan = me_ref[1]
    blocks, _, rows = recv_ref.shape
    width = gated_ref.shape[1]
    convolved = recv_ref[...].astype(F32)[:, 0:8].reshape(width, rows)
    gate_grad_ref[...] = (gg_ref[...] * convolved).T.astype(BF16)
    for step, out in enumerate((own_ref, s1, s2, s3)):
        owner = lax.rem(chan + step, 4)
        cols = pl.ds(pl.multiple_of(owner * width, width), width)
        out[...] = dot(gated_ref[...], w_ref[:, cols]).astype(out.dtype)


def unpack_kernel(me_ref, recv_ref, gi_ref, gf_ref, taps_ref, weight_ref, scratch):
    kind = lax.rem(me_ref[0], 4)
    groups, _, rows = recv_ref.shape
    width = groups * 32
    tap_rows = recv_ref[:, 192:208, :].astype(F32)[:, 0:8]
    for d in range(4):
        value = recv_ref[:, 16 * d : 16 * (d + 1), :].astype(F32)
        source = kind ^ d
        scratch[0, :, source] = value[:, 0:8]
        scratch[1, :, source] = value[:, 8:16]
        scratch[2, :, source] = pltpu.roll(tap_rows, rows - 8 * d, 2) if d else tap_rows
    gi_ref[...] = scratch[0].reshape(width, rows).T.astype(BF16)
    gf_ref[...] = scratch[1].reshape(width, rows).T
    flat = scratch[2].reshape(width, rows).T
    taps_ref[...] = flat[0:4] + flat[4:8]
    total = jnp.sum(recv_ref[:, 64:192, :].astype(F32), axis=0)
    for j in range(4):
        weight_ref[:, j * rows : (j + 1) * rows] = total[32 * j : 32 * (j + 1)]


def call(kernel, outs, in_specs, scratch=()):
    return pl.pallas_call(
        kernel,
        out_shape=outs,
        in_specs=in_specs,
        out_specs=jax.tree.map(lambda _: VMEM, outs),
        scratch_shapes=list(scratch),
        compiler_params=pltpu.CompilerParams(vmem_limit_bytes=50 * 1024 * 1024),
    )


def shifted(value, axis, steps):
    count = lax.axis_size(axis)
    return lax.ppermute(value, axis, [(i, (i + steps) % count) for i in range(count)])


def local(inputs, gate_branch, short_taps, filters, w_out, cotangent):
    shape = jax.ShapeDtypeStruct
    owners = lax.axis_size("seq")
    rows, width = inputs.shape
    me = jnp.stack([lax.axis_index("seq"), lax.axis_index("chan")]).astype(jnp.int32)
    tables = [jnp.asarray(t) for t in transform_tables(owners, rows)]
    my_taps = lax.dynamic_slice_in_dim(short_taps, me[0] * 8, 8, 1).T

    packed = call(
        pack_kernel,
        shape((owners, 24, rows), BF16),
        [ANY] * 2,
        [pltpu.VMEM((rows, width), BF16), pltpu.VMEM((rows, width), F32), pltpu.SemaphoreType.DMA((2,))],
    )(inputs, filters)
    received = lax.all_to_all(packed, "seq", 0, 0, tiled=True)

    pieces = [shifted(cotangent, "chan", d) for d in (1, 2, 3)]
    grad_packed, grad_gated = call(
        cotangent_kernel,
        (shape((width, rows), BF16), shape((width, rows), F32)),
        [SMEM] + [ANY] * 3 + [VMEM] * 3,
        [
            pltpu.VMEM((rows, width), BF16),
            pltpu.VMEM(w_out.shape, BF16),
            pltpu.VMEM((rows, width), BF16),
            pltpu.SemaphoreType.DMA((3,)),
        ],
    )(me, gate_branch, w_out, cotangent, *pieces)

    def work_space(signals):
        return [
            pltpu.VMEM((2, width, rows), F32),
            pltpu.VMEM((2 * width, 4 * rows), BF16),
            pltpu.VMEM((signals * width, 2 * rows), F32),
        ]

    def traded(values):
        return [values[0]] + [
            lax.ppermute(values[d], "seq", [(i, i ^ d) for i in range(owners)]) for d in (1, 2, 3)
        ]

    sent, spectra = call(
        forward_kernel,
        (shape((owners, 16, rows), BF16), shape((2 * width, 2 * rows), F32)),
        [VMEM] * 7,
        work_space(1),
    )(my_taps, received, grad_packed, *tables)
    back = lax.all_to_all(sent, "seq", 0, 0, tiled=True)

    cot_parts = traded(
        call(
            cot_kernel,
            (shape((16, 32, rows), BF16),) * 4,
            [SMEM] + [VMEM] * 4,
            [pltpu.VMEM((16, 4, 32, rows), BF16)],
        )(me, cotangent, *pieces)
    )

    gated = call(gate_kernel, shape((rows, width), BF16), [VMEM] * 2)(back, gate_branch)
    gated_parts = traded([gated] * 4)
    grad_parts = traded(
        call(
            backward_kernel,
            (shape((16, 24, rows), BF16),) * 4,
            [SMEM] + [VMEM] * 8,
            work_space(2) + [pltpu.VMEM((16, 4, 24, rows), F32)],
        )(me, my_taps, received, back, spectra, *tables)
    )
    last = call(weight_kernel, shape((16, 208, rows), BF16), [VMEM] * 12)(*cot_parts, *gated_parts, *grad_parts)
    groups = [list(range(k, owners, 4)) for k in range(4)]
    arrived = lax.all_to_all(last, "seq", 0, 0, axis_index_groups=groups, tiled=True)

    grad_gate, own, s1, s2, s3 = call(
        project_kernel,
        (shape((rows, width), BF16), shape((rows, width), F32)) + (shape((rows, width), BF16),) * 3,
        [SMEM] + [VMEM] * 4,
    )(me, back, gated, grad_gated, w_out)
    others = [shifted(s, "chan", d) for d, s in ((1, s1), (2, s2), (3, s3))]
    output = (own + others[0].astype(F32) + others[1].astype(F32) + others[2].astype(F32)).astype(BF16)

    grad_inputs, grad_filters, grad_taps, grad_wout = call(
        unpack_kernel,
        (
            shape((rows, width), BF16),
            shape((rows, width), F32),
            shape((4, width), F32),
            shape((32, width), F32),
        ),
        [SMEM, VMEM],
        [pltpu.VMEM((3, 16, 4, 8, rows), F32)],
    )(me, arrived)
    return (output, grad_inputs, grad_gate, grad_filters, grad_taps, grad_wout.T)


def solution(mesh):
    in_specs = (
        P("seq", "chan"),
        P("seq", "chan"),
        P(None, "chan"),
        P("seq", "chan"),
        P("chan", None),
        P("seq", "chan"),
    )
    out_specs = (
        P("seq", "chan"),
        P("seq", "chan"),
        P("seq", "chan"),
        P("seq", "chan"),
        P(None, "chan"),
        P("chan", "seq"),
    )
    return jax.shard_map(local, mesh=mesh, in_specs=in_specs, out_specs=out_specs, check_vma=False)
```

time: 116 us -> 107 us (0.922)
  waiting for transfers between devices: 61.7 us -> 42 us
  starting transfers between devices: 32.8 us -> 42.1 us
  Pallas kernels: 11.2 us -> 13.9 us
    all_to_all x1, waiting for transfers between devices: 17.5 us -> 0.01 us  [local(): received = lax.all_to_all(packed, 'seq', 0, 0, tiled=True)]
    all_to_all x2, waiting for transfers between devices: 31.6 us -> 22.4 us  [the longest x1 12.8 us: local(): lax.all_to_all(last, 'seq', 0, 0, axis_index_groups=groups, tiled=True)]
    ppermute x2 -> x9, waiting for transfers between devices: 1.23 us -> 8.24 us  [traded(): lax.ppermute(values[d], 'seq', [(i, i ^ d) for i in range(owners)])]
    ppermute x2 -> x9, starting transfers between devices: 0.26 us -> 6.06 us  [traded(): lax.ppermute(values[d], 'seq', [(i, i ^ d) for i in range(owners)])]
    all_to_all x2, starting transfers between devices: 11.1 us -> 14.7 us  [the longest x1 10.4 us: local(): back = lax.all_to_all(sent, 'seq', 0, 0, tiled=True)]
    pallas_call x7 -> x9, Pallas kernels: 11.2 us -> 13.9 us  [the longest x1 2.46 us: local(): call(backward_kernel, (shape((16, 24, rows), BF16),) * 4, [SMEM] + [VMEM]...]
    unnamed x30 -> x31, local copies, waits for them, and re-layouts: 7.07 us -> 6.38 us
  transfers between devices with their start and end apart: 11 -> 18, of which waited for: 10 -> 10; matrix products, arithmetic and copies ran while one was open for 1% -> 1% of each run, Pallas kernels for 3% -> 7%
where the time goes in v2:
time: 107 us; the launch traced here: 106 us
  starting transfers between devices  42.1 us (39%)
  waiting for transfers between devices  42 us (39%)
  Pallas kernels  13.9 us (13%)
  local copies, waits for them, and re-layouts  6.45 us (6%)
    all_to_all x1, waiting for transfers between devices, local(): lax.all_to_all(last, 'seq', 0, 0, axis_index_groups=groups, tiled=True)  12.8 us
    all_to_all x1, starting transfers between devices, local(): received = lax.all_to_all(packed, 'seq', 0, 0, tiled=True)  11.9 us
    ppermute x6, waiting for transfers between devices, shifted(): lax.ppermute(value, axis, [(i, (i + steps) % count) for i in range(count)])  11.4 us
    all_to_all x1, starting transfers between devices, local(): back = lax.all_to_all(sent, 'seq', 0, 0, tiled=True)  10.4 us
    all_to_all x1, waiting for transfers between devices, local(): back = lax.all_to_all(sent, 'seq', 0, 0, tiled=True)  9.61 us
    ppermute x6, starting transfers between devices, shifted(): lax.ppermute(value, axis, [(i, (i + steps) % count) for i in range(count)])  9.41 us
    ppermute x9, waiting for transfers between devices, traded(): lax.ppermute(values[d], 'seq', [(i, i ^ d) for i in range(owners)])  8.24 us
    unnamed x31, local copies, waits for them, and re-layouts  6.38 us
  transfers between devices with their start and end apart: 18, of which 10 were waited for; matrix products, arithmetic and copies ran while one was open for 1% of the time, Pallas kernels for 7%

profile of v2, /device:TPU:8, one launch (start us, length us, event | category | flops | bytes accessed | tf_op | source)
XLA Modules:
  0.0 106.1 jit_solution(12255875765049813365)
XLA Ops:
  0.6 0.0 copy-start
  0.6 0.0 copy-start.3
  0.7 0.0 copy-start.8
  0.7 1.0 copy-done.8
  1.7 0.9 copy-done.14
  2.6 1.1 %shard_map.145 = bf16[64,24,128]{2,1,0:T(8,128)(2,1)} custom-call(bf16[128,512]{1,0:T(8,128)(2,1)S(1)} %copy-done.14, f32[128,512]{1,0:T(8,128)S(1)} %copy-done.8), custom_call_target="tpu_custom_call" | custom-call | tf_op jit(solution)/shard_map/pallas_call | solution.py:304
  3.7 11.9 %all-to-all-start = ((bf16[64,24,128]{2,1,0:T(8,128)(2,1)}), bf16[64,24,128]{2,1,0:T(8,128)(2,1)S(1)}, u32[]{:S(2)}, u32[]{:S(2)}) async-start(bf16[64,24,128]{2,1,0:T(8,128)(2,1)} %shard_map.145), calls=%async_computation | async-start | bytes 786432 | tf_op jit(solution)/shard_map/all_to_all | solution.py:310
  15.7 1.7 %collective-permute-start = (bf16[128,512]{1,0:T(8,128)(2,1)}, bf16[128,512]{1,0:T(8,128)(2,1)S(1)}, u32[]{:S(2)}, u32[]{:S(2)}) collective-permute-start(bf16[128,512]{1,0:T(8,128)(2,1)} %c0.1), channel_id=1, source_target_pairs={{0,1},{1,2},{2,3},{3,0},{4,5},{5,6},{6,7},{7,4},{8,9},{9,10},{10,1... | collective-permute-start | bytes 393224 | tf_op jit(solution)/shard_map/ppermute | solution.py:293
  17.3 0.9 collective-permute-start.1
  18.3 2.4 %collective-permute-start.2 = (bf16[128,512]{1,0:T(8,128)(2,1)}, bf16[128,512]{1,0:T(8,128)(2,1)S(1)}, u32[]{:S(2)}, u32[]{:S(2)}) collective-permute-start(bf16[128,512]{1,0:T(8,128)(2,1)} %c0.1), channel_id=1, source_target_pairs={{0,3},{1,0},{2,1},{3,2},{4,7},{5,4},{6,5},{7,6},{8,11},{9,8},{10,9... | collective-permute-start | bytes 393224 | tf_op jit(solution)/shard_map/ppermute | solution.py:293
  20.7 0.0 copy-done
  20.7 0.1 constant_dynamic-slice_fusion
  20.7 0.1 copy.17
  20.8 0.1 pad_add_fusion.me_ref
  20.9 0.6 collective-permute-done.c1
  21.5 3.9 %collective-permute-done.1.c2 = bf16[128,512]{1,0:T(8,128)(2,1)S(1)} collective-permute-done((bf16[128,512]{1,0:T(8,128)(2,1)}, bf16[128,512]{1,0:T(8,128)(2,1)S(1)}, u32[]{:S(2)}, u32[]{:S(2)}) %collective-permute-start.1) | collective-permute-done | bytes 131104 | tf_op jit(solution)/shard_map/ppermute | solution.py:293
  25.4 0.9 collective-permute-done.2.c3
  26.3 1.6 %copy-done.1 = bf16[512,2048]{1,0:T(8,128)(2,1)S(1)} copy-done((bf16[512,2048]{1,0:T(8,128)(2,1)S(1)}, bf16[512,2048]{1,0:T(8,128)(2,1)}, u32[]{:S(2)}) %copy-start.1) | copy-done | bytes 2097176
  27.9 0.9 copy-done.4
  28.8 0.9 copy-done.6
  29.7 1.8 %shard_map.146 = (bf16[512,128]{1,0:T(8,128)(2,1)S(1)}, f32[512,128]{1,0:T(8,128)S(1)}) custom-call(s32[2]{0:T(128)S(1)} %pad_add_fusion.me_ref, bf16[128,512]{1,0:T(8,128)(2,1)S(1)} %copy-done.6, bf16[512,2048]{1,0:T(8,128)(2,1)S(1)} %copy-done.1, bf16[128,512]{1,0:T(8,128)(2,1)S(1)} %copy-done.4, bf16[128,512]{1,0:T(8,128)(2,1)S(1)} %collective-permute-done.c1, ...), custom_call_target="tpu_custom_call" | custom-call | tf_op jit(solution)/shard_map/pallas_call | solution.py:313
  31.5 0.0 copy-start.9
  31.5 0.0 all-to-all-done.recv_ref
  31.5 0.0 copy-done.3
  31.5 0.0 copy-done.11
  31.6 0.0 copy-start.7
  31.6 2.4 %shard_map.147 = (bf16[64,16,128]{2,1,0:T(8,128)(2,1)}, f32[1024,256]{1,0:T(8,128)S(1)}) custom-call(f32[8,4]{1,0:T(8,128)S(1)} %bitcast.4, bf16[64,24,128]{2,1,0:T(8,128)(2,1)S(1)} %all-to-all-done.recv_ref, bf16[512,128]{1,0:T(8,128)(2,1)S(1)} %get-tuple-element.27.grad_ref, bf16[128,192]{1,0:T(8,128)(2,1)S(1)} %copy-done.11, ...), custom_call_target="tpu_custom_call" | custom-call | tf_op jit(solution)/shard_map/pallas_call | solution.py:337
  34.0 10.4 %all-to-all-start.1 = ((bf16[64,16,128]{2,1,0:T(8,128)(2,1)}), bf16[64,16,128]{2,1,0:T(8,128)(2,1)S(1)}, u32[]{:S(2)}, u32[]{:S(2)}) async-start(bf16[64,16,128]{2,1,0:T(8,128)(2,1)} %get-tuple-element.28), calls=%async_computation.1 | async-start | bytes 524288 | tf_op jit(solution)/shard_map/all_to_all | solution.py:343
  44.4 1.5 %shard_map.150 = (bf16[16,32,128]{2,1,0:T(8,128)(2,1)S(1)}, bf16[16,32,128]{2,1,0:T(8,128)(2,1)}, bf16[16,32,128]{2,1,0:T(8,128)(2,1)}, bf16[16,32,128]{2,1,0:T(8,128)(2,1)S(1)}) custom-call(s32[2]{0:T(128)S(1)} %pad_add_fusion.me_ref, bf16[128,512]{1,0:T(8,128)(2,1)S(1)} %copy-done.5, bf16[128,512]{1,0:T(8,128)(2,1)S(1)} %collective-permute-done.c1, ...), custom_call_target="tpu_custom_call" | custom-call | tf_op jit(solution)/shard_map/pallas_call | solution.py:346
  45.9 0.1 collective-permute-start.6
  46.0 1.7 %collective-permute-start.7 = (bf16[16,32,128]{2,1,0:T(8,128)(2,1)}, bf16[16,32,128]{2,1,0:T(8,128)(2,1)S(1)}, u32[]{:S(2)}, u32[]{:S(2)}) collective-permute-start(bf16[16,32,128]{2,1,0:T(8,128)(2,1)} %get-tuple-element.36), channel_id=1, source_target_pairs={{0,8},{4,12},{8,0},{12,4},{16,24},{20,28},{24,16},{28,20},{32,40},... | collective-permute-start | bytes 393224 | tf_op jit(solution)/shard_map/ppermute | solution.py:334
  47.7 0.1 collective-permute-start.8
  47.8 9.6 %all-to-all-done.1.recv_ref.back_ref = bf16[64,16,128]{2,1,0:T(8,128)(2,1)S(1)} async-done(((bf16[64,16,128]{2,1,0:T(8,128)(2,1)}), bf16[64,16,128]{2,1,0:T(8,128)(2,1)S(1)}, u32[]{:S(2)}, u32[]{:S(2)}) %all-to-all-start.1) | async-done | bytes 262176 | tf_op jit(solution)/shard_map/all_to_all | solution.py:343
  57.4 2.5 %shard_map.151 = (bf16[16,24,128]{2,1,0:T(8,128)(2,1)S(1)}, bf16[16,24,128]{2,1,0:T(8,128)(2,1)S(1)}, bf16[16,24,128]{2,1,0:T(8,128)(2,1)S(1)}, bf16[16,24,128]{2,1,0:T(8,128)(2,1)S(1)}) custom-call(s32[2]{0:T(128)S(1)} %pad_add_fusion.me_ref, f32[8,4]{1,0:T(8,128)S(1)} %bitcast.5, bf16[64,24,128]{2,1,0:T(8,128)(2,1)S(1)} %all-to-all-done.recv_ref, ...), custom_call_target="tpu_custom_call" | custom-call | tf_op jit(solution)/shard_map/pallas_call | solution.py:357
  59.9 0.3 collective-permute-start.12
  60.2 0.1 shard_map.148.gated_ref.g0
  60.3 0.0 copy-start.2
  60.3 0.8 collective-permute-start.10
  61.1 0.0 collective-permute-done.6.k1
  61.1 0.9 collective-permute-start.11
  62.0 0.0 collective-permute-done.7.k2
  62.0 0.5 collective-permute-start.9
  62.6 0.0 collective-permute-done.8.k3
  62.6 0.7 collective-permute-start.13
  63.3 0.0 collective-permute-done.12.p1
  63.3 0.9 collective-permute-start.14
  64.2 7.5 %collective-permute-done.13.p2 = bf16[16,24,128]{2,1,0:T(8,128)(2,1)S(1)} collective-permute-done((bf16[16,24,128]{2,1,0:T(8,128)(2,1)S(1)}, bf16[16,24,128]{2,1,0:T(8,128)(2,1)S(1)}, u32[]{:S(2)}, u32[]{:S(2)}) %collective-permute-start.13) | collective-permute-done | bytes 98336 | tf_op jit(solution)/shard_map/ppermute | solution.py:334
  71.7 0.8 collective-permute-done.14.p3
  72.4 0.0 collective-permute-done.10.g2
  72.4 0.0 collective-permute-done.11.g3
  72.4 0.0 collective-permute-done.9.g1
  72.4 1.4 %shard_map.152 = bf16[16,208,128]{2,1,0:T(8,128)(2,1)} custom-call(bf16[16,32,128]{2,1,0:T(8,128)(2,1)S(1)} %get-tuple-element.34.k0, bf16[16,32,128]{2,1,0:T(8,128)(2,1)S(1)} %collective-permute-done.6.k1, bf16[16,32,128]{2,1,0:T(8,128)(2,1)S(1)} %collective-permute-done.7.k2, bf16[16,32,128]{2,1,0:T(8,128)(2,1)S(1)} %collective-permute-done.8.k3, ...), custom_call_target="tpu_custom_call" | custom-call | tf_op jit(solution)/shard_map/pallas_call | solution.py:364
  73.8 4.3 %all-to-all-start.2 = ((bf16[16,208,128]{2,1,0:T(8,128)(2,1)}), bf16[16,208,128]{2,1,0:T(8,128)(2,1)S(1)}, u32[]{:S(2)}, u32[]{:S(2)}) async-start(bf16[16,208,128]{2,1,0:T(8,128)(2,1)} %shard_map.152), calls=%async_computation.2 | async-start | bytes 1703936 | tf_op jit(solution)/shard_map/all_to_all | solution.py:366
  78.1 0.9 copy-done.10
  79.1 1.6 %shard_map.149 = (bf16[128,512]{1,0:T(8,128)(2,1)}, f32[128,512]{1,0:T(8,128)S(1)}, bf16[128,512]{1,0:T(8,128)(2,1)S(1)}, bf16[128,512]{1,0:T(8,128)(2,1)S(1)}, bf16[128,512]{1,0:T(8,128)(2,1)S(1)}) custom-call(s32[2]{0:T(128)S(1)} %pad_add_fusion.me_ref, bf16[64,16,128]{2,1,0:T(8,128)(2,1)S(1)} %all-to-all-done.1.recv_ref.back_ref, ...), custom_call_target="tpu_custom_call" | custom-call | tf_op jit(solution)/shard_map/pallas_call | solution.py:368
  80.7 1.3 %collective-permute-start.3 = (bf16[128,512]{1,0:T(8,128)(2,1)S(1)}, bf16[128,512]{1,0:T(8,128)(2,1)S(1)}, u32[]{:S(2)}, u32[]{:S(2)}) collective-permute-start(bf16[128,512]{1,0:T(8,128)(2,1)S(1)} %get-tuple-element.31), channel_id=1, source_target_pairs={{0,1},{1,2},{2,3},{3,0},{4,5},{5,6},{6,7},{7,4},{8,9},{9,10},{10,1... | collective-permute-start | bytes 393224 | tf_op jit(solution)/shard_map/ppermute | solution.py:293
  82.0 1.6 %collective-permute-start.4 = (bf16[128,512]{1,0:T(8,128)(2,1)S(1)}, bf16[128,512]{1,0:T(8,128)(2,1)S(1)}, u32[]{:S(2)}, u32[]{:S(2)}) collective-permute-start(bf16[128,512]{1,0:T(8,128)(2,1)S(1)} %get-tuple-element.32), channel_id=1, source_target_pairs={{0,2},{1,3},{2,0},{3,1},{4,6},{5,7},{6,4},{7,5},{8,10},{9,11},{10,... | collective-permute-start | bytes 393224 | tf_op jit(solution)/shard_map/ppermute | solution.py:293
  83.5 1.6 %collective-permute-start.5 = (bf16[128,512]{1,0:T(8,128)(2,1)S(1)}, bf16[128,512]{1,0:T(8,128)(2,1)S(1)}, u32[]{:S(2)}, u32[]{:S(2)}) collective-permute-start(bf16[128,512]{1,0:T(8,128)(2,1)S(1)} %get-tuple-element.33), channel_id=1, source_target_pairs={{0,3},{1,0},{2,1},{3,2},{4,7},{5,4},{6,5},{7,6},{8,11},{9,8},{10,9... | collective-permute-start | bytes 393224 | tf_op jit(solution)/shard_map/ppermute | solution.py:293
  85.1 1.6 %collective-permute-done.3 = bf16[128,512]{1,0:T(8,128)(2,1)S(1)} collective-permute-done((bf16[128,512]{1,0:T(8,128)(2,1)S(1)}, bf16[128,512]{1,0:T(8,128)(2,1)S(1)}, u32[]{:S(2)}, u32[]{:S(2)}) %collective-permute-start.3) | collective-permute-done | bytes 131104 | tf_op jit(solution)/shard_map/ppermute | solution.py:293
  86.6 3.2 %collective-permute-done.4 = bf16[128,512]{1,0:T(8,128)(2,1)S(1)} collective-permute-done((bf16[128,512]{1,0:T(8,128)(2,1)S(1)}, bf16[128,512]{1,0:T(8,128)(2,1)S(1)}, u32[]{:S(2)}, u32[]{:S(2)}) %collective-permute-start.4) | collective-permute-done | bytes 131104 | tf_op jit(solution)/shard_map/ppermute | solution.py:293
  89.9 1.2 %collective-permute-done.5 = bf16[128,512]{1,0:T(8,128)(2,1)S(1)} collective-permute-done((bf16[128,512]{1,0:T(8,128)(2,1)S(1)}, bf16[128,512]{1,0:T(8,128)(2,1)S(1)}, u32[]{:S(2)}, u32[]{:S(2)}) %collective-permute-start.5) | collective-permute-done | bytes 131104 | tf_op jit(solution)/shard_map/ppermute | solution.py:293
  91.1 0.7 add_convert_fusion
  91.8 12.8 %all-to-all-done.2.recv_ref = bf16[16,208,128]{2,1,0:T(8,128)(2,1)S(1)} async-done(((bf16[16,208,128]{2,1,0:T(8,128)(2,1)}), bf16[16,208,128]{2,1,0:T(8,128)(2,1)S(1)}, u32[]{:S(2)}, u32[]{:S(2)}) %all-to-all-start.2) | async-done | bytes 852000 | tf_op jit(solution)/shard_map/all_to_all | solution.py:366
  104.6 1.6 %shard_map.153 = (bf16[128,512]{1,0:T(8,128)(2,1)}, f32[128,512]{1,0:T(8,128)}, f32[4,512]{1,0:T(4,128)}, f32[32,512]{1,0:T(8,128)}) custom-call(s32[2]{0:T(128)S(1)} %pad_add_fusion.me_ref, bf16[16,208,128]{2,1,0:T(8,128)(2,1)S(1)} %all-to-all-done.2.recv_ref), custom_call_target="tpu_custom_call" | custom-call | tf_op jit(solution)/shard_map/pallas_call | solution.py:376
  (15 shorter events, 0.0 us)
Async XLA Ops:
  0.6 20.0 %copy-start = (f32[4,512]{1,0:T(4,128)S(1)}, f32[4,512]{1,0:T(4,128)}, u32[]{:S(2)}) copy-start(f32[4,512]{1,0:T(4,128)} %param.12) | copy-start | bytes 24580
  0.6 30.9 %copy-start.3 = (bf16[4,256,256]{2,1,0:T(8,128)(2,1)S(1)}, bf16[4,256,256]{2,1,0:T(8,128)(2,1)}, u32[]{:S(2)}) copy-start(bf16[4,256,256]{2,1,0:T(8,128)(2,1)} %constant.26.clone.second_ref) | copy-start | bytes 1572868
  0.7 1.0 copy-start.8
  1.7 0.9 copy-start.14
  2.6 29.0 %copy-start.11 = (bf16[128,192]{1,0:T(8,128)(2,1)S(1)}, bf16[128,192]{1,0:T(8,128)(2,1)}, u32[]{:S(2)}) copy-start(bf16[128,192]{1,0:T(8,128)(2,1)} %constant.23.clone.first_ref) | copy-start | bytes 147460
  2.6 29.0 %copy-start.12 = (f32[2,64,128]{2,1,0:T(8,128)S(1)}, f32[2,64,128]{2,1,0:T(8,128)}, u32[]{:S(2)}) copy-start(f32[2,64,128]{2,1,0:T(8,128)} %constant.25.clone.twist_ref) | copy-start | bytes 196612
  2.6 29.0 %copy-start.13 = (bf16[64,384]{1,0:T(8,128)(2,1)S(1)}, bf16[64,384]{1,0:T(8,128)(2,1)}, u32[]{:S(2)}) copy-start(bf16[64,384]{1,0:T(8,128)(2,1)} %constant.24.clone.last_ref) | copy-start | bytes 147460
  3.7 27.8 %all-to-all-start = ((bf16[64,24,128]{2,1,0:T(8,128)(2,1)}), bf16[64,24,128]{2,1,0:T(8,128)(2,1)S(1)}, u32[]{:S(2)}, u32[]{:S(2)}) async-start(bf16[64,24,128]{2,1,0:T(8,128)(2,1)} %shard_map.145), calls=%async_computation | async-start | bytes 786432 | tf_op jit(solution)/shard_map/all_to_all | solution.py:310
  15.7 5.9 %collective-permute-start = (bf16[128,512]{1,0:T(8,128)(2,1)}, bf16[128,512]{1,0:T(8,128)(2,1)S(1)}, u32[]{:S(2)}, u32[]{:S(2)}) collective-permute-start(bf16[128,512]{1,0:T(8,128)(2,1)} %c0.1), channel_id=1, source_target_pairs={{0,1},{1,2},{2,3},{3,0},{4,5},{5,6},{6,7},{7,4},{8,9},{9,10},{10,1... | collective-permute-start | bytes 393224 | tf_op jit(solution)/shard_map/ppermute | solution.py:293
  17.3 8.1 %collective-permute-start.1 = (bf16[128,512]{1,0:T(8,128)(2,1)}, bf16[128,512]{1,0:T(8,128)(2,1)S(1)}, u32[]{:S(2)}, u32[]{:S(2)}) collective-permute-start(bf16[128,512]{1,0:T(8,128)(2,1)} %c0.1), channel_id=1, source_target_pairs={{0,2},{1,3},{2,0},{3,1},{4,6},{5,7},{6,4},{7,5},{8,10},{9,11},{10,... | collective-permute-start | bytes 393224 | tf_op jit(solution)/shard_map/ppermute | solution.py:293
  18.3 8.1 %collective-permute-start.2 = (bf16[128,512]{1,0:T(8,128)(2,1)}, bf16[128,512]{1,0:T(8,128)(2,1)S(1)}, u32[]{:S(2)}, u32[]{:S(2)}) collective-permute-start(bf16[128,512]{1,0:T(8,128)(2,1)} %c0.1), channel_id=1, source_target_pairs={{0,3},{1,0},{2,1},{3,2},{4,7},{5,4},{6,5},{7,6},{8,11},{9,8},{10,9... | collective-permute-start | bytes 393224 | tf_op jit(solution)/shard_map/ppermute | solution.py:293
  26.3 1.6 %copy-start.1 = (bf16[512,2048]{1,0:T(8,128)(2,1)S(1)}, bf16[512,2048]{1,0:T(8,128)(2,1)}, u32[]{:S(2)}) copy-start(bf16[512,2048]{1,0:T(8,128)(2,1)} %w_ref.1) | copy-start | bytes 6291460
  27.9 0.9 copy-start.4
  28.8 0.9 copy-start.6
  29.7 14.7 %copy-start.5 = (bf16[128,512]{1,0:T(8,128)(2,1)S(1)}, bf16[128,512]{1,0:T(8,128)(2,1)}, u32[]{:S(2)}) copy-start(bf16[128,512]{1,0:T(8,128)(2,1)} %c0.1) | copy-start | bytes 393220
  31.5 2.5 %copy-start.9 = (f32[512,128]{1,0:T(8,128)}, f32[512,128]{1,0:T(8,128)S(1)}, u32[]{:S(2)}) copy-start(f32[512,128]{1,0:T(8,128)S(1)} %get-tuple-element.29.gg_ref) | copy-start | bytes 786436
  31.6 28.6 %copy-start.7 = (bf16[128,512]{1,0:T(8,128)(2,1)S(1)}, bf16[128,512]{1,0:T(8,128)(2,1)}, u32[]{:S(2)}) copy-start(bf16[128,512]{1,0:T(8,128)(2,1)} %gate_ref.1) | copy-start | bytes 393220
  34.0 23.4 %all-to-all-start.1 = ((bf16[64,16,128]{2,1,0:T(8,128)(2,1)}), bf16[64,16,128]{2,1,0:T(8,128)(2,1)S(1)}, u32[]{:S(2)}, u32[]{:S(2)}) async-start(bf16[64,16,128]{2,1,0:T(8,128)(2,1)} %get-tuple-element.28), calls=%async_computation.1 | async-start | bytes 524288 | tf_op jit(solution)/shard_map/all_to_all | solution.py:343
  45.9 15.2 %collective-permute-start.6 = (bf16[16,32,128]{2,1,0:T(8,128)(2,1)}, bf16[16,32,128]{2,1,0:T(8,128)(2,1)S(1)}, u32[]{:S(2)}, u32[]{:S(2)}) collective-permute-start(bf16[16,32,128]{2,1,0:T(8,128)(2,1)} %get-tuple-element.35), channel_id=1, source_target_pairs={{0,4},{4,0},{8,12},{12,8},{16,20},{20,16},{24,28},{28,24},{32,36},... | collective-permute-start | bytes 393224 | tf_op jit(solution)/shard_map/ppermute | solution.py:334
  46.0 16.1 %collective-permute-start.7 = (bf16[16,32,128]{2,1,0:T(8,128)(2,1)}, bf16[16,32,128]{2,1,0:T(8,128)(2,1)S(1)}, u32[]{:S(2)}, u32[]{:S(2)}) collective-permute-start(bf16[16,32,128]{2,1,0:T(8,128)(2,1)} %get-tuple-element.36), channel_id=1, source_target_pairs={{0,8},{4,12},{8,0},{12,4},{16,24},{20,28},{24,16},{28,20},{32,40},... | collective-permute-start | bytes 393224 | tf_op jit(solution)/shard_map/ppermute | solution.py:334
  47.7 14.9 %collective-permute-start.8 = (bf16[16,32,128]{2,1,0:T(8,128)(2,1)S(1)}, bf16[16,32,128]{2,1,0:T(8,128)(2,1)S(1)}, u32[]{:S(2)}, u32[]{:S(2)}) collective-permute-start(bf16[16,32,128]{2,1,0:T(8,128)(2,1)S(1)} %get-tuple-element.37), channel_id=1, source_target_pairs={{0,12},{4,8},{8,4},{12,0},{16,28},{20,24},{24,20},{28,16},{32,44},... | collective-permute-start | bytes 393224 | tf_op jit(solution)/shard_map/ppermute | solution.py:334
  59.9 3.4 %collective-permute-start.12 = (bf16[16,24,128]{2,1,0:T(8,128)(2,1)S(1)}, bf16[16,24,128]{2,1,0:T(8,128)(2,1)S(1)}, u32[]{:S(2)}, u32[]{:S(2)}) collective-permute-start(bf16[16,24,128]{2,1,0:T(8,128)(2,1)S(1)} %get-tuple-element.40), channel_id=1, source_target_pairs={{0,4},{4,0},{8,12},{12,8},{16,20},{20,16},{24,28},{28,24},{32,36},... | collective-permute-start | bytes 294920 | tf_op jit(solution)/shard_map/ppermute | solution.py:334
  60.3 17.8 %copy-start.2 = (bf16[512,2048]{1,0:T(8,128)(2,1)S(1)}, bf16[512,2048]{1,0:T(8,128)(2,1)}, u32[]{:S(2)}) copy-start(bf16[512,2048]{1,0:T(8,128)(2,1)} %w_ref.1) | copy-start | bytes 6291460
  60.3 12.1 %collective-permute-start.10 = (bf16[128,512]{1,0:T(8,128)(2,1)S(1)}, bf16[128,512]{1,0:T(8,128)(2,1)S(1)}, u32[]{:S(2)}, u32[]{:S(2)}) collective-permute-start(bf16[128,512]{1,0:T(8,128)(2,1)S(1)} %shard_map.148.gated_ref.g0), channel_id=1, source_target_pairs={{0,8},{4,12},{8,0},{12,4},{16,24},{20,28},{24,16},{28,20},{32,40},... | collective-permute-start | bytes 393224 | tf_op jit(solution)/shard_map/ppermute | solution.py:334
  61.1 11.3 %collective-permute-start.11 = (bf16[128,512]{1,0:T(8,128)(2,1)S(1)}, bf16[128,512]{1,0:T(8,128)(2,1)S(1)}, u32[]{:S(2)}, u32[]{:S(2)}) collective-permute-start(bf16[128,512]{1,0:T(8,128)(2,1)S(1)} %shard_map.148.gated_ref.g0), channel_id=1, source_target_pairs={{0,12},{4,8},{8,4},{12,0},{16,28},{20,24},{24,20},{28,16},{32,44},... | collective-permute-start | bytes 393224 | tf_op jit(solution)/shard_map/ppermute | solution.py:334
  62.0 10.4 %collective-permute-start.9 = (bf16[128,512]{1,0:T(8,128)(2,1)S(1)}, bf16[128,512]{1,0:T(8,128)(2,1)S(1)}, u32[]{:S(2)}, u32[]{:S(2)}) collective-permute-start(bf16[128,512]{1,0:T(8,128)(2,1)S(1)} %shard_map.148.gated_ref.g0), channel_id=1, source_target_pairs={{0,4},{4,0},{8,12},{12,8},{16,20},{20,16},{24,28},{28,24},{32,36},... | collective-permute-start | bytes 393224 | tf_op jit(solution)/shard_map/ppermute | solution.py:334
  62.6 9.1 %collective-permute-start.13 = (bf16[16,24,128]{2,1,0:T(8,128)(2,1)S(1)}, bf16[16,24,128]{2,1,0:T(8,128)(2,1)S(1)}, u32[]{:S(2)}, u32[]{:S(2)}) collective-permute-start(bf16[16,24,128]{2,1,0:T(8,128)(2,1)S(1)} %get-tuple-element.41), channel_id=1, source_target_pairs={{0,8},{4,12},{8,0},{12,4},{16,24},{20,28},{24,16},{28,20},{32,40},... | collective-permute-start | bytes 294920 | tf_op jit(solution)/shard_map/ppermute | solution.py:334
  63.3 9.1 %collective-permute-start.14 = (bf16[16,24,128]{2,1,0:T(8,128)(2,1)S(1)}, bf16[16,24,128]{2,1,0:T(8,128)(2,1)S(1)}, u32[]{:S(2)}, u32[]{:S(2)}) collective-permute-start(bf16[16,24,128]{2,1,0:T(8,128)(2,1)S(1)} %get-tuple-element.42), channel_id=1, source_target_pairs={{0,12},{4,8},{8,4},{12,0},{16,28},{20,24},{24,20},{28,16},{32,44},... | collective-permute-start | bytes 294920 | tf_op jit(solution)/shard_map/ppermute | solution.py:334
  73.8 30.8 %all-to-all-start.2 = ((bf16[16,208,128]{2,1,0:T(8,128)(2,1)}), bf16[16,208,128]{2,1,0:T(8,128)(2,1)S(1)}, u32[]{:S(2)}, u32[]{:S(2)}) async-start(bf16[16,208,128]{2,1,0:T(8,128)(2,1)} %shard_map.152), calls=%async_computation.2 | async-start | bytes 1703936 | tf_op jit(solution)/shard_map/all_to_all | solution.py:366
  78.1 1.0 copy-start.10
  80.7 6.0 %collective-permute-start.3 = (bf16[128,512]{1,0:T(8,128)(2,1)S(1)}, bf16[128,512]{1,0:T(8,128)(2,1)S(1)}, u32[]{:S(2)}, u32[]{:S(2)}) collective-permute-start(bf16[128,512]{1,0:T(8,128)(2,1)S(1)} %get-tuple-element.31), channel_id=1, source_target_pairs={{0,1},{1,2},{2,3},{3,0},{4,5},{5,6},{6,7},{7,4},{8,9},{9,10},{10,1... | collective-permute-start | bytes 393224 | tf_op jit(solution)/shard_map/ppermute | solution.py:293
  82.0 7.9 %collective-permute-start.4 = (bf16[128,512]{1,0:T(8,128)(2,1)S(1)}, bf16[128,512]{1,0:T(8,128)(2,1)S(1)}, u32[]{:S(2)}, u32[]{:S(2)}) collective-permute-start(bf16[128,512]{1,0:T(8,128)(2,1)S(1)} %get-tuple-element.32), channel_id=1, source_target_pairs={{0,2},{1,3},{2,0},{3,1},{4,6},{5,7},{6,4},{7,5},{8,10},{9,11},{10,... | collective-permute-start | bytes 393224 | tf_op jit(solution)/shard_map/ppermute | solution.py:293
  83.5 7.5 %collective-permute-start.5 = (bf16[128,512]{1,0:T(8,128)(2,1)S(1)}, bf16[128,512]{1,0:T(8,128)(2,1)S(1)}, u32[]{:S(2)}, u32[]{:S(2)}) collective-permute-start(bf16[128,512]{1,0:T(8,128)(2,1)S(1)} %get-tuple-element.33), channel_id=1, source_target_pairs={{0,3},{1,0},{2,1},{3,2},{4,7},{5,4},{6,5},{7,6},{8,11},{9,8},{10,9... | collective-permute-start | bytes 393224 | tf_op jit(solution)/shard_map/ppermute | solution.py:293

commit v3 on v2

--- a/solution.py
+++ b/solution.py
@@ -14,7 +14,7 @@
 BF16 = jnp.bfloat16
 VMEM = pl.BlockSpec(memory_space=pltpu.VMEM)
 SMEM = pl.BlockSpec(memory_space=pltpu.SMEM)
-ANY = pl.BlockSpec(memory_space=pl.ANY)
+HBM = pl.BlockSpec(memory_space=pltpu.HBM)
 
 
 def split_table(table):
@@ -28,19 +28,50 @@
     k1 = np.arange(coarse)[:, None] + 0.25
     angle = 2.0 * math.pi * k1 * np.arange(coarse)[None, :] / coarse
     first = np.concatenate([np.cos(angle), -np.sin(angle)], 0)
-    high, low = split_table(first)
-    first_cat = np.concatenate([high, high, low], 1)
     last = np.concatenate([np.cos(angle).T, -np.sin(angle).T], 1)
-    high, low = split_table(last)
-    last_cat = np.concatenate([high, high, low], 1)
     angle = 2.0 * math.pi * k1 * np.arange(fine)[None, :] / length
-    twist = np.stack([np.cos(angle), np.sin(angle)], 0).astype(np.float32)
+    twist = np.concatenate([np.cos(angle), np.sin(angle)], 0)
     angle = 2.0 * math.pi * (np.outer(np.arange(fine), np.arange(fine)) % fine) / fine
     cos, sin = np.cos(angle), np.sin(angle)
     forward = np.concatenate([np.concatenate([cos, -sin], 1), np.concatenate([sin, cos], 1)], 0)
     inverse = np.concatenate([np.concatenate([cos, sin], 1), np.concatenate([-sin, cos], 1)], 0) / length
-    second = np.stack([*split_table(forward), *split_table(inverse)], 0)
-    return first_cat, last_cat, twist, second
+    high, low = split_table(first)
+    pad = np.zeros((2 * coarse, 2 * fine - 3 * coarse), high.dtype)
+    rows = [*split_table(forward), *split_table(inverse), np.concatenate([high, high, low, pad], 1)]
+    high, low = split_table(last)
+    rows.append(np.concatenate([high, high], 1))
+    rows.append(np.concatenate([low, np.zeros_like(low)], 1))
+    rows.append(np.concatenate(split_table(twist), 1))
+    return np.concatenate(rows, 0)
+
+
+class Tables:
+    def __init__(self, ref, coarse, fine):
+        size = 2 * fine
+        self.ref, self.size, self.coarse, self.fine = ref, size, coarse, fine
+
+    def second(self, which):
+        return self.ref[which * self.size : (which + 1) * self.size, :]
+
+    def first(self):
+        start = 4 * self.size
+        return self.ref[start : start + 2 * self.coarse, : 3 * self.coarse]
+
+    def last(self):
+        start = 4 * self.size + 2 * self.coarse
+        return jnp.concatenate(
+            [
+                self.ref[start : start + self.coarse, :],
+                self.ref[start + self.coarse : start + 2 * self.coarse, : 2 * self.coarse],
+            ],
+            1,
+        )
+
+    def twist(self):
+        start = 4 * self.size + 4 * self.coarse
+        both = self.ref[start : start + 2 * self.coarse, :].astype(F32)
+        both = both[:, : self.fine] + both[:, self.fine :]
+        return both[: self.coarse], both[self.coarse :]
 
 
 def split(value):
@@ -61,6 +92,10 @@
         copy.start()
     for copy in copies:
         copy.wait()
+
+
+def far(value):
+    return pltpu.with_memory_space_constraint(value, pltpu.HBM)
 
 
 def pack_kernel(inputs_hbm, filters_hbm, out_ref, inputs_ref, filters_ref, sems):
@@ -73,18 +108,24 @@
     out_ref[...] = jnp.concatenate(rows, 1).astype(BF16)
 
 
-def cotangent_kernel(me_ref, gate_hbm, w_hbm, c0_hbm, c1, c2, c3, out_ref, gg_ref, gate_ref, w_ref, c0, sems):
-    load((gate_hbm, w_hbm, c0_hbm), (gate_ref, w_ref, c0), sems)
+def own_kernel(me_ref, gate_hbm, piece_hbm, w_ref, part_ref, gate_out, gate_ref, piece, sems):
+    load((gate_hbm, piece_hbm), (gate_ref, piece), sems)
+    width = gate_ref.shape[1]
+    cols = pl.ds(pl.multiple_of(me_ref[1] * width, width), width)
+    part_ref[...] = dot(w_ref[:, cols], piece[...], NT)
+    gate_out[...] = gate_ref[...].astype(F32).T
+
+
+def cotangent_kernel(me_ref, gate_ref, part_ref, w_ref, c1, c2, c3, out_ref, gg_ref):
     chan = me_ref[1]
-    width = gate_ref.shape[1]
-    total = None
-    for step, piece in enumerate((c0, c1, c2, c3)):
-        owner = lax.rem(chan + 4 - step, 4)
+    width = gate_ref.shape[0]
+    total = part_ref[...]
+    for step, piece in enumerate((c1, c2, c3)):
+        owner = lax.rem(chan + 3 - step, 4)
         cols = pl.ds(pl.multiple_of(owner * width, width), width)
-        term = dot(w_ref[:, cols], piece[...], NT)
-        total = term if total is None else total + term
+        total = total + dot(w_ref[:, cols], piece[...], NT)
     gg_ref[...] = total
-    out_ref[...] = (total * gate_ref[...].astype(F32).T).astype(BF16)
+    out_ref[...] = (total * gate_ref[...]).astype(BF16)
 
 
 def cot_kernel(me_ref, c0, c1, c2, c3, o0, o1, o2, o3, scratch):
@@ -107,13 +148,14 @@
     return jnp.where(lane < t, before, turned)
 
 
-def coarse_stage(sig, s, first_ref, twist_ref, stage):
-    blocks, fine = twist_ref.shape[1:]
-    twist_re, twist_im = twist_ref[0], twist_ref[1]
+def coarse_stage(sig, s, tables, stage):
+    blocks, fine = tables.coarse, tables.fine
+    twist_re, twist_im = tables.twist()
+    first = tables.first()
     for pair in range(4):
         both = jnp.concatenate([sig[s, pl.ds(2 * pair + h, blocks, stride=8), :] for h in range(2)], 1)
         high, low = split(both)
-        coarse = dot(first_ref[...], jnp.concatenate([high, low, high], 0))
+        coarse = dot(first, jnp.concatenate([high, low, high], 0))
         for h in range(2):
             re = coarse[:blocks, h * fine : (h + 1) * fine]
             im = coarse[blocks:, h * fine : (h + 1) * fine]
@@ -128,17 +170,19 @@
     stage[rows, 2 * fine :] = low
 
 
-def fine_stage(stage, s, second_ref, which):
+def fine_stage(stage, s, tables, which):
     count = stage.shape[1]
     rows = pl.ds(s * count, count)
     high = stage[rows, : stage.shape[1] // 2]
     low = stage[rows, stage.shape[1] // 2 :]
-    return dot(high, second_ref[which]) + dot(low, second_ref[which]) + dot(high, second_ref[which + 1])
-
-
-def back_stage(spec, s, last_ref, twist_ref, sig):
-    blocks, fine = twist_ref.shape[1:]
-    twist_re, twist_im = twist_ref[0], twist_ref[1]
+    table = tables.second(which)
+    return dot(high, table) + dot(low, table) + dot(high, tables.second(which + 1))
+
+
+def back_stage(spec, s, tables, sig):
+    blocks, fine = tables.coarse, tables.fine
+    twist_re, twist_im = tables.twist()
+    last = tables.last()
     for pair in range(4):
         halves = []
         for h in range(2):
@@ -146,14 +190,15 @@
             re, im = spec[rows, :fine], spec[rows, fine:]
             halves.append(jnp.concatenate([re * twist_re - im * twist_im, im * twist_re + re * twist_im], 0))
         high, low = split(jnp.concatenate(halves, 1))
-        back = dot(last_ref[...], jnp.concatenate([high, low, high], 0))
+        back = dot(last, jnp.concatenate([high, low, high], 0))
         for h in range(2):
             sig[s, pl.ds(2 * pair + h, blocks, stride=8), :] = back[:, h * fine : (h + 1) * fine]
 
 
-def forward_kernel(taps_ref, recv_ref, grad_ref, first_ref, last_ref, twist_ref, second_ref, out_ref, spec, sig, stage, work):
+def forward_kernel(taps_ref, recv_ref, grad_ref, table_ref, out_ref, spec, sig, stage, work):
     blocks, _, fine = recv_ref.shape
     count = 8 * blocks
+    tables = Tables(table_ref, blocks, fine)
     taps = taps_ref[...]
     received = recv_ref[...].astype(F32)
     given = received[:, 0:8]
@@ -163,32 +208,33 @@
     sig[0] = mixed.reshape(count, fine)
     sig[1] = (received[:, 8:16] + received[:, 16:24]).reshape(count, fine)
     for s in range(2):
-        coarse_stage(sig, s, first_ref, twist_ref, stage)
+        coarse_stage(sig, s, tables, stage)
     for s in range(2):
-        spec[pl.ds(s * count, count), :] = fine_stage(stage, s, second_ref, 0)
+        spec[pl.ds(s * count, count), :] = fine_stage(stage, s, tables, 0)
     for c in range(8):
         (mr, mi), (fr, fi) = (
             (spec[pl.ds((s * 8 + c) * blocks, blocks), :fine], spec[pl.ds((s * 8 + c) * blocks, blocks), fine:])
             for s in range(2)
         )
         put(stage, 0, c, mr * fr - mi * fi, mr * fi + mi * fr)
-    work[...] = fine_stage(stage, 0, second_ref, 2)
-    back_stage(work, 0, last_ref, twist_ref, sig)
+    work[...] = fine_stage(stage, 0, tables, 2)
+    back_stage(work, 0, tables, sig)
     convolved = sig[0].reshape(blocks, 8, fine)
     grad_conv = grad_ref[...].astype(F32).reshape(blocks, 8, fine)
     out_ref[...] = jnp.concatenate([convolved, grad_conv], 1).astype(BF16)
 
 
 def backward_kernel(
-    me_ref, taps_ref, recv_ref, back_ref, spec, first_ref, last_ref, twist_ref, second_ref,
+    me_ref, _, taps_ref, recv_ref, back_ref, spec, table_ref,
     o0, o1, o2, o3, sig, stage, work, parts
 ):
     blocks, _, fine = recv_ref.shape
     count = 8 * blocks
+    tables = Tables(table_ref, blocks, fine)
     taps = taps_ref[...]
     sig[0] = back_ref[...].astype(F32)[:, 8:16].reshape(count, fine)
-    coarse_stage(sig, 0, first_ref, twist_ref, stage)
-    work[pl.ds(0, count), :] = fine_stage(stage, 0, second_ref, 0)
+    coarse_stage(sig, 0, tables, stage)
+    work[pl.ds(0, count), :] = fine_stage(stage, 0, tables, 0)
     for c in range(8):
         rows = pl.ds(c * blocks, blocks)
         gr, gi = work[rows, :fine], work[rows, fine:]
@@ -197,9 +243,9 @@
             re, im = spec[rows, :fine], spec[rows, fine:]
             put(stage, s, c, re * gr + im * gi, re * gi - im * gr)
     for s in range(2):
-        work[pl.ds(s * count, count), :] = fine_stage(stage, s, second_ref, 2)
+        work[pl.ds(s * count, count), :] = fine_stage(stage, s, tables, 2)
     for s in range(2):
-        back_stage(work, s, last_ref, twist_ref, sig)
+        back_stage(work, s, tables, sig)
     grad_mixed, grad_filters = (sig[s].reshape(blocks, 8, fine) for s in range(2))
     lane = lax.broadcasted_iota(jnp.int32, (blocks, 8, fine), 2)
     zero = jnp.zeros((1, 8, fine), F32)
@@ -216,11 +262,12 @@
         high = total.astype(BF16).astype(F32)
         tap_tile = jnp.where(column == t, high, tap_tile)
         tap_tile = jnp.where(column == t + 4, total - high, tap_tile)
-    tap_rows = jnp.broadcast_to(tap_tile[None], (blocks, 8, fine))
-    parts[...] = jnp.concatenate([grad_inputs, grad_filters, tap_rows], 1).reshape(blocks // 4, 4, 24, fine)
+    parts[...] = jnp.concatenate([grad_inputs, grad_filters], 1).reshape(blocks // 4, 4, 16, fine)
+    tap_tile = jnp.concatenate([tap_tile, jnp.zeros_like(tap_tile)], 0).astype(BF16)
     kind = lax.rem(me_ref[0], 4)
     for d, out in enumerate((o0, o1, o2, o3)):
-        out[...] = parts[:, kind ^ d].astype(BF16)
+        out[0 : blocks // 4] = parts[:, kind ^ d].astype(BF16)
+        out[blocks // 4] = tap_tile
 
 
 def gate_kernel(recv_ref, gate_ref, gated_ref):
@@ -238,11 +285,11 @@
         out_ref[:, 64 + j * rows : 64 + (j + 1) * rows, :] = columns.astype(BF16)
     tap_rows = None
     for d, part in enumerate((p0, p1, p2, p3)):
-        value = part[...].astype(F32)
-        out_ref[:, 16 * d : 16 * (d + 1), :] = value[:, 0:16].astype(BF16)
-        tile = pltpu.roll(value[:, 16:24], 8 * d, 2) if d else value[:, 16:24]
+        out_ref[:, 16 * d : 16 * (d + 1), :] = part[0:groups]
+        tile = part[groups].astype(F32)
+        tile = pltpu.roll(tile, 8 * d, 1) if d else tile
         tap_rows = tile if tap_rows is None else tap_rows + tile
-    out_ref[:, 192:208, :] = jnp.concatenate([tap_rows, jnp.zeros_like(tap_rows)], 1).astype(BF16)
+    out_ref[:, 192:208, :] = jnp.broadcast_to(tap_rows[None], (groups, 16, depth)).astype(BF16)
 
 
 def project_kernel(me_ref, recv_ref, gated_ref, gg_ref, w_ref, gate_grad_ref, own_ref, s1, s2, s3):
@@ -284,7 +331,7 @@
         in_specs=in_specs,
         out_specs=jax.tree.map(lambda _: VMEM, outs),
         scratch_shapes=list(scratch),
-        compiler_params=pltpu.CompilerParams(vmem_limit_bytes=50 * 1024 * 1024),
+        compiler_params=pltpu.CompilerParams(vmem_limit_bytes=12 * 1024 * 1024),
     )
 
 
@@ -298,29 +345,29 @@
     owners = lax.axis_size("seq")
     rows, width = inputs.shape
     me = jnp.stack([lax.axis_index("seq"), lax.axis_index("chan")]).astype(jnp.int32)
-    tables = [jnp.asarray(t) for t in transform_tables(owners, rows)]
+    table = jnp.asarray(transform_tables(owners, rows))
     my_taps = lax.dynamic_slice_in_dim(short_taps, me[0] * 8, 8, 1).T
 
     packed = call(
         pack_kernel,
         shape((owners, 24, rows), BF16),
-        [ANY] * 2,
+        [HBM] * 2,
         [pltpu.VMEM((rows, width), BF16), pltpu.VMEM((rows, width), F32), pltpu.SemaphoreType.DMA((2,))],
-    )(inputs, filters)
+    )(far(inputs), far(filters))
     received = lax.all_to_all(packed, "seq", 0, 0, tiled=True)
 
     pieces = [shifted(cotangent, "chan", d) for d in (1, 2, 3)]
+    own_part, gate_flipped = call(
+        own_kernel,
+        (shape((width, rows), F32),) * 2,
+        [SMEM, HBM, HBM, VMEM],
+        [pltpu.VMEM((rows, width), BF16)] * 2 + [pltpu.SemaphoreType.DMA((2,))],
+    )(me, far(gate_branch), far(cotangent), w_out)
     grad_packed, grad_gated = call(
         cotangent_kernel,
         (shape((width, rows), BF16), shape((width, rows), F32)),
-        [SMEM] + [ANY] * 3 + [VMEM] * 3,
-        [
-            pltpu.VMEM((rows, width), BF16),
-            pltpu.VMEM(w_out.shape, BF16),
-            pltpu.VMEM((rows, width), BF16),
-            pltpu.SemaphoreType.DMA((3,)),
-        ],
-    )(me, gate_branch, w_out, cotangent, *pieces)
+        [SMEM] + [VMEM] * 6,
+    )(me, gate_flipped, own_part, w_out, *pieces)
 
     def work_space(signals):
         return [
@@ -329,17 +376,18 @@
             pltpu.VMEM((signals * width, 2 * rows), F32),
         ]
 
+    def swapped(value, distance):
+        return lax.ppermute(value, "seq", [(i, i ^ distance) for i in range(owners)])
+
     def traded(values):
-        return [values[0]] + [
-            lax.ppermute(values[d], "seq", [(i, i ^ d) for i in range(owners)]) for d in (1, 2, 3)
-        ]
+        return [values[0]] + [swapped(values[d], d) for d in (1, 2, 3)]
 
     sent, spectra = call(
         forward_kernel,
         (shape((owners, 16, rows), BF16), shape((2 * width, 2 * rows), F32)),
-        [VMEM] * 7,
+        [VMEM] * 4,
         work_space(1),
-    )(my_taps, received, grad_packed, *tables)
+    )(my_taps, received, grad_packed, table)
     back = lax.all_to_all(sent, "seq", 0, 0, tiled=True)
 
     cot_parts = traded(
@@ -352,14 +400,16 @@
     )
 
     gated = call(gate_kernel, shape((rows, width), BF16), [VMEM] * 2)(back, gate_branch)
-    gated_parts = traded([gated] * 4)
+    across = swapped(gated, 2)
+    beside = swapped(gated, 1)
+    gated_parts = [gated, beside, across, swapped(across, 1)]
     grad_parts = traded(
         call(
             backward_kernel,
-            (shape((16, 24, rows), BF16),) * 4,
-            [SMEM] + [VMEM] * 8,
-            work_space(2) + [pltpu.VMEM((16, 4, 24, rows), F32)],
-        )(me, my_taps, received, back, spectra, *tables)
+            (shape((17, 16, rows), BF16),) * 4,
+            [SMEM] + [VMEM] * 6,
+            work_space(2) + [pltpu.VMEM((16, 4, 16, rows), F32)],
+        )(me, beside, my_taps, received, back, spectra, table)
     )
     last = call(weight_kernel, shape((16, 208, rows), BF16), [VMEM] * 12)(*cot_parts, *gated_parts, *grad_parts)
     groups = [list(range(k, owners, 4)) for k in range(4)]

time: 107 us -> 101 us (0.944)
  blocking collectives: 0 us -> 20.8 us
  waiting for transfers between devices: 42 us -> 29.8 us
  starting transfers between devices: 42.1 us -> 30.4 us
  local copies, waits for them, and re-layouts: 6.45 us -> 3.42 us
    all_to_all x0 -> x1, blocking collectives: none -> 20.8 us  [local(): back = lax.all_to_all(sent, 'seq', 0, 0, tiled=True)]
    all_to_all x1 -> x0, starting transfers between devices: 10.4 us -> none  [local(): back = lax.all_to_all(sent, 'seq', 0, 0, tiled=True)]
    all_to_all x1 -> x0, waiting for transfers between devices: 9.61 us -> none  [local(): back = lax.all_to_all(sent, 'seq', 0, 0, tiled=True)]
    ppermute x6, waiting for transfers between devices: 11.4 us -> 8.35 us  [shifted(): lax.ppermute(value, axis, [(i, (i + steps) % count) for i in range(count)])]
    unnamed x31 -> x17, local copies, waits for them, and re-layouts: 6.38 us -> 3.35 us
    pallas_call x2 -> x3, Pallas kernels: 3.57 us -> 6.18 us  [the longest x1 2.41 us: local(): call(backward_kernel, (shape((17, 16, rows), BF16),) * 4, [SMEM] + [VMEM]...]
    all_to_all x1, waiting for transfers between devices: 0.01 us -> 2.37 us  [local(): received = lax.all_to_all(packed, 'seq', 0, 0, tiled=True)]
    ppermute x9, waiting for transfers between devices: 8.24 us -> 6.25 us  [swapped(): lax.ppermute(value, 'seq', [(i, i ^ distance) for i in range(owners)])]
  transfers between devices with their start and end apart: 18 -> 17, of which waited for: 10 -> 10; matrix products, arithmetic and copies ran while one was open for 1% -> 1% of each run, Pallas kernels for 7% -> 8%
where the time goes in v3:
time: 101 us; the launch traced here: 100 us
  starting transfers between devices  30.4 us (30%)
  waiting for transfers between devices  29.8 us (30%)
  blocking collectives  20.8 us (21%)
  Pallas kernels  14.4 us (14%)
  local copies, waits for them, and re-layouts  3.42 us (3%)
    all_to_all x1, blocking collectives, local(): back = lax.all_to_all(sent, 'seq', 0, 0, tiled=True)  20.8 us
    all_to_all x1, waiting for transfers between devices, local(): lax.all_to_all(last, 'seq', 0, 0, axis_index_groups=groups, tiled=True)  12.8 us
    all_to_all x1, starting transfers between devices, local(): received = lax.all_to_all(packed, 'seq', 0, 0, tiled=True)  11.9 us
    ppermute x6, starting transfers between devices, shifted(): lax.ppermute(value, axis, [(i, (i + steps) % count) for i in range(count)])  9.42 us
    ppermute x6, waiting for transfers between devices, shifted(): lax.ppermute(value, axis, [(i, (i + steps) % count) for i in range(count)])  8.35 us
    ppermute x9, waiting for transfers between devices, swapped(): lax.ppermute(value, 'seq', [(i, i ^ distance) for i in range(owners)])  6.25 us
    ppermute x9, starting transfers between devices, swapped(): lax.ppermute(value, 'seq', [(i, i ^ distance) for i in range(owners)])  5.2 us
    all_to_all x1, starting transfers between devices, local(): lax.all_to_all(last, 'seq', 0, 0, axis_index_groups=groups, tiled=True)  3.81 us
  transfers between devices with their start and end apart: 17, of which 10 were waited for; matrix products, arithmetic and copies ran while one was open for 1% of the time, Pallas kernels for 8%

profile of v3, /device:TPU:8, one launch (start us, length us, event | category | flops | bytes accessed | tf_op | source)
XLA Modules:
  0.0 100.4 jit_solution(12506592897136324734)
XLA Ops:
  0.6 0.0 copy-start
  0.6 2.0 %shard_map.118 = bf16[64,24,128]{2,1,0:T(8,128)(2,1)} custom-call(bf16[128,512]{1,0:T(8,128)(2,1)} %inputs_hbm.1, f32[128,512]{1,0:T(8,128)} %filters_hbm.1), custom_call_target="tpu_custom_call" | custom-call | tf_op jit(solution)/shard_map/pallas_call | solution.py:351
  2.6 11.9 %all-to-all-start = ((bf16[64,24,128]{2,1,0:T(8,128)(2,1)}), bf16[64,24,128]{2,1,0:T(8,128)(2,1)S(1)}, u32[]{:S(2)}, u32[]{:S(2)}) async-start(bf16[64,24,128]{2,1,0:T(8,128)(2,1)} %shard_map.118), calls=%async_computation | async-start | bytes 786432 | tf_op jit(solution)/shard_map/all_to_all | solution.py:357
  14.6 1.7 %collective-permute-start = (bf16[128,512]{1,0:T(8,128)(2,1)}, bf16[128,512]{1,0:T(8,128)(2,1)S(1)}, u32[]{:S(2)}, u32[]{:S(2)}) collective-permute-start(bf16[128,512]{1,0:T(8,128)(2,1)} %c0.1), channel_id=1, source_target_pairs={{0,1},{1,2},{2,3},{3,0},{4,5},{5,6},{6,7},{7,4},{8,9},{9,10},{10,1... | collective-permute-start | bytes 393224 | tf_op jit(solution)/shard_map/ppermute | solution.py:340
  16.2 0.9 collective-permute-start.1
  17.2 2.4 %collective-permute-start.2 = (bf16[128,512]{1,0:T(8,128)(2,1)}, bf16[128,512]{1,0:T(8,128)(2,1)S(1)}, u32[]{:S(2)}, u32[]{:S(2)}) collective-permute-start(bf16[128,512]{1,0:T(8,128)(2,1)} %c0.1), channel_id=1, source_target_pairs={{0,3},{1,0},{2,1},{3,2},{4,7},{5,4},{6,5},{7,6},{8,11},{9,8},{10,9... | collective-permute-start | bytes 393224 | tf_op jit(solution)/shard_map/ppermute | solution.py:340
  19.6 0.0 copy-done
  19.6 0.1 constant_dynamic-slice_fusion
  19.6 0.1 copy.14
  19.7 0.1 pad_add_fusion.me_ref
  19.8 0.0 copy-start.1
  19.8 1.6 %copy-done.1 = bf16[512,2048]{1,0:T(8,128)(2,1)S(1)} copy-done((bf16[512,2048]{1,0:T(8,128)(2,1)S(1)}, bf16[512,2048]{1,0:T(8,128)(2,1)}, u32[]{:S(2)}) %copy-start.1) | copy-done | bytes 2097176
  21.4 1.8 %shard_map.119 = (f32[512,128]{1,0:T(8,128)S(1)}, f32[512,128]{1,0:T(8,128)S(1)}) custom-call(s32[2]{0:T(128)S(1)} %pad_add_fusion.me_ref, bf16[128,512]{1,0:T(8,128)(2,1)} %gate_ref.1, bf16[128,512]{1,0:T(8,128)(2,1)} %c0.1, bf16[512,2048]{1,0:T(8,128)(2,1)S(1)} %copy-done.1), custom_call_target="tpu_custom_call" | custom-call | tf_op jit(solution)/shard_map/pallas_call | solution.py:360
  23.2 0.0 copy-start.3
  23.2 0.0 collective-permute-done.c1
  23.2 1.1 %collective-permute-done.1.c2 = bf16[128,512]{1,0:T(8,128)(2,1)S(1)} collective-permute-done((bf16[128,512]{1,0:T(8,128)(2,1)}, bf16[128,512]{1,0:T(8,128)(2,1)S(1)}, u32[]{:S(2)}, u32[]{:S(2)}) %collective-permute-start.1) | collective-permute-done | bytes 131104 | tf_op jit(solution)/shard_map/ppermute | solution.py:340
  24.3 0.9 collective-permute-done.2.c3
  25.2 0.0 copy-start.5
  25.2 1.1 %shard_map.120 = (bf16[512,128]{1,0:T(8,128)(2,1)S(1)}, f32[512,128]{1,0:T(8,128)S(1)}) custom-call(s32[2]{0:T(128)S(1)} %pad_add_fusion.me_ref, f32[512,128]{1,0:T(8,128)S(1)} %get-tuple-element.29.gate_ref, f32[512,128]{1,0:T(8,128)S(1)} %get-tuple-element.30.part_ref, bf16[512,2048]{1,0:T(8,128)(2,1)S(1)} %copy-done.1, ...), custom_call_target="tpu_custom_call" | custom-call | tf_op jit(solution)/shard_map/pallas_call | solution.py:366
  26.4 0.0 copy-start.6
  26.4 0.7 copy-done.6
  27.1 2.4 %all-to-all-done.recv_ref = bf16[64,24,128]{2,1,0:T(8,128)(2,1)S(1)} async-done(((bf16[64,24,128]{2,1,0:T(8,128)(2,1)}), bf16[64,24,128]{2,1,0:T(8,128)(2,1)S(1)}, u32[]{:S(2)}, u32[]{:S(2)}) %all-to-all-start) | async-done | bytes 393248 | tf_op jit(solution)/shard_map/all_to_all | solution.py:357
  29.4 0.0 copy-done.3
  29.4 1.7 %shard_map.121 = (bf16[64,16,128]{2,1,0:T(8,128)(2,1)S(1)}, f32[1024,256]{1,0:T(8,128)S(1)}) custom-call(f32[8,4]{1,0:T(8,128)S(1)} %bitcast.4, bf16[64,24,128]{2,1,0:T(8,128)(2,1)S(1)} %all-to-all-done.recv_ref, bf16[512,128]{1,0:T(8,128)(2,1)S(1)} %get-tuple-element.31.grad_ref, bf16[1408,256]{1,0:T(8,128)(2,1)S(1)} %copy-done.3), custom_call_target="tpu_custom_call" | custom-call | tf_op jit(solution)/shard_map/pallas_call | solution.py:385
  31.2 20.8 %all_to_all.15.recv_ref.back_ref = bf16[64,16,128]{2,1,0:T(8,128)(2,1)S(1)} all-to-all(bf16[64,16,128]{2,1,0:T(8,128)(2,1)S(1)} %get-tuple-element.32), channel_id=1, replica_groups=mesh['seq'=64,'chan'=4] {'seq'}, dimensions={0} | all-to-all | bytes 524288 | tf_op jit(solution)/shard_map/all_to_all | solution.py:391
  52.0 0.0 copy-done.5
  52.0 0.1 shard_map.122.gated_ref.g0
  52.1 0.9 collective-permute-start.10
  53.0 0.0 collective-permute-start.9
  53.0 0.0 copy-done.4
  53.0 0.8 shard_map.124
  53.8 0.6 collective-permute-start.6
  54.4 1.2 %collective-permute-start.7 = (bf16[16,32,128]{2,1,0:T(8,128)(2,1)S(1)}, bf16[16,32,128]{2,1,0:T(8,128)(2,1)S(1)}, u32[]{:S(2)}, u32[]{:S(2)}) collective-permute-start(bf16[16,32,128]{2,1,0:T(8,128)(2,1)S(1)} %get-tuple-element.40), channel_id=1, source_target_pairs={{0,8},{4,12},{8,0},{12,4},{16,24},{20,28},{24,16},{28,20},{32,40},... | collective-permute-start | bytes 393224 | tf_op jit(solution)/shard_map/ppermute | solution.py:380
  55.6 0.2 collective-permute-start.8
  55.8 2.7 %collective-permute-done.10.g2 = bf16[128,512]{1,0:T(8,128)(2,1)S(1)} collective-permute-done((bf16[128,512]{1,0:T(8,128)(2,1)S(1)}, bf16[128,512]{1,0:T(8,128)(2,1)S(1)}, u32[]{:S(2)}, u32[]{:S(2)}) %collective-permute-start.10) | collective-permute-done | bytes 131104 | tf_op jit(solution)/shard_map/ppermute | solution.py:380
  58.5 0.0 collective-permute-start.11
  58.5 0.0 collective-permute-done.9._.g1
  58.5 2.4 %shard_map.125 = (bf16[17,16,128]{2,1,0:T(8,128)(2,1)S(1)}, bf16[17,16,128]{2,1,0:T(8,128)(2,1)S(1)}, bf16[17,16,128]{2,1,0:T(8,128)(2,1)S(1)}, bf16[17,16,128]{2,1,0:T(8,128)(2,1)S(1)}) custom-call(s32[2]{0:T(128)S(1)} %pad_add_fusion.me_ref, bf16[128,512]{1,0:T(8,128)(2,1)S(1)} %collective-permute-done.9._.g1, f32[8,4]{1,0:T(8,128)S(1)} %bitcast.5, ...), custom_call_target="tpu_custom_call" | custom-call | tf_op jit(solution)/shard_map/pallas_call | solution.py:407
  60.9 0.0 copy-start.2
  60.9 0.6 collective-permute-start.12
  61.5 0.0 collective-permute-done.6.k1
  61.5 0.2 collective-permute-start.13
  61.7 0.0 collective-permute-done.7.k2
  61.7 1.4 %collective-permute-start.14 = (bf16[17,16,128]{2,1,0:T(8,128)(2,1)S(1)}, bf16[17,16,128]{2,1,0:T(8,128)(2,1)S(1)}, u32[]{:S(2)}, u32[]{:S(2)}) collective-permute-start(bf16[17,16,128]{2,1,0:T(8,128)(2,1)S(1)} %get-tuple-element.46), channel_id=1, source_target_pairs={{0,12},{4,8},{8,4},{12,0},{16,28},{20,24},{24,20},{28,16},{32,44},... | collective-permute-start | bytes 208904 | tf_op jit(solution)/shard_map/ppermute | solution.py:380
  63.1 0.0 collective-permute-done.8.k3
  63.1 0.0 collective-permute-done.12.p1
  63.2 3.4 %collective-permute-done.13.p2 = bf16[17,16,128]{2,1,0:T(8,128)(2,1)S(1)} collective-permute-done((bf16[17,16,128]{2,1,0:T(8,128)(2,1)S(1)}, bf16[17,16,128]{2,1,0:T(8,128)(2,1)S(1)}, u32[]{:S(2)}, u32[]{:S(2)}) %collective-permute-start.13) | collective-permute-done | bytes 69664 | tf_op jit(solution)/shard_map/ppermute | solution.py:380
  66.5 0.2 collective-permute-done.14.p3
  66.7 0.0 collective-permute-done.11.g3
  66.7 1.4 %shard_map.126 = bf16[16,208,128]{2,1,0:T(8,128)(2,1)} custom-call(bf16[16,32,128]{2,1,0:T(8,128)(2,1)S(1)} %get-tuple-element.38.k0, bf16[16,32,128]{2,1,0:T(8,128)(2,1)S(1)} %collective-permute-done.6.k1, bf16[16,32,128]{2,1,0:T(8,128)(2,1)S(1)} %collective-permute-done.7.k2, bf16[16,32,128]{2,1,0:T(8,128)(2,1)S(1)} %collective-permute-done.8.k3, ...), custom_call_target="tpu_custom_call" | custom-call | tf_op jit(solution)/shard_map/pallas_call | solution.py:414
  68.1 3.8 %all-to-all-start.2 = ((bf16[16,208,128]{2,1,0:T(8,128)(2,1)}), bf16[16,208,128]{2,1,0:T(8,128)(2,1)S(1)}, u32[]{:S(2)}, u32[]{:S(2)}) async-start(bf16[16,208,128]{2,1,0:T(8,128)(2,1)} %shard_map.126), calls=%async_computation.2 | async-start | bytes 1703936 | tf_op jit(solution)/shard_map/all_to_all | solution.py:416
  71.9 0.0 copy-done.2
  71.9 0.0 copy-start.7
  71.9 0.9 copy-done.7
  72.9 1.6 %shard_map.123 = (bf16[128,512]{1,0:T(8,128)(2,1)}, f32[128,512]{1,0:T(8,128)S(1)}, bf16[128,512]{1,0:T(8,128)(2,1)S(1)}, bf16[128,512]{1,0:T(8,128)(2,1)S(1)}, bf16[128,512]{1,0:T(8,128)(2,1)S(1)}) custom-call(s32[2]{0:T(128)S(1)} %pad_add_fusion.me_ref, bf16[64,16,128]{2,1,0:T(8,128)(2,1)S(1)} %all_to_all.15.recv_ref.back_ref, ...), custom_call_target="tpu_custom_call" | custom-call | tf_op jit(solution)/shard_map/pallas_call | solution.py:418
  74.5 1.3 %collective-permute-start.3 = (bf16[128,512]{1,0:T(8,128)(2,1)S(1)}, bf16[128,512]{1,0:T(8,128)(2,1)S(1)}, u32[]{:S(2)}, u32[]{:S(2)}) collective-permute-start(bf16[128,512]{1,0:T(8,128)(2,1)S(1)} %get-tuple-element.35), channel_id=1, source_target_pairs={{0,1},{1,2},{2,3},{3,0},{4,5},{5,6},{6,7},{7,4},{8,9},{9,10},{10,1... | collective-permute-start | bytes 393224 | tf_op jit(solution)/shard_map/ppermute | solution.py:340
  75.8 1.6 %collective-permute-start.4 = (bf16[128,512]{1,0:T(8,128)(2,1)S(1)}, bf16[128,512]{1,0:T(8,128)(2,1)S(1)}, u32[]{:S(2)}, u32[]{:S(2)}) collective-permute-start(bf16[128,512]{1,0:T(8,128)(2,1)S(1)} %get-tuple-element.36), channel_id=1, source_target_pairs={{0,2},{1,3},{2,0},{3,1},{4,6},{5,7},{6,4},{7,5},{8,10},{9,11},{10,... | collective-permute-start | bytes 393224 | tf_op jit(solution)/shard_map/ppermute | solution.py:340
  77.3 1.6 %collective-permute-start.5 = (bf16[128,512]{1,0:T(8,128)(2,1)S(1)}, bf16[128,512]{1,0:T(8,128)(2,1)S(1)}, u32[]{:S(2)}, u32[]{:S(2)}) collective-permute-start(bf16[128,512]{1,0:T(8,128)(2,1)S(1)} %get-tuple-element.37), channel_id=1, source_target_pairs={{0,3},{1,0},{2,1},{3,2},{4,7},{5,4},{6,5},{7,6},{8,11},{9,8},{10,9... | collective-permute-start | bytes 393224 | tf_op jit(solution)/shard_map/ppermute | solution.py:340
  78.9 1.9 %collective-permute-done.3 = bf16[128,512]{1,0:T(8,128)(2,1)S(1)} collective-permute-done((bf16[128,512]{1,0:T(8,128)(2,1)S(1)}, bf16[128,512]{1,0:T(8,128)(2,1)S(1)}, u32[]{:S(2)}, u32[]{:S(2)}) %collective-permute-start.3) | collective-permute-done | bytes 131104 | tf_op jit(solution)/shard_map/ppermute | solution.py:340
  80.8 2.9 %collective-permute-done.4 = bf16[128,512]{1,0:T(8,128)(2,1)S(1)} collective-permute-done((bf16[128,512]{1,0:T(8,128)(2,1)S(1)}, bf16[128,512]{1,0:T(8,128)(2,1)S(1)}, u32[]{:S(2)}, u32[]{:S(2)}) %collective-permute-start.4) | collective-permute-done | bytes 131104 | tf_op jit(solution)/shard_map/ppermute | solution.py:340
  83.7 1.6 %collective-permute-done.5 = bf16[128,512]{1,0:T(8,128)(2,1)S(1)} collective-permute-done((bf16[128,512]{1,0:T(8,128)(2,1)S(1)}, bf16[128,512]{1,0:T(8,128)(2,1)S(1)}, u32[]{:S(2)}, u32[]{:S(2)}) %collective-permute-start.5) | collective-permute-done | bytes 131104 | tf_op jit(solution)/shard_map/ppermute | solution.py:340
  85.3 0.7 add_convert_fusion
  86.0 12.8 %all-to-all-done.2.recv_ref = bf16[16,208,128]{2,1,0:T(8,128)(2,1)S(1)} async-done(((bf16[16,208,128]{2,1,0:T(8,128)(2,1)}), bf16[16,208,128]{2,1,0:T(8,128)(2,1)S(1)}, u32[]{:S(2)}, u32[]{:S(2)}) %all-to-all-start.2) | async-done | bytes 852000 | tf_op jit(solution)/shard_map/all_to_all | solution.py:416
  98.8 1.6 %shard_map.127 = (bf16[128,512]{1,0:T(8,128)(2,1)}, f32[128,512]{1,0:T(8,128)}, f32[4,512]{1,0:T(4,128)}, f32[32,512]{1,0:T(8,128)}) custom-call(s32[2]{0:T(128)S(1)} %pad_add_fusion.me_ref, bf16[16,208,128]{2,1,0:T(8,128)(2,1)S(1)} %all-to-all-done.2.recv_ref), custom_call_target="tpu_custom_call" | custom-call | tf_op jit(solution)/shard_map/pallas_call | solution.py:426
  (1 shorter events, 0.0 us)
Async XLA Ops:
  0.6 18.9 %copy-start = (f32[4,512]{1,0:T(4,128)S(1)}, f32[4,512]{1,0:T(4,128)}, u32[]{:S(2)}) copy-start(f32[4,512]{1,0:T(4,128)} %param.9) | copy-start | bytes 24580
  2.6 26.8 %all-to-all-start = ((bf16[64,24,128]{2,1,0:T(8,128)(2,1)}), bf16[64,24,128]{2,1,0:T(8,128)(2,1)S(1)}, u32[]{:S(2)}, u32[]{:S(2)}) async-start(bf16[64,24,128]{2,1,0:T(8,128)(2,1)} %shard_map.118), calls=%async_computation | async-start | bytes 786432 | tf_op jit(solution)/shard_map/all_to_all | solution.py:357
  14.6 8.7 %collective-permute-start = (bf16[128,512]{1,0:T(8,128)(2,1)}, bf16[128,512]{1,0:T(8,128)(2,1)S(1)}, u32[]{:S(2)}, u32[]{:S(2)}) collective-permute-start(bf16[128,512]{1,0:T(8,128)(2,1)} %c0.1), channel_id=1, source_target_pairs={{0,1},{1,2},{2,3},{3,0},{4,5},{5,6},{6,7},{7,4},{8,9},{9,10},{10,1... | collective-permute-start | bytes 393224 | tf_op jit(solution)/shard_map/ppermute | solution.py:340
  16.2 8.1 %collective-permute-start.1 = (bf16[128,512]{1,0:T(8,128)(2,1)}, bf16[128,512]{1,0:T(8,128)(2,1)S(1)}, u32[]{:S(2)}, u32[]{:S(2)}) collective-permute-start(bf16[128,512]{1,0:T(8,128)(2,1)} %c0.1), channel_id=1, source_target_pairs={{0,2},{1,3},{2,0},{3,1},{4,6},{5,7},{6,4},{7,5},{8,10},{9,11},{10,... | collective-permute-start | bytes 393224 | tf_op jit(solution)/shard_map/ppermute | solution.py:340
  17.2 8.1 %collective-permute-start.2 = (bf16[128,512]{1,0:T(8,128)(2,1)}, bf16[128,512]{1,0:T(8,128)(2,1)S(1)}, u32[]{:S(2)}, u32[]{:S(2)}) collective-permute-start(bf16[128,512]{1,0:T(8,128)(2,1)} %c0.1), channel_id=1, source_target_pairs={{0,3},{1,0},{2,1},{3,2},{4,7},{5,4},{6,5},{7,6},{8,11},{9,8},{10,9... | collective-permute-start | bytes 393224 | tf_op jit(solution)/shard_map/ppermute | solution.py:340
  19.8 1.6 %copy-start.1 = (bf16[512,2048]{1,0:T(8,128)(2,1)S(1)}, bf16[512,2048]{1,0:T(8,128)(2,1)}, u32[]{:S(2)}) copy-start(bf16[512,2048]{1,0:T(8,128)(2,1)} %w_ref.5) | copy-start | bytes 6291460
  23.2 6.2 %copy-start.3 = (bf16[1408,256]{1,0:T(8,128)(2,1)S(1)}, bf16[1408,256]{1,0:T(8,128)(2,1)}, u32[]{:S(2)}) copy-start(bf16[1408,256]{1,0:T(8,128)(2,1)} %constant.17.clone.table_ref) | copy-start | bytes 2162692
  25.2 26.7 %copy-start.5 = (bf16[128,512]{1,0:T(8,128)(2,1)S(1)}, bf16[128,512]{1,0:T(8,128)(2,1)}, u32[]{:S(2)}) copy-start(bf16[128,512]{1,0:T(8,128)(2,1)} %gate_ref.1) | copy-start | bytes 393220
  25.2 27.8 %copy-start.4 = (bf16[128,512]{1,0:T(8,128)(2,1)S(1)}, bf16[128,512]{1,0:T(8,128)(2,1)}, u32[]{:S(2)}) copy-start(bf16[128,512]{1,0:T(8,128)(2,1)} %c0.1) | copy-start | bytes 393220
  26.4 0.7 copy-start.6
  52.1 6.4 %collective-permute-start.10 = (bf16[128,512]{1,0:T(8,128)(2,1)S(1)}, bf16[128,512]{1,0:T(8,128)(2,1)S(1)}, u32[]{:S(2)}, u32[]{:S(2)}) collective-permute-start(bf16[128,512]{1,0:T(8,128)(2,1)S(1)} %shard_map.122.gated_ref.g0), channel_id=1, source_target_pairs={{0,8},{4,12},{8,0},{12,4},{16,24},{20,28},{24,16},{28,20},{32,40},... | collective-permute-start | bytes 393224 | tf_op jit(solution)/shard_map/ppermute | solution.py:380
  53.0 5.5 %collective-permute-start.9 = (bf16[128,512]{1,0:T(8,128)(2,1)S(1)}, bf16[128,512]{1,0:T(8,128)(2,1)S(1)}, u32[]{:S(2)}, u32[]{:S(2)}) collective-permute-start(bf16[128,512]{1,0:T(8,128)(2,1)S(1)} %shard_map.122.gated_ref.g0), channel_id=1, source_target_pairs={{0,4},{4,0},{8,12},{12,8},{16,20},{20,16},{24,28},{28,24},{32,36},... | collective-permute-start | bytes 393224 | tf_op jit(solution)/shard_map/ppermute | solution.py:380
  53.8 7.7 %collective-permute-start.6 = (bf16[16,32,128]{2,1,0:T(8,128)(2,1)S(1)}, bf16[16,32,128]{2,1,0:T(8,128)(2,1)S(1)}, u32[]{:S(2)}, u32[]{:S(2)}) collective-permute-start(bf16[16,32,128]{2,1,0:T(8,128)(2,1)S(1)} %get-tuple-element.39), channel_id=1, source_target_pairs={{0,4},{4,0},{8,12},{12,8},{16,20},{20,16},{24,28},{28,24},{32,36},... | collective-permute-start | bytes 393224 | tf_op jit(solution)/shard_map/ppermute | solution.py:380
  54.4 7.4 %collective-permute-start.7 = (bf16[16,32,128]{2,1,0:T(8,128)(2,1)S(1)}, bf16[16,32,128]{2,1,0:T(8,128)(2,1)S(1)}, u32[]{:S(2)}, u32[]{:S(2)}) collective-permute-start(bf16[16,32,128]{2,1,0:T(8,128)(2,1)S(1)} %get-tuple-element.40), channel_id=1, source_target_pairs={{0,8},{4,12},{8,0},{12,4},{16,24},{20,28},{24,16},{28,20},{32,40},... | collective-permute-start | bytes 393224 | tf_op jit(solution)/shard_map/ppermute | solution.py:380
  55.6 7.6 %collective-permute-start.8 = (bf16[16,32,128]{2,1,0:T(8,128)(2,1)S(1)}, bf16[16,32,128]{2,1,0:T(8,128)(2,1)S(1)}, u32[]{:S(2)}, u32[]{:S(2)}) collective-permute-start(bf16[16,32,128]{2,1,0:T(8,128)(2,1)S(1)} %get-tuple-element.41), channel_id=1, source_target_pairs={{0,12},{4,8},{8,4},{12,0},{16,28},{20,24},{24,20},{28,16},{32,44},... | collective-permute-start | bytes 393224 | tf_op jit(solution)/shard_map/ppermute | solution.py:380
  58.5 8.3 %collective-permute-start.11 = (bf16[128,512]{1,0:T(8,128)(2,1)S(1)}, bf16[128,512]{1,0:T(8,128)(2,1)S(1)}, u32[]{:S(2)}, u32[]{:S(2)}) collective-permute-start(bf16[128,512]{1,0:T(8,128)(2,1)S(1)} %collective-permute-done.10.g2), channel_id=1, source_target_pairs={{0,4},{4,0},{8,12},{12,8},{16,20},{20,16},{24,28},{28,24},{32,36},... | collective-permute-start | bytes 393224 | tf_op jit(solution)/shard_map/ppermute | solution.py:380
  60.9 11.0 %copy-start.2 = (bf16[512,2048]{1,0:T(8,128)(2,1)S(1)}, bf16[512,2048]{1,0:T(8,128)(2,1)}, u32[]{:S(2)}) copy-start(bf16[512,2048]{1,0:T(8,128)(2,1)} %w_ref.5) | copy-start | bytes 6291460
  60.9 2.2 %collective-permute-start.12 = (bf16[17,16,128]{2,1,0:T(8,128)(2,1)S(1)}, bf16[17,16,128]{2,1,0:T(8,128)(2,1)S(1)}, u32[]{:S(2)}, u32[]{:S(2)}) collective-permute-start(bf16[17,16,128]{2,1,0:T(8,128)(2,1)S(1)} %get-tuple-element.44), channel_id=1, source_target_pairs={{0,4},{4,0},{8,12},{12,8},{16,20},{20,16},{24,28},{28,24},{32,36},... | collective-permute-start | bytes 208904 | tf_op jit(solution)/shard_map/ppermute | solution.py:380
  61.5 5.0 %collective-permute-start.13 = (bf16[17,16,128]{2,1,0:T(8,128)(2,1)S(1)}, bf16[17,16,128]{2,1,0:T(8,128)(2,1)S(1)}, u32[]{:S(2)}, u32[]{:S(2)}) collective-permute-start(bf16[17,16,128]{2,1,0:T(8,128)(2,1)S(1)} %get-tuple-element.45), channel_id=1, source_target_pairs={{0,8},{4,12},{8,0},{12,4},{16,24},{20,28},{24,16},{28,20},{32,40},... | collective-permute-start | bytes 208904 | tf_op jit(solution)/shard_map/ppermute | solution.py:380
  61.7 5.0 %collective-permute-start.14 = (bf16[17,16,128]{2,1,0:T(8,128)(2,1)S(1)}, bf16[17,16,128]{2,1,0:T(8,128)(2,1)S(1)}, u32[]{:S(2)}, u32[]{:S(2)}) collective-permute-start(bf16[17,16,128]{2,1,0:T(8,128)(2,1)S(1)} %get-tuple-element.46), channel_id=1, source_target_pairs={{0,12},{4,8},{8,4},{12,0},{16,28},{20,24},{24,20},{28,16},{32,44},... | collective-permute-start | bytes 208904 | tf_op jit(solution)/shard_map/ppermute | solution.py:380
  68.1 30.7 %all-to-all-start.2 = ((bf16[16,208,128]{2,1,0:T(8,128)(2,1)}), bf16[16,208,128]{2,1,0:T(8,128)(2,1)S(1)}, u32[]{:S(2)}, u32[]{:S(2)}) async-start(bf16[16,208,128]{2,1,0:T(8,128)(2,1)} %shard_map.126), calls=%async_computation.2 | async-start | bytes 1703936 | tf_op jit(solution)/shard_map/all_to_all | solution.py:416
  71.9 1.0 copy-start.7
  74.5 6.3 %collective-permute-start.3 = (bf16[128,512]{1,0:T(8,128)(2,1)S(1)}, bf16[128,512]{1,0:T(8,128)(2,1)S(1)}, u32[]{:S(2)}, u32[]{:S(2)}) collective-permute-start(bf16[128,512]{1,0:T(8,128)(2,1)S(1)} %get-tuple-element.35), channel_id=1, source_target_pairs={{0,1},{1,2},{2,3},{3,0},{4,5},{5,6},{6,7},{7,4},{8,9},{9,10},{10,1... | collective-permute-start | bytes 393224 | tf_op jit(solution)/shard_map/ppermute | solution.py:340
  75.8 7.9 %collective-permute-start.4 = (bf16[128,512]{1,0:T(8,128)(2,1)S(1)}, bf16[128,512]{1,0:T(8,128)(2,1)S(1)}, u32[]{:S(2)}, u32[]{:S(2)}) collective-permute-start(bf16[128,512]{1,0:T(8,128)(2,1)S(1)} %get-tuple-element.36), channel_id=1, source_target_pairs={{0,2},{1,3},{2,0},{3,1},{4,6},{5,7},{6,4},{7,5},{8,10},{9,11},{10,... | collective-permute-start | bytes 393224 | tf_op jit(solution)/shard_map/ppermute | solution.py:340
  77.3 7.9 %collective-permute-start.5 = (bf16[128,512]{1,0:T(8,128)(2,1)S(1)}, bf16[128,512]{1,0:T(8,128)(2,1)S(1)}, u32[]{:S(2)}, u32[]{:S(2)}) collective-permute-start(bf16[128,512]{1,0:T(8,128)(2,1)S(1)} %get-tuple-element.37), channel_id=1, source_target_pairs={{0,3},{1,0},{2,1},{3,2},{4,7},{5,4},{6,5},{7,6},{8,11},{9,8},{10,9... | collective-permute-start | bytes 393224 | tf_op jit(solution)/shard_map/ppermute | solution.py:340

commit v4 on v3

--- a/solution.py
+++ b/solution.py
@@ -289,7 +289,7 @@
         tile = part[groups].astype(F32)
         tile = pltpu.roll(tile, 8 * d, 1) if d else tile
         tap_rows = tile if tap_rows is None else tap_rows + tile
-    out_ref[:, 192:208, :] = jnp.broadcast_to(tap_rows[None], (groups, 16, depth)).astype(BF16)
+    out_ref[:, 192:200, :] = jnp.broadcast_to(tap_rows[None, :8], (groups, 8, depth)).astype(BF16)
 
 
 def project_kernel(me_ref, recv_ref, gated_ref, gg_ref, w_ref, gate_grad_ref, own_ref, s1, s2, s3):
@@ -308,7 +308,7 @@
     kind = lax.rem(me_ref[0], 4)
     groups, _, rows = recv_ref.shape
     width = groups * 32
-    tap_rows = recv_ref[:, 192:208, :].astype(F32)[:, 0:8]
+    tap_rows = recv_ref[:, 192:200, :].astype(F32)
     for d in range(4):
         value = recv_ref[:, 16 * d : 16 * (d + 1), :].astype(F32)
         source = kind ^ d
@@ -402,26 +402,26 @@
     gated = call(gate_kernel, shape((rows, width), BF16), [VMEM] * 2)(back, gate_branch)
     across = swapped(gated, 2)
     beside = swapped(gated, 1)
-    gated_parts = [gated, beside, across, swapped(across, 1)]
-    grad_parts = traded(
-        call(
+    grad_pieces = call(
             backward_kernel,
             (shape((17, 16, rows), BF16),) * 4,
             [SMEM] + [VMEM] * 6,
             work_space(2) + [pltpu.VMEM((16, 4, 16, rows), F32)],
         )(me, beside, my_taps, received, back, spectra, table)
-    )
-    last = call(weight_kernel, shape((16, 208, rows), BF16), [VMEM] * 12)(*cot_parts, *gated_parts, *grad_parts)
+    grad_parts = traded(grad_pieces)
+    across, _ = lax.optimization_barrier((across, grad_pieces[1]))
+    gated_parts = [gated, beside, across, swapped(across, 1)]
+    last = call(weight_kernel, shape((16, 200, rows), BF16), [VMEM] * 12)(*cot_parts, *gated_parts, *grad_parts)
     groups = [list(range(k, owners, 4)) for k in range(4)]
     arrived = lax.all_to_all(last, "seq", 0, 0, axis_index_groups=groups, tiled=True)
 
     grad_gate, own, s1, s2, s3 = call(
         project_kernel,
-        (shape((rows, width), BF16), shape((rows, width), F32)) + (shape((rows, width), BF16),) * 3,
+        (shape((rows, width), BF16),) + (shape((rows, width), F32),) * 4,
         [SMEM] + [VMEM] * 4,
     )(me, back, gated, grad_gated, w_out)
     others = [shifted(s, "chan", d) for d, s in ((1, s1), (2, s2), (3, s3))]
-    output = (own + others[0].astype(F32) + others[1].astype(F32) + others[2].astype(F32)).astype(BF16)
+    output = (own + others[0] + others[1] + others[2]).astype(BF16)
 
     grad_inputs, grad_filters, grad_taps, grad_wout = call(
         unpack_kernel,

time: 101 us -> 99.4 us (0.984)
    all_to_all x1, waiting for transfers between devices: 12.8 us -> 6.48 us  [local(): lax.all_to_all(last, 'seq', 0, 0, axis_index_groups=groups, tiled=True)]
    ppermute x6, waiting for transfers between devices: 8.35 us -> 13.7 us  [shifted(): lax.ppermute(value, axis, [(i, (i + steps) % count) for i in range(count)])]
  transfers between devices with their start and end apart: 17 -> 17, of which waited for: 10 -> 12; matrix products, arithmetic and copies ran while one was open for 1% -> 1% of each run, Pallas kernels for 8% -> 8%
where the time goes in v4:
time: 99.4 us; the launch traced here: 99.1 us
  starting transfers between devices  30 us (30%)
  waiting for transfers between devices  28.8 us (29%)
  blocking collectives  20.8 us (21%)
  Pallas kernels  14.4 us (14%)
  local copies, waits for them, and re-layouts  3.42 us (3%)
    all_to_all x1, blocking collectives, local(): back = lax.all_to_all(sent, 'seq', 0, 0, tiled=True)  20.8 us
    ppermute x6, waiting for transfers between devices, shifted(): lax.ppermute(value, axis, [(i, (i + steps) % count) for i in range(count)])  13.7 us
    all_to_all x1, starting transfers between devices, local(): received = lax.all_to_all(packed, 'seq', 0, 0, tiled=True)  11.9 us
    ppermute x6, starting transfers between devices, shifted(): lax.ppermute(value, axis, [(i, (i + steps) % count) for i in range(count)])  9.42 us
    all_to_all x1, waiting for transfers between devices, local(): lax.all_to_all(last, 'seq', 0, 0, axis_index_groups=groups, tiled=True)  6.48 us
    ppermute x9, waiting for transfers between devices, swapped(): lax.ppermute(value, 'seq', [(i, i ^ distance) for i in range(owners)])  6.25 us
    ppermute x9, starting transfers between devices, swapped(): lax.ppermute(value, 'seq', [(i, i ^ distance) for i in range(owners)])  4.55 us
    all_to_all x1, starting transfers between devices, local(): lax.all_to_all(last, 'seq', 0, 0, axis_index_groups=groups, tiled=True)  4.09 us
  transfers between devices with their start and end apart: 17, of which 12 were waited for; matrix products, arithmetic and copies ran while one was open for 1% of the time, Pallas kernels for 8%

profile of v4, /device:TPU:8, one launch (start us, length us, event | category | flops | bytes accessed | tf_op | source)
XLA Modules:
  0.0 99.1 jit_solution(10310227641782295287)
XLA Ops:
  0.6 0.0 copy-start
  0.6 2.0 %shard_map.118 = bf16[64,24,128]{2,1,0:T(8,128)(2,1)} custom-call(bf16[128,512]{1,0:T(8,128)(2,1)} %inputs_hbm.1, f32[128,512]{1,0:T(8,128)} %filters_hbm.1), custom_call_target="tpu_custom_call" | custom-call | tf_op jit(solution)/shard_map/pallas_call | solution.py:351
  2.6 11.9 %all-to-all-start = ((bf16[64,24,128]{2,1,0:T(8,128)(2,1)}), bf16[64,24,128]{2,1,0:T(8,128)(2,1)S(1)}, u32[]{:S(2)}, u32[]{:S(2)}) async-start(bf16[64,24,128]{2,1,0:T(8,128)(2,1)} %shard_map.118), calls=%async_computation | async-start | bytes 786432 | tf_op jit(solution)/shard_map/all_to_all | solution.py:357
  14.6 1.7 %collective-permute-start = (bf16[128,512]{1,0:T(8,128)(2,1)}, bf16[128,512]{1,0:T(8,128)(2,1)S(1)}, u32[]{:S(2)}, u32[]{:S(2)}) collective-permute-start(bf16[128,512]{1,0:T(8,128)(2,1)} %c0.1), channel_id=1, source_target_pairs={{0,1},{1,2},{2,3},{3,0},{4,5},{5,6},{6,7},{7,4},{8,9},{9,10},{10,1... | collective-permute-start | bytes 393224 | tf_op jit(solution)/shard_map/ppermute | solution.py:340
  16.2 0.9 collective-permute-start.1
  17.2 2.4 %collective-permute-start.2 = (bf16[128,512]{1,0:T(8,128)(2,1)}, bf16[128,512]{1,0:T(8,128)(2,1)S(1)}, u32[]{:S(2)}, u32[]{:S(2)}) collective-permute-start(bf16[128,512]{1,0:T(8,128)(2,1)} %c0.1), channel_id=1, source_target_pairs={{0,3},{1,0},{2,1},{3,2},{4,7},{5,4},{6,5},{7,6},{8,11},{9,8},{10,9... | collective-permute-start | bytes 393224 | tf_op jit(solution)/shard_map/ppermute | solution.py:340
  19.6 0.0 copy-done
  19.6 0.1 constant_dynamic-slice_fusion
  19.6 0.1 copy.14
  19.7 0.1 pad_add_fusion.me_ref
  19.8 0.0 copy-start.1
  19.8 1.6 %copy-done.1 = bf16[512,2048]{1,0:T(8,128)(2,1)S(1)} copy-done((bf16[512,2048]{1,0:T(8,128)(2,1)S(1)}, bf16[512,2048]{1,0:T(8,128)(2,1)}, u32[]{:S(2)}) %copy-start.1) | copy-done | bytes 2097176
  21.4 1.8 %shard_map.119 = (f32[512,128]{1,0:T(8,128)S(1)}, f32[512,128]{1,0:T(8,128)S(1)}) custom-call(s32[2]{0:T(128)S(1)} %pad_add_fusion.me_ref, bf16[128,512]{1,0:T(8,128)(2,1)} %gate_ref.1, bf16[128,512]{1,0:T(8,128)(2,1)} %c0.1, bf16[512,2048]{1,0:T(8,128)(2,1)S(1)} %copy-done.1), custom_call_target="tpu_custom_call" | custom-call | tf_op jit(solution)/shard_map/pallas_call | solution.py:360
  23.2 0.0 copy-start.3
  23.2 0.0 collective-permute-done.c1
  23.2 1.1 %collective-permute-done.1.c2 = bf16[128,512]{1,0:T(8,128)(2,1)S(1)} collective-permute-done((bf16[128,512]{1,0:T(8,128)(2,1)}, bf16[128,512]{1,0:T(8,128)(2,1)S(1)}, u32[]{:S(2)}, u32[]{:S(2)}) %collective-permute-start.1) | collective-permute-done | bytes 131104 | tf_op jit(solution)/shard_map/ppermute | solution.py:340
  24.3 0.9 collective-permute-done.2.c3
  25.2 0.0 copy-start.5
  25.2 1.1 %shard_map.120 = (bf16[512,128]{1,0:T(8,128)(2,1)S(1)}, f32[512,128]{1,0:T(8,128)S(1)}) custom-call(s32[2]{0:T(128)S(1)} %pad_add_fusion.me_ref, f32[512,128]{1,0:T(8,128)S(1)} %get-tuple-element.30.gate_ref, f32[512,128]{1,0:T(8,128)S(1)} %get-tuple-element.31.part_ref, bf16[512,2048]{1,0:T(8,128)(2,1)S(1)} %copy-done.1, ...), custom_call_target="tpu_custom_call" | custom-call | tf_op jit(solution)/shard_map/pallas_call | solution.py:366
  26.4 0.0 copy-start.6
  26.4 0.7 copy-done.6
  27.1 2.4 %all-to-all-done.recv_ref = bf16[64,24,128]{2,1,0:T(8,128)(2,1)S(1)} async-done(((bf16[64,24,128]{2,1,0:T(8,128)(2,1)}), bf16[64,24,128]{2,1,0:T(8,128)(2,1)S(1)}, u32[]{:S(2)}, u32[]{:S(2)}) %all-to-all-start) | async-done | bytes 393248 | tf_op jit(solution)/shard_map/all_to_all | solution.py:357
  29.4 0.0 copy-done.3
  29.4 1.7 %shard_map.121 = (bf16[64,16,128]{2,1,0:T(8,128)(2,1)S(1)}, f32[1024,256]{1,0:T(8,128)S(1)}) custom-call(f32[8,4]{1,0:T(8,128)S(1)} %bitcast.4, bf16[64,24,128]{2,1,0:T(8,128)(2,1)S(1)} %all-to-all-done.recv_ref, bf16[512,128]{1,0:T(8,128)(2,1)S(1)} %get-tuple-element.32.grad_ref, bf16[1408,256]{1,0:T(8,128)(2,1)S(1)} %copy-done.3), custom_call_target="tpu_custom_call" | custom-call | tf_op jit(solution)/shard_map/pallas_call | solution.py:385
  31.2 20.8 %all_to_all.15.recv_ref.back_ref = bf16[64,16,128]{2,1,0:T(8,128)(2,1)S(1)} all-to-all(bf16[64,16,128]{2,1,0:T(8,128)(2,1)S(1)} %get-tuple-element.33), channel_id=1, replica_groups=mesh['seq'=64,'chan'=4] {'seq'}, dimensions={0} | all-to-all | bytes 524288 | tf_op jit(solution)/shard_map/all_to_all | solution.py:391
  52.0 0.0 copy-done.5
  52.0 0.1 shard_map.122.gated_ref.g0
  52.1 0.3 collective-permute-start.9
  52.4 0.7 collective-permute-start.10
  53.1 0.0 copy-done.4
  53.1 0.8 shard_map.124
  53.9 0.2 collective-permute-start.6
  54.1 1.3 %collective-permute-start.7 = (bf16[16,32,128]{2,1,0:T(8,128)(2,1)S(1)}, bf16[16,32,128]{2,1,0:T(8,128)(2,1)S(1)}, u32[]{:S(2)}, u32[]{:S(2)}) collective-permute-start(bf16[16,32,128]{2,1,0:T(8,128)(2,1)S(1)} %get-tuple-element.41), channel_id=1, source_target_pairs={{0,8},{4,12},{8,0},{12,4},{16,24},{20,28},{24,16},{28,20},{32,40},... | collective-permute-start | bytes 393224 | tf_op jit(solution)/shard_map/ppermute | solution.py:380
  55.4 0.5 collective-permute-start.8
  55.9 0.0 collective-permute-done.9._.g1
  55.9 2.4 %shard_map.125 = (bf16[17,16,128]{2,1,0:T(8,128)(2,1)S(1)}, bf16[17,16,128]{2,1,0:T(8,128)(2,1)S(1)}, bf16[17,16,128]{2,1,0:T(8,128)(2,1)S(1)}, bf16[17,16,128]{2,1,0:T(8,128)(2,1)S(1)}) custom-call(s32[2]{0:T(128)S(1)} %pad_add_fusion.me_ref, bf16[128,512]{1,0:T(8,128)(2,1)S(1)} %collective-permute-done.9._.g1, f32[8,4]{1,0:T(8,128)S(1)} %bitcast.5, ...), custom_call_target="tpu_custom_call" | custom-call | tf_op jit(solution)/shard_map/pallas_call | solution.py:405
  58.3 0.0 copy-start.2
  58.3 0.4 collective-permute-done.10.g2
  58.7 0.0 collective-permute-start.11
  58.8 0.5 collective-permute-start.12
  59.2 0.0 collective-permute-done.6.k1
  59.2 1.0 %collective-permute-start.13 = (bf16[17,16,128]{2,1,0:T(8,128)(2,1)S(1)}, bf16[17,16,128]{2,1,0:T(8,128)(2,1)S(1)}, u32[]{:S(2)}, u32[]{:S(2)}) collective-permute-start(bf16[17,16,128]{2,1,0:T(8,128)(2,1)S(1)} %get-tuple-element.47), channel_id=1, source_target_pairs={{0,8},{4,12},{8,0},{12,4},{16,24},{20,28},{24,16},{28,20},{32,40},... | collective-permute-start | bytes 208904 | tf_op jit(solution)/shard_map/ppermute | solution.py:380
  60.3 1.3 %collective-permute-done.7.k2 = bf16[16,32,128]{2,1,0:T(8,128)(2,1)S(1)} collective-permute-done((bf16[16,32,128]{2,1,0:T(8,128)(2,1)S(1)}, bf16[16,32,128]{2,1,0:T(8,128)(2,1)S(1)}, u32[]{:S(2)}, u32[]{:S(2)}) %collective-permute-start.7) | collective-permute-done | bytes 131104 | tf_op jit(solution)/shard_map/ppermute | solution.py:380
  61.5 0.0 collective-permute-start.14
  61.5 1.5 %collective-permute-done.8.k3 = bf16[16,32,128]{2,1,0:T(8,128)(2,1)S(1)} collective-permute-done((bf16[16,32,128]{2,1,0:T(8,128)(2,1)S(1)}, bf16[16,32,128]{2,1,0:T(8,128)(2,1)S(1)}, u32[]{:S(2)}, u32[]{:S(2)}) %collective-permute-start.8) | collective-permute-done | bytes 131104 | tf_op jit(solution)/shard_map/ppermute | solution.py:380
  63.0 0.0 collective-permute-done.12.p1
  63.0 2.7 %collective-permute-done.13.p2 = bf16[17,16,128]{2,1,0:T(8,128)(2,1)S(1)} collective-permute-done((bf16[17,16,128]{2,1,0:T(8,128)(2,1)S(1)}, bf16[17,16,128]{2,1,0:T(8,128)(2,1)S(1)}, u32[]{:S(2)}, u32[]{:S(2)}) %collective-permute-start.13) | collective-permute-done | bytes 69664 | tf_op jit(solution)/shard_map/ppermute | solution.py:380
  65.8 0.3 collective-permute-done.14.p3
  66.1 0.0 collective-permute-done.11.g3
  66.1 1.4 %shard_map.126 = bf16[16,200,128]{2,1,0:T(8,128)(2,1)} custom-call(bf16[16,32,128]{2,1,0:T(8,128)(2,1)S(1)} %get-tuple-element.39.k0, bf16[16,32,128]{2,1,0:T(8,128)(2,1)S(1)} %collective-permute-done.6.k1, bf16[16,32,128]{2,1,0:T(8,128)(2,1)S(1)} %collective-permute-done.7.k2, bf16[16,32,128]{2,1,0:T(8,128)(2,1)S(1)} %collective-permute-done.8.k3, ...), custom_call_target="tpu_custom_call" | custom-call | tf_op jit(solution)/shard_map/pallas_call | solution.py:414
  67.4 4.1 %all-to-all-start.2 = ((bf16[16,200,128]{2,1,0:T(8,128)(2,1)}), bf16[16,200,128]{2,1,0:T(8,128)(2,1)S(1)}, u32[]{:S(2)}, u32[]{:S(2)}) async-start(bf16[16,200,128]{2,1,0:T(8,128)(2,1)} %shard_map.126), calls=%async_computation.2 | async-start | bytes 1638400 | tf_op jit(solution)/shard_map/all_to_all | solution.py:416
  71.5 0.0 copy-done.2
  71.6 0.0 copy-start.7
  71.6 0.9 copy-done.7
  72.5 1.6 %shard_map.123 = (bf16[128,512]{1,0:T(8,128)(2,1)}, f32[128,512]{1,0:T(8,128)S(1)}, f32[128,512]{1,0:T(8,128)S(1)}, f32[128,512]{1,0:T(8,128)S(1)}, f32[128,512]{1,0:T(8,128)S(1)}) custom-call(s32[2]{0:T(128)S(1)} %pad_add_fusion.me_ref, bf16[64,16,128]{2,1,0:T(8,128)(2,1)S(1)} %all_to_all.15.recv_ref.back_ref, ...), custom_call_target="tpu_custom_call" | custom-call | tf_op jit(solution)/shard_map/pallas_call | solution.py:418
  74.1 1.3 %collective-permute-start.3 = (f32[128,512]{1,0:T(8,128)S(1)}, f32[128,512]{1,0:T(8,128)S(1)}, u32[]{:S(2)}, u32[]{:S(2)}) collective-permute-start(f32[128,512]{1,0:T(8,128)S(1)} %get-tuple-element.36), channel_id=1, source_target_pairs={{0,1},{1,2},{2,3},{3,0},{4,5},{5,6},{6,7},{7,4},{8,9},{9,10},{10,1... | collective-permute-start | bytes 786440 | tf_op jit(solution)/shard_map/ppermute | solution.py:340
  75.4 1.6 %collective-permute-start.4 = (f32[128,512]{1,0:T(8,128)S(1)}, f32[128,512]{1,0:T(8,128)S(1)}, u32[]{:S(2)}, u32[]{:S(2)}) collective-permute-start(f32[128,512]{1,0:T(8,128)S(1)} %get-tuple-element.37), channel_id=1, source_target_pairs={{0,2},{1,3},{2,0},{3,1},{4,6},{5,7},{6,4},{7,5},{8,10},{9,11},{10,... | collective-permute-start | bytes 786440 | tf_op jit(solution)/shard_map/ppermute | solution.py:340
  77.0 1.6 %collective-permute-start.5 = (f32[128,512]{1,0:T(8,128)S(1)}, f32[128,512]{1,0:T(8,128)S(1)}, u32[]{:S(2)}, u32[]{:S(2)}) collective-permute-start(f32[128,512]{1,0:T(8,128)S(1)} %get-tuple-element.38), channel_id=1, source_target_pairs={{0,3},{1,0},{2,1},{3,2},{4,7},{5,4},{6,5},{7,6},{8,11},{9,8},{10,9... | collective-permute-start | bytes 786440 | tf_op jit(solution)/shard_map/ppermute | solution.py:340
  78.5 4.8 %collective-permute-done.3 = f32[128,512]{1,0:T(8,128)S(1)} collective-permute-done((f32[128,512]{1,0:T(8,128)S(1)}, f32[128,512]{1,0:T(8,128)S(1)}, u32[]{:S(2)}, u32[]{:S(2)}) %collective-permute-start.3) | collective-permute-done | bytes 262176 | tf_op jit(solution)/shard_map/ppermute | solution.py:340
  83.3 2.8 %collective-permute-done.4 = f32[128,512]{1,0:T(8,128)S(1)} collective-permute-done((f32[128,512]{1,0:T(8,128)S(1)}, f32[128,512]{1,0:T(8,128)S(1)}, u32[]{:S(2)}, u32[]{:S(2)}) %collective-permute-start.4) | collective-permute-done | bytes 262176 | tf_op jit(solution)/shard_map/ppermute | solution.py:340
  86.1 4.1 %collective-permute-done.5 = f32[128,512]{1,0:T(8,128)S(1)} collective-permute-done((f32[128,512]{1,0:T(8,128)S(1)}, f32[128,512]{1,0:T(8,128)S(1)}, u32[]{:S(2)}, u32[]{:S(2)}) %collective-permute-start.5) | collective-permute-done | bytes 262176 | tf_op jit(solution)/shard_map/ppermute | solution.py:340
  90.3 0.7 add_convert_fusion
  91.0 6.5 %all-to-all-done.2.recv_ref = bf16[16,200,128]{2,1,0:T(8,128)(2,1)S(1)} async-done(((bf16[16,200,128]{2,1,0:T(8,128)(2,1)}), bf16[16,200,128]{2,1,0:T(8,128)(2,1)S(1)}, u32[]{:S(2)}, u32[]{:S(2)}) %all-to-all-start.2) | async-done | bytes 819232 | tf_op jit(solution)/shard_map/all_to_all | solution.py:416
  97.5 1.6 %shard_map.127 = (bf16[128,512]{1,0:T(8,128)(2,1)}, f32[128,512]{1,0:T(8,128)}, f32[4,512]{1,0:T(4,128)}, f32[32,512]{1,0:T(8,128)}) custom-call(s32[2]{0:T(128)S(1)} %pad_add_fusion.me_ref, bf16[16,200,128]{2,1,0:T(8,128)(2,1)S(1)} %all-to-all-done.2.recv_ref), custom_call_target="tpu_custom_call" | custom-call | tf_op jit(solution)/shard_map/pallas_call | solution.py:426
  (1 shorter events, 0.0 us)
Async XLA Ops:
  0.6 18.9 %copy-start = (f32[4,512]{1,0:T(4,128)S(1)}, f32[4,512]{1,0:T(4,128)}, u32[]{:S(2)}) copy-start(f32[4,512]{1,0:T(4,128)} %param.9) | copy-start | bytes 24580
  2.6 26.8 %all-to-all-start = ((bf16[64,24,128]{2,1,0:T(8,128)(2,1)}), bf16[64,24,128]{2,1,0:T(8,128)(2,1)S(1)}, u32[]{:S(2)}, u32[]{:S(2)}) async-start(bf16[64,24,128]{2,1,0:T(8,128)(2,1)} %shard_map.118), calls=%async_computation | async-start | bytes 786432 | tf_op jit(solution)/shard_map/all_to_all | solution.py:357
  14.6 8.7 %collective-permute-start = (bf16[128,512]{1,0:T(8,128)(2,1)}, bf16[128,512]{1,0:T(8,128)(2,1)S(1)}, u32[]{:S(2)}, u32[]{:S(2)}) collective-permute-start(bf16[128,512]{1,0:T(8,128)(2,1)} %c0.1), channel_id=1, source_target_pairs={{0,1},{1,2},{2,3},{3,0},{4,5},{5,6},{6,7},{7,4},{8,9},{9,10},{10,1... | collective-permute-start | bytes 393224 | tf_op jit(solution)/shard_map/ppermute | solution.py:340
  16.2 8.1 %collective-permute-start.1 = (bf16[128,512]{1,0:T(8,128)(2,1)}, bf16[128,512]{1,0:T(8,128)(2,1)S(1)}, u32[]{:S(2)}, u32[]{:S(2)}) collective-permute-start(bf16[128,512]{1,0:T(8,128)(2,1)} %c0.1), channel_id=1, source_target_pairs={{0,2},{1,3},{2,0},{3,1},{4,6},{5,7},{6,4},{7,5},{8,10},{9,11},{10,... | collective-permute-start | bytes 393224 | tf_op jit(solution)/shard_map/ppermute | solution.py:340
  17.2 8.1 %collective-permute-start.2 = (bf16[128,512]{1,0:T(8,128)(2,1)}, bf16[128,512]{1,0:T(8,128)(2,1)S(1)}, u32[]{:S(2)}, u32[]{:S(2)}) collective-permute-start(bf16[128,512]{1,0:T(8,128)(2,1)} %c0.1), channel_id=1, source_target_pairs={{0,3},{1,0},{2,1},{3,2},{4,7},{5,4},{6,5},{7,6},{8,11},{9,8},{10,9... | collective-permute-start | bytes 393224 | tf_op jit(solution)/shard_map/ppermute | solution.py:340
  19.8 1.6 %copy-start.1 = (bf16[512,2048]{1,0:T(8,128)(2,1)S(1)}, bf16[512,2048]{1,0:T(8,128)(2,1)}, u32[]{:S(2)}) copy-start(bf16[512,2048]{1,0:T(8,128)(2,1)} %w_ref.5) | copy-start | bytes 6291460
  23.2 6.2 %copy-start.3 = (bf16[1408,256]{1,0:T(8,128)(2,1)S(1)}, bf16[1408,256]{1,0:T(8,128)(2,1)}, u32[]{:S(2)}) copy-start(bf16[1408,256]{1,0:T(8,128)(2,1)} %constant.17.clone.table_ref) | copy-start | bytes 2162692
  25.2 26.7 %copy-start.5 = (bf16[128,512]{1,0:T(8,128)(2,1)S(1)}, bf16[128,512]{1,0:T(8,128)(2,1)}, u32[]{:S(2)}) copy-start(bf16[128,512]{1,0:T(8,128)(2,1)} %gate_ref.1) | copy-start | bytes 393220
  25.2 27.9 %copy-start.4 = (bf16[128,512]{1,0:T(8,128)(2,1)S(1)}, bf16[128,512]{1,0:T(8,128)(2,1)}, u32[]{:S(2)}) copy-start(bf16[128,512]{1,0:T(8,128)(2,1)} %c0.1) | copy-start | bytes 393220
  26.4 0.7 copy-start.6
  52.1 3.8 %collective-permute-start.9 = (bf16[128,512]{1,0:T(8,128)(2,1)S(1)}, bf16[128,512]{1,0:T(8,128)(2,1)S(1)}, u32[]{:S(2)}, u32[]{:S(2)}) collective-permute-start(bf16[128,512]{1,0:T(8,128)(2,1)S(1)} %shard_map.122.gated_ref.g0), channel_id=1, source_target_pairs={{0,4},{4,0},{8,12},{12,8},{16,20},{20,16},{24,28},{28,24},{32,36},... | collective-permute-start | bytes 393224 | tf_op jit(solution)/shard_map/ppermute | solution.py:380
  52.4 6.3 %collective-permute-start.10 = (bf16[128,512]{1,0:T(8,128)(2,1)S(1)}, bf16[128,512]{1,0:T(8,128)(2,1)S(1)}, u32[]{:S(2)}, u32[]{:S(2)}) collective-permute-start(bf16[128,512]{1,0:T(8,128)(2,1)S(1)} %shard_map.122.gated_ref.g0), channel_id=1, source_target_pairs={{0,8},{4,12},{8,0},{12,4},{16,24},{20,28},{24,16},{28,20},{32,40},... | collective-permute-start | bytes 393224 | tf_op jit(solution)/shard_map/ppermute | solution.py:380
  53.9 5.3 %collective-permute-start.6 = (bf16[16,32,128]{2,1,0:T(8,128)(2,1)S(1)}, bf16[16,32,128]{2,1,0:T(8,128)(2,1)S(1)}, u32[]{:S(2)}, u32[]{:S(2)}) collective-permute-start(bf16[16,32,128]{2,1,0:T(8,128)(2,1)S(1)} %get-tuple-element.40), channel_id=1, source_target_pairs={{0,4},{4,0},{8,12},{12,8},{16,20},{20,16},{24,28},{28,24},{32,36},... | collective-permute-start | bytes 393224 | tf_op jit(solution)/shard_map/ppermute | solution.py:380
  54.1 7.4 %collective-permute-start.7 = (bf16[16,32,128]{2,1,0:T(8,128)(2,1)S(1)}, bf16[16,32,128]{2,1,0:T(8,128)(2,1)S(1)}, u32[]{:S(2)}, u32[]{:S(2)}) collective-permute-start(bf16[16,32,128]{2,1,0:T(8,128)(2,1)S(1)} %get-tuple-element.41), channel_id=1, source_target_pairs={{0,8},{4,12},{8,0},{12,4},{16,24},{20,28},{24,16},{28,20},{32,40},... | collective-permute-start | bytes 393224 | tf_op jit(solution)/shard_map/ppermute | solution.py:380
  55.4 7.6 %collective-permute-start.8 = (bf16[16,32,128]{2,1,0:T(8,128)(2,1)S(1)}, bf16[16,32,128]{2,1,0:T(8,128)(2,1)S(1)}, u32[]{:S(2)}, u32[]{:S(2)}) collective-permute-start(bf16[16,32,128]{2,1,0:T(8,128)(2,1)S(1)} %get-tuple-element.42), channel_id=1, source_target_pairs={{0,12},{4,8},{8,4},{12,0},{16,28},{20,24},{24,20},{28,16},{32,44},... | collective-permute-start | bytes 393224 | tf_op jit(solution)/shard_map/ppermute | solution.py:380
  58.3 13.2 %copy-start.2 = (bf16[512,2048]{1,0:T(8,128)(2,1)S(1)}, bf16[512,2048]{1,0:T(8,128)(2,1)}, u32[]{:S(2)}) copy-start(bf16[512,2048]{1,0:T(8,128)(2,1)} %w_ref.5) | copy-start | bytes 6291460
  58.7 7.4 %collective-permute-start.11 = (bf16[128,512]{1,0:T(8,128)(2,1)S(1)}, bf16[128,512]{1,0:T(8,128)(2,1)S(1)}, u32[]{:S(2)}, u32[]{:S(2)}) collective-permute-start(bf16[128,512]{1,0:T(8,128)(2,1)S(1)} %collective-permute-done.10.g2), channel_id=1, source_target_pairs={{0,4},{4,0},{8,12},{12,8},{16,20},{20,16},{24,28},{28,24},{32,36},... | collective-permute-start | bytes 393224 | tf_op jit(solution)/shard_map/ppermute | solution.py:380
  58.8 4.2 %collective-permute-start.12 = (bf16[17,16,128]{2,1,0:T(8,128)(2,1)S(1)}, bf16[17,16,128]{2,1,0:T(8,128)(2,1)S(1)}, u32[]{:S(2)}, u32[]{:S(2)}) collective-permute-start(bf16[17,16,128]{2,1,0:T(8,128)(2,1)S(1)} %get-tuple-element.44), channel_id=1, source_target_pairs={{0,4},{4,0},{8,12},{12,8},{16,20},{20,16},{24,28},{28,24},{32,36},... | collective-permute-start | bytes 208904 | tf_op jit(solution)/shard_map/ppermute | solution.py:380
  59.2 6.5 %collective-permute-start.13 = (bf16[17,16,128]{2,1,0:T(8,128)(2,1)S(1)}, bf16[17,16,128]{2,1,0:T(8,128)(2,1)S(1)}, u32[]{:S(2)}, u32[]{:S(2)}) collective-permute-start(bf16[17,16,128]{2,1,0:T(8,128)(2,1)S(1)} %get-tuple-element.47), channel_id=1, source_target_pairs={{0,8},{4,12},{8,0},{12,4},{16,24},{20,28},{24,16},{28,20},{32,40},... | collective-permute-start | bytes 208904 | tf_op jit(solution)/shard_map/ppermute | solution.py:380
  61.5 4.5 %collective-permute-start.14 = (bf16[17,16,128]{2,1,0:T(8,128)(2,1)S(1)}, bf16[17,16,128]{2,1,0:T(8,128)(2,1)S(1)}, u32[]{:S(2)}, u32[]{:S(2)}) collective-permute-start(bf16[17,16,128]{2,1,0:T(8,128)(2,1)S(1)} %get-tuple-element.48), channel_id=1, source_target_pairs={{0,12},{4,8},{8,4},{12,0},{16,28},{20,24},{24,20},{28,16},{32,44},... | collective-permute-start | bytes 208904 | tf_op jit(solution)/shard_map/ppermute | solution.py:380
  67.4 30.0 %all-to-all-start.2 = ((bf16[16,200,128]{2,1,0:T(8,128)(2,1)}), bf16[16,200,128]{2,1,0:T(8,128)(2,1)S(1)}, u32[]{:S(2)}, u32[]{:S(2)}) async-start(bf16[16,200,128]{2,1,0:T(8,128)(2,1)} %shard_map.126), calls=%async_computation.2 | async-start | bytes 1638400 | tf_op jit(solution)/shard_map/all_to_all | solution.py:416
  71.6 1.0 copy-start.7
  74.1 9.2 %collective-permute-start.3 = (f32[128,512]{1,0:T(8,128)S(1)}, f32[128,512]{1,0:T(8,128)S(1)}, u32[]{:S(2)}, u32[]{:S(2)}) collective-permute-start(f32[128,512]{1,0:T(8,128)S(1)} %get-tuple-element.36), channel_id=1, source_target_pairs={{0,1},{1,2},{2,3},{3,0},{4,5},{5,6},{6,7},{7,4},{8,9},{9,10},{10,1... | collective-permute-start | bytes 786440 | tf_op jit(solution)/shard_map/ppermute | solution.py:340
  75.4 10.7 %collective-permute-start.4 = (f32[128,512]{1,0:T(8,128)S(1)}, f32[128,512]{1,0:T(8,128)S(1)}, u32[]{:S(2)}, u32[]{:S(2)}) collective-permute-start(f32[128,512]{1,0:T(8,128)S(1)} %get-tuple-element.37), channel_id=1, source_target_pairs={{0,2},{1,3},{2,0},{3,1},{4,6},{5,7},{6,4},{7,5},{8,10},{9,11},{10,... | collective-permute-start | bytes 786440 | tf_op jit(solution)/shard_map/ppermute | solution.py:340
  77.0 13.3 %collective-permute-start.5 = (f32[128,512]{1,0:T(8,128)S(1)}, f32[128,512]{1,0:T(8,128)S(1)}, u32[]{:S(2)}, u32[]{:S(2)}) collective-permute-start(f32[128,512]{1,0:T(8,128)S(1)} %get-tuple-element.38), channel_id=1, source_target_pairs={{0,3},{1,0},{2,1},{3,2},{4,7},{5,4},{6,5},{7,6},{8,11},{9,8},{10,9... | collective-permute-start | bytes 786440 | tf_op jit(solution)/shard_map/ppermute | solution.py:340

commit v5 on v4

--- a/solution.py
+++ b/solution.py
@@ -116,7 +116,7 @@
     gate_out[...] = gate_ref[...].astype(F32).T
 
 
-def cotangent_kernel(me_ref, gate_ref, part_ref, w_ref, c1, c2, c3, out_ref, gg_ref):
+def cotangent_kernel(me_ref, gate_ref, part_ref, w_ref, c1, c2, c3, out_ref):
     chan = me_ref[1]
     width = gate_ref.shape[0]
     total = part_ref[...]
@@ -124,7 +124,6 @@
         owner = lax.rem(chan + 3 - step, 4)
         cols = pl.ds(pl.multiple_of(owner * width, width), width)
         total = total + dot(w_ref[:, cols], piece[...], NT)
-    gg_ref[...] = total
     out_ref[...] = (total * gate_ref[...]).astype(BF16)
 
 
@@ -292,12 +291,23 @@
     out_ref[:, 192:200, :] = jnp.broadcast_to(tap_rows[None, :8], (groups, 8, depth)).astype(BF16)
 
 
-def project_kernel(me_ref, recv_ref, gated_ref, gg_ref, w_ref, gate_grad_ref, own_ref, s1, s2, s3):
+def gate_grad_kernel(me_ref, recv_ref, w_ref, c0, c1, c2, c3, gate_grad_ref):
     chan = me_ref[1]
     blocks, _, rows = recv_ref.shape
+    width = c0.shape[1]
+    total = None
+    for step, piece in enumerate((c0, c1, c2, c3)):
+        owner = lax.rem(chan + 4 - step, 4)
+        cols = pl.ds(pl.multiple_of(owner * width, width), width)
+        term = dot(w_ref[:, cols], piece[...], NT)
+        total = term if total is None else total + term
+    convolved = recv_ref[...].astype(F32)[:, 0:8].reshape(width, rows)
+    gate_grad_ref[...] = (total * convolved).T.astype(BF16)
+
+
+def project_kernel(me_ref, gated_ref, w_ref, own_ref, s1, s2, s3):
+    chan = me_ref[1]
     width = gated_ref.shape[1]
-    convolved = recv_ref[...].astype(F32)[:, 0:8].reshape(width, rows)
-    gate_grad_ref[...] = (gg_ref[...] * convolved).T.astype(BF16)
     for step, out in enumerate((own_ref, s1, s2, s3)):
         owner = lax.rem(chan + step, 4)
         cols = pl.ds(pl.multiple_of(owner * width, width), width)
@@ -363,9 +373,9 @@
         [SMEM, HBM, HBM, VMEM],
         [pltpu.VMEM((rows, width), BF16)] * 2 + [pltpu.SemaphoreType.DMA((2,))],
     )(me, far(gate_branch), far(cotangent), w_out)
-    grad_packed, grad_gated = call(
+    grad_packed = call(
         cotangent_kernel,
-        (shape((width, rows), BF16), shape((width, rows), F32)),
+        shape((width, rows), BF16),
         [SMEM] + [VMEM] * 6,
     )(me, gate_flipped, own_part, w_out, *pieces)
 
@@ -411,15 +421,16 @@
     grad_parts = traded(grad_pieces)
     across, _ = lax.optimization_barrier((across, grad_pieces[1]))
     gated_parts = [gated, beside, across, swapped(across, 1)]
+    grad_gate = call(gate_grad_kernel, shape((rows, width), BF16), [SMEM] + [VMEM] * 6)(
+        me, back, w_out, cotangent, *pieces
+    )
     last = call(weight_kernel, shape((16, 200, rows), BF16), [VMEM] * 12)(*cot_parts, *gated_parts, *grad_parts)
     groups = [list(range(k, owners, 4)) for k in range(4)]
     arrived = lax.all_to_all(last, "seq", 0, 0, axis_index_groups=groups, tiled=True)
 
-    grad_gate, own, s1, s2, s3 = call(
-        project_kernel,
-        (shape((rows, width), BF16),) + (shape((rows, width), F32),) * 4,
-        [SMEM] + [VMEM] * 4,
-    )(me, back, gated, grad_gated, w_out)
+    own, s1, s2, s3 = call(
+        project_kernel, (shape((rows, width), F32),) * 4, [SMEM] + [VMEM] * 2
+    )(me, gated, w_out)
     others = [shifted(s, "chan", d) for d, s in ((1, s1), (2, s2), (3, s3))]
     output = (own + others[0] + others[1] + others[2]).astype(BF16)
 

time: 99.4 us -> 98.7 us (level)
  local copies, waits for them, and re-layouts: 3.42 us -> 1.81 us
  Pallas kernels: 14.4 us -> 15.8 us
    ppermute x6, waiting for transfers between devices: 13.7 us -> 11.7 us  [shifted(): lax.ppermute(value, axis, [(i, (i + steps) % count) for i in range(count)])]
    unnamed x17 -> x25, local copies, waits for them, and re-layouts: 3.35 us -> 1.74 us
    all_to_all x1, waiting for transfers between devices: 6.48 us -> 7.92 us  [local(): lax.all_to_all(last, 'seq', 0, 0, axis_index_groups=groups, tiled=True)]
    pallas_call x2 -> x3, Pallas kernels: 2.73 us -> 4.09 us  [the longest x1 1.98 us: local(): call(gate_grad_kernel, shape((rows, width), BF16), [SMEM] + [VMEM] * 6)]
  transfers between devices with their start and end apart: 17 -> 17, of which waited for: 12 -> 12; matrix products, arithmetic and copies ran while one was open for 1% -> 1% of each run, Pallas kernels for 8% -> 9%
where the time goes in v5:
time: 98.7 us; the launch traced here: 98.4 us
  starting transfers between devices  30.1 us (30%)
  waiting for transfers between devices  29 us (29%)
  blocking collectives  20.1 us (20%)
  Pallas kernels  15.8 us (16%)
  local copies, waits for them, and re-layouts  1.81 us (2%)
    all_to_all x1, blocking collectives, local(): back = lax.all_to_all(sent, 'seq', 0, 0, tiled=True)  20.1 us
    all_to_all x1, starting transfers between devices, local(): received = lax.all_to_all(packed, 'seq', 0, 0, tiled=True)  11.9 us
    ppermute x6, waiting for transfers between devices, shifted(): lax.ppermute(value, axis, [(i, (i + steps) % count) for i in range(count)])  11.7 us
    ppermute x6, starting transfers between devices, shifted(): lax.ppermute(value, axis, [(i, (i + steps) % count) for i in range(count)])  9.5 us
    all_to_all x1, waiting for transfers between devices, local(): lax.all_to_all(last, 'seq', 0, 0, axis_index_groups=groups, tiled=True)  7.92 us
    ppermute x9, waiting for transfers between devices, swapped(): lax.ppermute(value, 'seq', [(i, i ^ distance) for i in range(owners)])  6.22 us
    ppermute x9, starting transfers between devices, swapped(): lax.ppermute(value, 'seq', [(i, i ^ distance) for i in range(owners)])  4.56 us
    all_to_all x1, starting transfers between devices, local(): lax.all_to_all(last, 'seq', 0, 0, axis_index_groups=groups, tiled=True)  4.09 us
  transfers between devices with their start and end apart: 17, of which 12 were waited for; matrix products, arithmetic and copies ran while one was open for 1% of the time, Pallas kernels for 9%

profile of v5, /device:TPU:8, one launch (start us, length us, event | category | flops | bytes accessed | tf_op | source)
XLA Modules:
  0.0 98.4 jit_solution(2588100314463285304)
XLA Ops:
  0.6 0.0 copy-start
  0.6 2.0 %shard_map.118 = bf16[64,24,128]{2,1,0:T(8,128)(2,1)} custom-call(bf16[128,512]{1,0:T(8,128)(2,1)} %inputs_hbm.1, f32[128,512]{1,0:T(8,128)} %filters_hbm.1), custom_call_target="tpu_custom_call" | custom-call | tf_op jit(solution)/shard_map/pallas_call | solution.py:361
  2.6 11.9 %all-to-all-start = ((bf16[64,24,128]{2,1,0:T(8,128)(2,1)}), bf16[64,24,128]{2,1,0:T(8,128)(2,1)S(1)}, u32[]{:S(2)}, u32[]{:S(2)}) async-start(bf16[64,24,128]{2,1,0:T(8,128)(2,1)} %shard_map.118), calls=%async_computation | async-start | bytes 786432 | tf_op jit(solution)/shard_map/all_to_all | solution.py:367
  14.6 1.7 %collective-permute-start = (bf16[128,512]{1,0:T(8,128)(2,1)}, bf16[128,512]{1,0:T(8,128)(2,1)S(1)}, u32[]{:S(2)}, u32[]{:S(2)}) collective-permute-start(bf16[128,512]{1,0:T(8,128)(2,1)} %c0.3), channel_id=1, source_target_pairs={{0,1},{1,2},{2,3},{3,0},{4,5},{5,6},{6,7},{7,4},{8,9},{9,10},{10,1... | collective-permute-start | bytes 393224 | tf_op jit(solution)/shard_map/ppermute | solution.py:350
  16.2 0.9 collective-permute-start.1
  17.2 2.4 %collective-permute-start.2 = (bf16[128,512]{1,0:T(8,128)(2,1)}, bf16[128,512]{1,0:T(8,128)(2,1)S(1)}, u32[]{:S(2)}, u32[]{:S(2)}) collective-permute-start(bf16[128,512]{1,0:T(8,128)(2,1)} %c0.3), channel_id=1, source_target_pairs={{0,3},{1,0},{2,1},{3,2},{4,7},{5,4},{6,5},{7,6},{8,11},{9,8},{10,9... | collective-permute-start | bytes 393224 | tf_op jit(solution)/shard_map/ppermute | solution.py:350
  19.6 0.0 copy-done
  19.6 0.1 constant_dynamic-slice_fusion
  19.6 0.1 copy.14
  19.7 0.1 pad_add_fusion.me_ref
  19.8 1.6 %copy-done.1 = bf16[512,2048]{1,0:T(8,128)(2,1)S(1)} copy-done((bf16[512,2048]{1,0:T(8,128)(2,1)S(1)}, bf16[512,2048]{1,0:T(8,128)(2,1)}, u32[]{:S(2)}) %copy-start.1) | copy-done | bytes 2097176
  21.4 1.8 %shard_map.119 = (f32[512,128]{1,0:T(8,128)S(1)}, f32[512,128]{1,0:T(8,128)S(1)}) custom-call(s32[2]{0:T(128)S(1)} %pad_add_fusion.me_ref, bf16[128,512]{1,0:T(8,128)(2,1)} %gate_ref.1, bf16[128,512]{1,0:T(8,128)(2,1)} %c0.3, bf16[512,2048]{1,0:T(8,128)(2,1)S(1)} %copy-done.1), custom_call_target="tpu_custom_call" | custom-call | tf_op jit(solution)/shard_map/pallas_call | solution.py:370
  23.2 0.0 copy-start.3
  23.2 0.0 collective-permute-done.c1
  23.3 0.0 copy-start.5
  23.3 1.1 %collective-permute-done.1.c2 = bf16[128,512]{1,0:T(8,128)(2,1)S(1)} collective-permute-done((bf16[128,512]{1,0:T(8,128)(2,1)}, bf16[128,512]{1,0:T(8,128)(2,1)S(1)}, u32[]{:S(2)}, u32[]{:S(2)}) %collective-permute-start.1) | collective-permute-done | bytes 131104 | tf_op jit(solution)/shard_map/ppermute | solution.py:350
  24.3 0.9 collective-permute-done.2.c3
  25.2 1.1 %shard_map.120.grad_ref = bf16[512,128]{1,0:T(8,128)(2,1)S(1)} custom-call(s32[2]{0:T(128)S(1)} %pad_add_fusion.me_ref, f32[512,128]{1,0:T(8,128)S(1)} %get-tuple-element.27.gate_ref, f32[512,128]{1,0:T(8,128)S(1)} %get-tuple-element.28.part_ref, bf16[512,2048]{1,0:T(8,128)(2,1)S(1)} %copy-done.1, bf16[128,512]{1,0:T(8,128)(2,1)S(1)} %collective-permute-done.c1, ...), custom_call_target="tpu_custom_call" | custom-call | tf_op jit(solution)/shard_map/pallas_call | solution.py:376
  26.4 3.1 %all-to-all-done.recv_ref = bf16[64,24,128]{2,1,0:T(8,128)(2,1)S(1)} async-done(((bf16[64,24,128]{2,1,0:T(8,128)(2,1)}), bf16[64,24,128]{2,1,0:T(8,128)(2,1)S(1)}, u32[]{:S(2)}, u32[]{:S(2)}) %all-to-all-start) | async-done | bytes 393248 | tf_op jit(solution)/shard_map/all_to_all | solution.py:367
  29.4 0.0 copy-done.3
  29.4 1.7 %shard_map.121 = (bf16[64,16,128]{2,1,0:T(8,128)(2,1)S(1)}, f32[1024,256]{1,0:T(8,128)S(1)}) custom-call(f32[8,4]{1,0:T(8,128)S(1)} %bitcast.4, bf16[64,24,128]{2,1,0:T(8,128)(2,1)S(1)} %all-to-all-done.recv_ref, bf16[512,128]{1,0:T(8,128)(2,1)S(1)} %shard_map.120.grad_ref, bf16[1408,256]{1,0:T(8,128)(2,1)S(1)} %copy-done.3), custom_call_target="tpu_custom_call" | custom-call | tf_op jit(solution)/shard_map/pallas_call | solution.py:395
  31.2 20.1 %all_to_all.15.recv_ref.back_ref = bf16[64,16,128]{2,1,0:T(8,128)(2,1)S(1)} all-to-all(bf16[64,16,128]{2,1,0:T(8,128)(2,1)S(1)} %get-tuple-element.29), channel_id=1, replica_groups=mesh['seq'=64,'chan'=4] {'seq'}, dimensions={0} | all-to-all | bytes 524288 | tf_op jit(solution)/shard_map/all_to_all | solution.py:401
  51.3 0.0 copy-done.11
  51.3 0.1 shard_map.122.gated_ref.g0
  51.4 0.3 collective-permute-start.9
  51.7 0.7 collective-permute-start.10
  52.4 0.0 copy-done.5
  52.4 0.0 copy-done.7
  52.5 0.8 shard_map.124
  53.3 0.2 collective-permute-start.6
  53.4 1.3 %collective-permute-start.7 = (bf16[16,32,128]{2,1,0:T(8,128)(2,1)S(1)}, bf16[16,32,128]{2,1,0:T(8,128)(2,1)S(1)}, u32[]{:S(2)}, u32[]{:S(2)}) collective-permute-start(bf16[16,32,128]{2,1,0:T(8,128)(2,1)S(1)} %get-tuple-element.36), channel_id=1, source_target_pairs={{0,8},{4,12},{8,0},{12,4},{16,24},{20,28},{24,16},{28,20},{32,40},... | collective-permute-start | bytes 393224 | tf_op jit(solution)/shard_map/ppermute | solution.py:390
  54.7 0.5 collective-permute-start.8
  55.2 0.0 collective-permute-done.9._.g1
  55.2 2.4 %shard_map.125 = (bf16[17,16,128]{2,1,0:T(8,128)(2,1)S(1)}, bf16[17,16,128]{2,1,0:T(8,128)(2,1)S(1)}, bf16[17,16,128]{2,1,0:T(8,128)(2,1)S(1)}, bf16[17,16,128]{2,1,0:T(8,128)(2,1)S(1)}) custom-call(s32[2]{0:T(128)S(1)} %pad_add_fusion.me_ref, bf16[128,512]{1,0:T(8,128)(2,1)S(1)} %collective-permute-done.9._.g1, f32[8,4]{1,0:T(8,128)S(1)} %bitcast.5, ...), custom_call_target="tpu_custom_call" | custom-call | tf_op jit(solution)/shard_map/pallas_call | solution.py:415
  57.6 0.0 copy-start.2
  57.6 0.4 collective-permute-done.10.g2
  58.0 0.1 collective-permute-start.11
  58.1 0.5 collective-permute-start.12
  58.6 0.0 collective-permute-done.6.k1
  58.6 1.0 %collective-permute-start.13 = (bf16[17,16,128]{2,1,0:T(8,128)(2,1)S(1)}, bf16[17,16,128]{2,1,0:T(8,128)(2,1)S(1)}, u32[]{:S(2)}, u32[]{:S(2)}) collective-permute-start(bf16[17,16,128]{2,1,0:T(8,128)(2,1)S(1)} %get-tuple-element.42), channel_id=1, source_target_pairs={{0,8},{4,12},{8,0},{12,4},{16,24},{20,28},{24,16},{28,20},{32,40},... | collective-permute-start | bytes 208904 | tf_op jit(solution)/shard_map/ppermute | solution.py:390
  59.6 1.3 %collective-permute-done.7.k2 = bf16[16,32,128]{2,1,0:T(8,128)(2,1)S(1)} collective-permute-done((bf16[16,32,128]{2,1,0:T(8,128)(2,1)S(1)}, bf16[16,32,128]{2,1,0:T(8,128)(2,1)S(1)}, u32[]{:S(2)}, u32[]{:S(2)}) %collective-permute-start.7) | collective-permute-done | bytes 131104 | tf_op jit(solution)/shard_map/ppermute | solution.py:390
  60.9 0.0 collective-permute-start.14
  60.9 1.5 %collective-permute-done.8.k3 = bf16[16,32,128]{2,1,0:T(8,128)(2,1)S(1)} collective-permute-done((bf16[16,32,128]{2,1,0:T(8,128)(2,1)S(1)}, bf16[16,32,128]{2,1,0:T(8,128)(2,1)S(1)}, u32[]{:S(2)}, u32[]{:S(2)}) %collective-permute-start.8) | collective-permute-done | bytes 131104 | tf_op jit(solution)/shard_map/ppermute | solution.py:390
  62.3 0.0 collective-permute-done.12.p1
  62.3 2.7 %collective-permute-done.13.p2 = bf16[17,16,128]{2,1,0:T(8,128)(2,1)S(1)} collective-permute-done((bf16[17,16,128]{2,1,0:T(8,128)(2,1)S(1)}, bf16[17,16,128]{2,1,0:T(8,128)(2,1)S(1)}, u32[]{:S(2)}, u32[]{:S(2)}) %collective-permute-start.13) | collective-permute-done | bytes 69664 | tf_op jit(solution)/shard_map/ppermute | solution.py:390
  65.1 0.3 collective-permute-done.14.p3
  65.4 0.0 collective-permute-done.11.g3
  65.4 1.3 %shard_map.126 = bf16[16,200,128]{2,1,0:T(8,128)(2,1)} custom-call(bf16[16,32,128]{2,1,0:T(8,128)(2,1)S(1)} %get-tuple-element.34.k0, bf16[16,32,128]{2,1,0:T(8,128)(2,1)S(1)} %collective-permute-done.6.k1, bf16[16,32,128]{2,1,0:T(8,128)(2,1)S(1)} %collective-permute-done.7.k2, bf16[16,32,128]{2,1,0:T(8,128)(2,1)S(1)} %collective-permute-done.8.k3, ...), custom_call_target="tpu_custom_call" | custom-call | tf_op jit(solution)/shard_map/pallas_call | solution.py:427
  66.7 4.1 %all-to-all-start.2 = ((bf16[16,200,128]{2,1,0:T(8,128)(2,1)}), bf16[16,200,128]{2,1,0:T(8,128)(2,1)S(1)}, u32[]{:S(2)}, u32[]{:S(2)}) async-start(bf16[16,200,128]{2,1,0:T(8,128)(2,1)} %shard_map.126), calls=%async_computation.2 | async-start | bytes 1638400 | tf_op jit(solution)/shard_map/all_to_all | solution.py:429
  70.8 0.0 copy-done.2
  70.9 0.0 copy-start.6
  70.9 0.0 copy-start.8
  70.9 0.0 copy-start.10
  70.9 1.0 %shard_map.123 = (f32[128,512]{1,0:T(8,128)S(1)}, f32[128,512]{1,0:T(8,128)S(1)}, f32[128,512]{1,0:T(8,128)S(1)}, f32[128,512]{1,0:T(8,128)S(1)}) custom-call(s32[2]{0:T(128)S(1)} %pad_add_fusion.me_ref, bf16[128,512]{1,0:T(8,128)(2,1)S(1)} %shard_map.122.gated_ref.g0, bf16[512,2048]{1,0:T(8,128)(2,1)S(1)} %copy-done.2), custom_call_target="tpu_custom_call" | custom-call | tf_op jit(solution)/shard_map/pallas_call | solution.py:431
  71.9 1.4 %collective-permute-start.3 = (f32[128,512]{1,0:T(8,128)S(1)}, f32[128,512]{1,0:T(8,128)S(1)}, u32[]{:S(2)}, u32[]{:S(2)}) collective-permute-start(f32[128,512]{1,0:T(8,128)S(1)} %get-tuple-element.31), channel_id=1, source_target_pairs={{0,1},{1,2},{2,3},{3,0},{4,5},{5,6},{6,7},{7,4},{8,9},{9,10},{10,1... | collective-permute-start | bytes 786440 | tf_op jit(solution)/shard_map/ppermute | solution.py:350
  73.3 1.6 %collective-permute-start.4 = (f32[128,512]{1,0:T(8,128)S(1)}, f32[128,512]{1,0:T(8,128)S(1)}, u32[]{:S(2)}, u32[]{:S(2)}) collective-permute-start(f32[128,512]{1,0:T(8,128)S(1)} %get-tuple-element.32), channel_id=1, source_target_pairs={{0,2},{1,3},{2,0},{3,1},{4,6},{5,7},{6,4},{7,5},{8,10},{9,11},{10,... | collective-permute-start | bytes 786440 | tf_op jit(solution)/shard_map/ppermute | solution.py:350
  74.9 1.5 %collective-permute-start.5 = (f32[128,512]{1,0:T(8,128)S(1)}, f32[128,512]{1,0:T(8,128)S(1)}, u32[]{:S(2)}, u32[]{:S(2)}) collective-permute-start(f32[128,512]{1,0:T(8,128)S(1)} %get-tuple-element.33), channel_id=1, source_target_pairs={{0,3},{1,0},{2,1},{3,2},{4,7},{5,4},{6,5},{7,6},{8,11},{9,8},{10,9... | collective-permute-start | bytes 786440 | tf_op jit(solution)/shard_map/ppermute | solution.py:350
  76.4 2.0 %shard_map.128 = bf16[128,512]{1,0:T(8,128)(2,1)} custom-call(s32[2]{0:T(128)S(1)} %pad_add_fusion.me_ref, bf16[64,16,128]{2,1,0:T(8,128)(2,1)S(1)} %all_to_all.15.recv_ref.back_ref, bf16[512,2048]{1,0:T(8,128)(2,1)S(1)} %copy-done.2, bf16[128,512]{1,0:T(8,128)(2,1)S(1)} %copy-done.4, bf16[128,512]{1,0:T(8,128)(2,1)S(1)} %copy-done.6, ...), custom_call_target="tpu_custom_call" | custom-call | tf_op jit(solution)/shard_map/pallas_call | solution.py:424
  78.4 2.8 %collective-permute-done.3 = f32[128,512]{1,0:T(8,128)S(1)} collective-permute-done((f32[128,512]{1,0:T(8,128)S(1)}, f32[128,512]{1,0:T(8,128)S(1)}, u32[]{:S(2)}, u32[]{:S(2)}) %collective-permute-start.3) | collective-permute-done | bytes 262176 | tf_op jit(solution)/shard_map/ppermute | solution.py:350
  81.1 2.9 %collective-permute-done.4 = f32[128,512]{1,0:T(8,128)S(1)} collective-permute-done((f32[128,512]{1,0:T(8,128)S(1)}, f32[128,512]{1,0:T(8,128)S(1)}, u32[]{:S(2)}, u32[]{:S(2)}) %collective-permute-start.4) | collective-permute-done | bytes 262176 | tf_op jit(solution)/shard_map/ppermute | solution.py:350
  84.0 4.1 %collective-permute-done.5 = f32[128,512]{1,0:T(8,128)S(1)} collective-permute-done((f32[128,512]{1,0:T(8,128)S(1)}, f32[128,512]{1,0:T(8,128)S(1)}, u32[]{:S(2)}, u32[]{:S(2)}) %collective-permute-start.5) | collective-permute-done | bytes 262176 | tf_op jit(solution)/shard_map/ppermute | solution.py:350
  88.1 0.7 add_convert_fusion
  88.9 7.9 %all-to-all-done.2.recv_ref = bf16[16,200,128]{2,1,0:T(8,128)(2,1)S(1)} async-done(((bf16[16,200,128]{2,1,0:T(8,128)(2,1)}), bf16[16,200,128]{2,1,0:T(8,128)(2,1)S(1)}, u32[]{:S(2)}, u32[]{:S(2)}) %all-to-all-start.2) | async-done | bytes 819232 | tf_op jit(solution)/shard_map/all_to_all | solution.py:429
  96.8 1.6 %shard_map.127 = (bf16[128,512]{1,0:T(8,128)(2,1)}, f32[128,512]{1,0:T(8,128)}, f32[4,512]{1,0:T(4,128)}, f32[32,512]{1,0:T(8,128)}) custom-call(s32[2]{0:T(128)S(1)} %pad_add_fusion.me_ref, bf16[16,200,128]{2,1,0:T(8,128)(2,1)S(1)} %all-to-all-done.2.recv_ref), custom_call_target="tpu_custom_call" | custom-call | tf_op jit(solution)/shard_map/pallas_call | solution.py:437
  (10 shorter events, 0.0 us)
Async XLA Ops:
  0.6 18.9 %copy-start = (f32[4,512]{1,0:T(4,128)S(1)}, f32[4,512]{1,0:T(4,128)}, u32[]{:S(2)}) copy-start(f32[4,512]{1,0:T(4,128)} %param.9) | copy-start | bytes 24580
  2.6 26.8 %all-to-all-start = ((bf16[64,24,128]{2,1,0:T(8,128)(2,1)}), bf16[64,24,128]{2,1,0:T(8,128)(2,1)S(1)}, u32[]{:S(2)}, u32[]{:S(2)}) async-start(bf16[64,24,128]{2,1,0:T(8,128)(2,1)} %shard_map.118), calls=%async_computation | async-start | bytes 786432 | tf_op jit(solution)/shard_map/all_to_all | solution.py:367
  14.6 8.7 %collective-permute-start = (bf16[128,512]{1,0:T(8,128)(2,1)}, bf16[128,512]{1,0:T(8,128)(2,1)S(1)}, u32[]{:S(2)}, u32[]{:S(2)}) collective-permute-start(bf16[128,512]{1,0:T(8,128)(2,1)} %c0.3), channel_id=1, source_target_pairs={{0,1},{1,2},{2,3},{3,0},{4,5},{5,6},{6,7},{7,4},{8,9},{9,10},{10,1... | collective-permute-start | bytes 393224 | tf_op jit(solution)/shard_map/ppermute | solution.py:350
  16.2 8.1 %collective-permute-start.1 = (bf16[128,512]{1,0:T(8,128)(2,1)}, bf16[128,512]{1,0:T(8,128)(2,1)S(1)}, u32[]{:S(2)}, u32[]{:S(2)}) collective-permute-start(bf16[128,512]{1,0:T(8,128)(2,1)} %c0.3), channel_id=1, source_target_pairs={{0,2},{1,3},{2,0},{3,1},{4,6},{5,7},{6,4},{7,5},{8,10},{9,11},{10,... | collective-permute-start | bytes 393224 | tf_op jit(solution)/shard_map/ppermute | solution.py:350
  17.2 8.1 %collective-permute-start.2 = (bf16[128,512]{1,0:T(8,128)(2,1)}, bf16[128,512]{1,0:T(8,128)(2,1)S(1)}, u32[]{:S(2)}, u32[]{:S(2)}) collective-permute-start(bf16[128,512]{1,0:T(8,128)(2,1)} %c0.3), channel_id=1, source_target_pairs={{0,3},{1,0},{2,1},{3,2},{4,7},{5,4},{6,5},{7,6},{8,11},{9,8},{10,9... | collective-permute-start | bytes 393224 | tf_op jit(solution)/shard_map/ppermute | solution.py:350
  19.8 1.6 %copy-start.1 = (bf16[512,2048]{1,0:T(8,128)(2,1)S(1)}, bf16[512,2048]{1,0:T(8,128)(2,1)}, u32[]{:S(2)}) copy-start(bf16[512,2048]{1,0:T(8,128)(2,1)} %w_ref.7) | copy-start | bytes 6291460
  23.2 6.2 %copy-start.3 = (bf16[1408,256]{1,0:T(8,128)(2,1)S(1)}, bf16[1408,256]{1,0:T(8,128)(2,1)}, u32[]{:S(2)}) copy-start(bf16[1408,256]{1,0:T(8,128)(2,1)} %constant.17.clone.table_ref) | copy-start | bytes 2162692
  23.3 29.2 %copy-start.5 = (bf16[128,512]{1,0:T(8,128)(2,1)}, bf16[128,512]{1,0:T(8,128)(2,1)S(1)}, u32[]{:S(2)}) copy-start(bf16[128,512]{1,0:T(8,128)(2,1)S(1)} %collective-permute-done.c1) | copy-start | bytes 393220
  24.3 28.1 %copy-start.7 = (bf16[128,512]{1,0:T(8,128)(2,1)}, bf16[128,512]{1,0:T(8,128)(2,1)S(1)}, u32[]{:S(2)}) copy-start(bf16[128,512]{1,0:T(8,128)(2,1)S(1)} %collective-permute-done.1.c2) | copy-start | bytes 393220
  25.2 27.2 %copy-start.9 = (bf16[128,512]{1,0:T(8,128)(2,1)}, bf16[128,512]{1,0:T(8,128)(2,1)S(1)}, u32[]{:S(2)}) copy-start(bf16[128,512]{1,0:T(8,128)(2,1)S(1)} %collective-permute-done.2.c3) | copy-start | bytes 393220
  25.2 26.0 %copy-start.11 = (bf16[128,512]{1,0:T(8,128)(2,1)S(1)}, bf16[128,512]{1,0:T(8,128)(2,1)}, u32[]{:S(2)}) copy-start(bf16[128,512]{1,0:T(8,128)(2,1)} %gate_ref.1) | copy-start | bytes 393220
  25.2 27.2 %copy-start.4 = (bf16[128,512]{1,0:T(8,128)(2,1)S(1)}, bf16[128,512]{1,0:T(8,128)(2,1)}, u32[]{:S(2)}) copy-start(bf16[128,512]{1,0:T(8,128)(2,1)} %c0.3) | copy-start | bytes 393220
  51.4 3.8 %collective-permute-start.9 = (bf16[128,512]{1,0:T(8,128)(2,1)S(1)}, bf16[128,512]{1,0:T(8,128)(2,1)S(1)}, u32[]{:S(2)}, u32[]{:S(2)}) collective-permute-start(bf16[128,512]{1,0:T(8,128)(2,1)S(1)} %shard_map.122.gated_ref.g0), channel_id=1, source_target_pairs={{0,4},{4,0},{8,12},{12,8},{16,20},{20,16},{24,28},{28,24},{32,36},... | collective-permute-start | bytes 393224 | tf_op jit(solution)/shard_map/ppermute | solution.py:390
  51.7 6.3 %collective-permute-start.10 = (bf16[128,512]{1,0:T(8,128)(2,1)S(1)}, bf16[128,512]{1,0:T(8,128)(2,1)S(1)}, u32[]{:S(2)}, u32[]{:S(2)}) collective-permute-start(bf16[128,512]{1,0:T(8,128)(2,1)S(1)} %shard_map.122.gated_ref.g0), channel_id=1, source_target_pairs={{0,8},{4,12},{8,0},{12,4},{16,24},{20,28},{24,16},{28,20},{32,40},... | collective-permute-start | bytes 393224 | tf_op jit(solution)/shard_map/ppermute | solution.py:390
  53.3 5.3 %collective-permute-start.6 = (bf16[16,32,128]{2,1,0:T(8,128)(2,1)S(1)}, bf16[16,32,128]{2,1,0:T(8,128)(2,1)S(1)}, u32[]{:S(2)}, u32[]{:S(2)}) collective-permute-start(bf16[16,32,128]{2,1,0:T(8,128)(2,1)S(1)} %get-tuple-element.35), channel_id=1, source_target_pairs={{0,4},{4,0},{8,12},{12,8},{16,20},{20,16},{24,28},{28,24},{32,36},... | collective-permute-start | bytes 393224 | tf_op jit(solution)/shard_map/ppermute | solution.py:390
  53.4 7.4 %collective-permute-start.7 = (bf16[16,32,128]{2,1,0:T(8,128)(2,1)S(1)}, bf16[16,32,128]{2,1,0:T(8,128)(2,1)S(1)}, u32[]{:S(2)}, u32[]{:S(2)}) collective-permute-start(bf16[16,32,128]{2,1,0:T(8,128)(2,1)S(1)} %get-tuple-element.36), channel_id=1, source_target_pairs={{0,8},{4,12},{8,0},{12,4},{16,24},{20,28},{24,16},{28,20},{32,40},... | collective-permute-start | bytes 393224 | tf_op jit(solution)/shard_map/ppermute | solution.py:390
  54.7 7.6 %collective-permute-start.8 = (bf16[16,32,128]{2,1,0:T(8,128)(2,1)S(1)}, bf16[16,32,128]{2,1,0:T(8,128)(2,1)S(1)}, u32[]{:S(2)}, u32[]{:S(2)}) collective-permute-start(bf16[16,32,128]{2,1,0:T(8,128)(2,1)S(1)} %get-tuple-element.37), channel_id=1, source_target_pairs={{0,12},{4,8},{8,4},{12,0},{16,28},{20,24},{24,20},{28,16},{32,44},... | collective-permute-start | bytes 393224 | tf_op jit(solution)/shard_map/ppermute | solution.py:390
  57.6 13.2 %copy-start.2 = (bf16[512,2048]{1,0:T(8,128)(2,1)S(1)}, bf16[512,2048]{1,0:T(8,128)(2,1)}, u32[]{:S(2)}) copy-start(bf16[512,2048]{1,0:T(8,128)(2,1)} %w_ref.7) | copy-start | bytes 6291460
  58.0 7.4 %collective-permute-start.11 = (bf16[128,512]{1,0:T(8,128)(2,1)S(1)}, bf16[128,512]{1,0:T(8,128)(2,1)S(1)}, u32[]{:S(2)}, u32[]{:S(2)}) collective-permute-start(bf16[128,512]{1,0:T(8,128)(2,1)S(1)} %collective-permute-done.10.g2), channel_id=1, source_target_pairs={{0,4},{4,0},{8,12},{12,8},{16,20},{20,16},{24,28},{28,24},{32,36},... | collective-permute-start | bytes 393224 | tf_op jit(solution)/shard_map/ppermute | solution.py:390
  58.1 4.2 %collective-permute-start.12 = (bf16[17,16,128]{2,1,0:T(8,128)(2,1)S(1)}, bf16[17,16,128]{2,1,0:T(8,128)(2,1)S(1)}, u32[]{:S(2)}, u32[]{:S(2)}) collective-permute-start(bf16[17,16,128]{2,1,0:T(8,128)(2,1)S(1)} %get-tuple-element.39), channel_id=1, source_target_pairs={{0,4},{4,0},{8,12},{12,8},{16,20},{20,16},{24,28},{28,24},{32,36},... | collective-permute-start | bytes 208904 | tf_op jit(solution)/shard_map/ppermute | solution.py:390
  58.6 6.5 %collective-permute-start.13 = (bf16[17,16,128]{2,1,0:T(8,128)(2,1)S(1)}, bf16[17,16,128]{2,1,0:T(8,128)(2,1)S(1)}, u32[]{:S(2)}, u32[]{:S(2)}) collective-permute-start(bf16[17,16,128]{2,1,0:T(8,128)(2,1)S(1)} %get-tuple-element.42), channel_id=1, source_target_pairs={{0,8},{4,12},{8,0},{12,4},{16,24},{20,28},{24,16},{28,20},{32,40},... | collective-permute-start | bytes 208904 | tf_op jit(solution)/shard_map/ppermute | solution.py:390
  60.9 4.5 %collective-permute-start.14 = (bf16[17,16,128]{2,1,0:T(8,128)(2,1)S(1)}, bf16[17,16,128]{2,1,0:T(8,128)(2,1)S(1)}, u32[]{:S(2)}, u32[]{:S(2)}) collective-permute-start(bf16[17,16,128]{2,1,0:T(8,128)(2,1)S(1)} %get-tuple-element.43), channel_id=1, source_target_pairs={{0,12},{4,8},{8,4},{12,0},{16,28},{20,24},{24,20},{28,16},{32,44},... | collective-permute-start | bytes 208904 | tf_op jit(solution)/shard_map/ppermute | solution.py:390
  66.7 30.0 %all-to-all-start.2 = ((bf16[16,200,128]{2,1,0:T(8,128)(2,1)}), bf16[16,200,128]{2,1,0:T(8,128)(2,1)S(1)}, u32[]{:S(2)}, u32[]{:S(2)}) async-start(bf16[16,200,128]{2,1,0:T(8,128)(2,1)} %shard_map.126), calls=%async_computation.2 | async-start | bytes 1638400 | tf_op jit(solution)/shard_map/all_to_all | solution.py:429
  70.9 5.5 %copy-start.6 = (bf16[128,512]{1,0:T(8,128)(2,1)S(1)}, bf16[128,512]{1,0:T(8,128)(2,1)}, u32[]{:S(2)}) copy-start(bf16[128,512]{1,0:T(8,128)(2,1)} %copy-done.5) | copy-start | bytes 393220
  70.9 5.5 %copy-start.8 = (bf16[128,512]{1,0:T(8,128)(2,1)S(1)}, bf16[128,512]{1,0:T(8,128)(2,1)}, u32[]{:S(2)}) copy-start(bf16[128,512]{1,0:T(8,128)(2,1)} %copy-done.7) | copy-start | bytes 393220
  70.9 5.5 %copy-start.10 = (bf16[128,512]{1,0:T(8,128)(2,1)S(1)}, bf16[128,512]{1,0:T(8,128)(2,1)}, u32[]{:S(2)}) copy-start(bf16[128,512]{1,0:T(8,128)(2,1)} %copy-done.9) | copy-start | bytes 393220
  71.9 9.2 %collective-permute-start.3 = (f32[128,512]{1,0:T(8,128)S(1)}, f32[128,512]{1,0:T(8,128)S(1)}, u32[]{:S(2)}, u32[]{:S(2)}) collective-permute-start(f32[128,512]{1,0:T(8,128)S(1)} %get-tuple-element.31), channel_id=1, source_target_pairs={{0,1},{1,2},{2,3},{3,0},{4,5},{5,6},{6,7},{7,4},{8,9},{9,10},{10,1... | collective-permute-start | bytes 786440 | tf_op jit(solution)/shard_map/ppermute | solution.py:350
  73.3 10.7 %collective-permute-start.4 = (f32[128,512]{1,0:T(8,128)S(1)}, f32[128,512]{1,0:T(8,128)S(1)}, u32[]{:S(2)}, u32[]{:S(2)}) collective-permute-start(f32[128,512]{1,0:T(8,128)S(1)} %get-tuple-element.32), channel_id=1, source_target_pairs={{0,2},{1,3},{2,0},{3,1},{4,6},{5,7},{6,4},{7,5},{8,10},{9,11},{10,... | collective-permute-start | bytes 786440 | tf_op jit(solution)/shard_map/ppermute | solution.py:350
  74.9 13.3 %collective-permute-start.5 = (f32[128,512]{1,0:T(8,128)S(1)}, f32[128,512]{1,0:T(8,128)S(1)}, u32[]{:S(2)}, u32[]{:S(2)}) collective-permute-start(f32[128,512]{1,0:T(8,128)S(1)} %get-tuple-element.33), channel_id=1, source_target_pairs={{0,3},{1,0},{2,1},{3,2},{4,7},{5,4},{6,5},{7,6},{8,11},{9,8},{10,9... | collective-permute-start | bytes 786440 | tf_op jit(solution)/shard_map/ppermute | solution.py:350
